TPU v7x, 128 devices: a whole 4x4x4 slice. The times are simulated.
128 devices in a mesh: leaf: 16 (over x_hi, z, core), load: 8 (over x_lo, y).
Axes of the slice: x: 4 (x_hi: 2, x_lo: 2; x = x_hi * 2 + x_lo), y: 4, z: 4, core: 2. Of those that a mesh axis runs over, the one named last changes fastest.
Arguments:
- rhs_leaves: bfloat16 [384, 256, 4096], P('leaf', None, 'load'), may hold values from -6 to 6
- rhs_roots: bfloat16 [16, 256, 4096], P('leaf', None, 'load'), may hold values from -6 to 6
- rhs_seps: bfloat16 [16, 256, 4096], P('leaf', None, 'load'), may hold values from -6 to 6
- above_solution: bfloat16 [256, 4096], P(None, 'load'), may hold values from -6 to 6
- leaf_inverse: bfloat16 [384, 256, 256], P('leaf', 'load'), may hold values from -0.375 to 0.375
- leaf_update: bfloat16 [384, 128, 256], P('leaf', 'load'), may hold values from -0.109375 to 0.109375
- leaf_rows: int32 [384, 128], P('leaf'), may hold values from 0 to 255, as said below
- root_inverse: bfloat16 [16, 256, 256], P('leaf', 'load'), may hold values from -0.375 to 0.375
- root_coupling: bfloat16 [16, 256, 256], P('leaf', 'load'), may hold values from -0.25 to 0.25
- sep_inverse: bfloat16 [16, 256, 256], P('leaf', 'load'), may hold values from -0.375 to 0.375
- sep_coupling: bfloat16 [16, 256, 256], P('leaf', 'load'), may hold values from -0.25 to 0.25
Outputs:
- solution_leaves: bfloat16 [384, 256, 4096], P('leaf', None, 'load')
- solution_roots: bfloat16 [16, 256, 4096], P('leaf', None, 'load')
- solution_seps: bfloat16 [16, 256, 4096], P('leaf', None, 'load')
Inputs may be any that keep to these rules, and one draw needn't show every extreme that they name: `leaf_rows`: each row names 128 different rows of its subtree root's 256 unknowns.
All inputs are finite; a program needn't handle non-finite values.
Results may differ from a plain program's by a relative error of at most 0.023.
Values may be sent and summed in bfloat16 or wider, within the bound.
No kernel may reach another device: no remote copies, remote signals or barrier semaphores. Data moves between devices by JAX's collectives and lax.ppermute only.
A program may use at most 128 MiB of HBM per device.

v0:
```python
import jax
import jax.numpy as jnp
from jax import lax
from jax.sharding import PartitionSpec as P


def from_behind(value, axis, steps):
    count = lax.axis_size(axis)
    leading, last = (max(0, -steps), min(count, count - steps))
    return lax.ppermute(value, axis, [(source, source + steps) for source in range(leading, last)])


def product(left, right):
    return jnp.dot(left, right, preferred_element_type=jnp.float32)


def product_transposed(left, right):
    return lax.dot_general(
        left, right, (((0,), (0,)), ((), ())), preferred_element_type=jnp.float32
    )


def from_above(block, stride):
    return from_behind(block, "leaf", -stride)


def from_below(block, stride):
    return from_behind(block, "leaf", stride)


def local(
    rhs_leaves,
    rhs_roots,
    rhs_seps,
    above_solution,
    leaf_inverse,
    leaf_update,
    leaf_rows,
    root_inverse,
    root_coupling,
    sep_inverse,
    sep_coupling,
):
    width = rhs_leaves.shape[1]
    onehot = (leaf_rows[:, :, None] == lax.broadcasted_iota(jnp.int32, (1, 1, width), 2)).astype(
        jnp.bfloat16
    )
    solved_leaves = jnp.einsum(
        "jnw,jwr->jnr",
        lax.all_gather(leaf_inverse, "load", axis=1, tiled=True),
        rhs_leaves,
        preferred_element_type=jnp.float32,
    ).astype(jnp.bfloat16)
    leaf_flow = jnp.einsum(
        "jkw,jwr->jkr",
        lax.all_gather(leaf_update, "load", axis=1, tiled=True),
        solved_leaves,
        preferred_element_type=jnp.float32,
    ).astype(jnp.bfloat16)
    root_sum = jnp.einsum("jkw,jkr->wr", onehot, leaf_flow, preferred_element_type=jnp.float32)
    root_inv, root_cpl, node_inv, node_cpl = (
        lax.all_gather(root_inverse, "load", axis=1, tiled=True),
        lax.all_gather(root_coupling, "load", axis=1, tiled=True),
        lax.all_gather(sep_inverse, "load", axis=1, tiled=True),
        lax.all_gather(sep_coupling, "load", axis=1, tiled=True),
    )
    root_inv = root_inv[0]
    root_cpl = root_cpl[0]
    node_inv = node_inv[0]
    node_cpl = node_cpl[0]
    root_rhs = (rhs_roots[0].astype(jnp.float32) - root_sum).astype(jnp.bfloat16)
    solved_root = product(root_inv, root_rhs).astype(jnp.bfloat16)
    root_flow = product(root_cpl, solved_root).astype(jnp.bfloat16)
    count = lax.axis_size("leaf")
    depth = count.bit_length() - 1
    position = lax.axis_index("leaf")
    level = jnp.int32(1)
    for bit in range(1, depth + 1):
        level = level + ((position + 1) % 2**bit == 0).astype(jnp.int32)
    solved_sep = jnp.zeros_like(root_flow)
    sep_flow = jnp.zeros_like(root_flow)
    for height in range(1, depth + 2):
        if height == 1:
            inflow = root_flow.astype(jnp.float32) + from_above(root_flow, 1).astype(jnp.float32)
        else:
            stride = 2 ** (height - 2)
            from_lower = from_behind(sep_flow, "leaf", stride)
            inflow = from_lower.astype(jnp.float32) + from_above(sep_flow, stride).astype(
                jnp.float32
            )
        sep_rhs = (rhs_seps[0].astype(jnp.float32) - inflow).astype(jnp.bfloat16)
        fresh = product(node_inv, sep_rhs).astype(jnp.bfloat16)
        active = level == height
        solved_sep = jnp.where(active, fresh, solved_sep)
        sep_flow = jnp.where(active, product(node_cpl, fresh).astype(jnp.bfloat16), sep_flow)
    own_answer = jnp.zeros_like(root_flow)
    for height in range(depth + 1, 0, -1):
        if height == depth + 1:
            parent_side = above_solution
        else:
            stride = 2 ** (height - 1)
            down_from_higher = from_behind(own_answer, "leaf", -stride)
            down_from_lower = from_below(own_answer, stride)
            order = (position + 1 - stride) // (2 * stride)
            parent_side = jnp.where(order % 2 == 0, down_from_higher, down_from_lower)
        sep_reduced = (
            solved_sep.astype(jnp.float32) - product_transposed(node_cpl, parent_side)
        ).astype(jnp.bfloat16)
        fresh = product_transposed(node_inv, sep_reduced).astype(jnp.bfloat16)
        own_answer = jnp.where(level == height, fresh, own_answer)
    from_parent = from_below(own_answer, 1)
    parent_answer = jnp.where(position % 2 == 0, own_answer, from_parent)
    root_reduced = (
        solved_root.astype(jnp.float32) - product_transposed(root_cpl, parent_answer)
    ).astype(jnp.bfloat16)
    root_answer = product_transposed(root_inv, root_reduced).astype(jnp.bfloat16)
    picked = jnp.einsum(
        "jkw,wr->jkr", onehot, root_answer, preferred_element_type=jnp.float32
    ).astype(jnp.bfloat16)
    rows_now = picked
    lowered = jnp.einsum(
        "jnw,jnr->jwr",
        lax.all_gather(leaf_update, "load", axis=1, tiled=True),
        rows_now,
        preferred_element_type=jnp.float32,
    )
    leaf_reduced = (solved_leaves.astype(jnp.float32) - lowered).astype(jnp.bfloat16)
    rows_now = leaf_reduced
    leaf_answer = jnp.einsum(
        "jnw,jnr->jwr",
        lax.all_gather(leaf_inverse, "load", axis=1, tiled=True),
        rows_now,
        preferred_element_type=jnp.float32,
    ).astype(jnp.bfloat16)
    return (leaf_answer, root_answer[None], own_answer[None])


def solution(mesh):
    in_specs = (
        P("leaf", None, "load"),
        P("leaf", None, "load"),
        P("leaf", None, "load"),
        P(None, "load"),
        P("leaf", "load", None),
        P("leaf", "load", None),
        P("leaf", None),
        P("leaf", "load", None),
        P("leaf", "load", None),
        P("leaf", "load", None),
        P("leaf", "load", None),
    )
    out_specs = (P("leaf", None, "load"), P("leaf", None, "load"), P("leaf", None, "load"))
    return jax.shard_map(local, mesh=mesh, in_specs=in_specs, out_specs=out_specs, check_vma=False)
```

profile of v0, /device:TPU:4, one launch (start us, length us, event | category | flops | bytes accessed | tf_op | source)
XLA Modules:
  0.0 319.6 jit_solution(3465651614092065867)
XLA Ops:
  7.2 0.7 all-gather.3.cloned.1.call-update
  8.0 0.7 all-gather.5.cloned.1.call-update
  8.7 28.8 %all_gather.22 = bf16[1,256,256]{2,1,0:T(8,128)(2,1)S(1)} all-gather(bf16[1,32,256]{2,1,0:T(8,128)(2,1)} %param.18), channel_id=1, replica_groups=mesh['leaf'=16,'load'=8] {'load'}, dimensions={1}, use_global_device_ids=true | all-gather | bytes 147456 | tf_op jit(solution)/shard_map/all_gather | solution.py:62
  37.5 28.5 %all_gather.23 = bf16[1,256,256]{2,1,0:T(8,128)(2,1)S(1)} all-gather(bf16[1,32,256]{2,1,0:T(8,128)(2,1)} %param.19), channel_id=1, replica_groups=mesh['leaf'=16,'load'=8] {'load'}, dimensions={1}, use_global_device_ids=true | all-gather | bytes 147456 | tf_op jit(solution)/shard_map/all_gather | solution.py:63
  66.0 8.3 %convolution_convert_fusion = bf16[24,256,512]{2,1,0:T(8,128)(2,1)} fusion(bf16[24,256,256]{2,1,0:T(8,128)(2,1)} %all-gather.3.cloned.1.call-done, bf16[24,256,512]{2,1,0:T(8,128)(2,1)} %param.11), kind=kOutput, calls=%fused_computation.5 | convolution fusion | flops 1613758464 | bytes 15728640 | tf_op jit(solution)/shard_map/jnw,jwr->jnr/dot_general | solution.py:48
  74.4 24.0 %all-gather.5.cloned.1.call-done = bf16[24,128,256]{2,1,0:T(8,128)(2,1)} async-done(((bf16[24,16,256]{2,1,0:T(8,128)(2,1)}), bf16[24,128,256]{2,1,0:T(8,128)(2,1)}) %all-gather.5.cloned.1.call-update) | async-done | bytes 1572880 | tf_op jit(solution)/shard_map/all_gather | solution.py:123
  98.4 6.4 %fusion.33 = bf16[256,512]{1,0:T(8,128)(2,1)S(1)} fusion(bf16[24,256,512]{2,1,0:T(8,128)(2,1)} %convolution_convert_fusion, bf16[24,128,256]{2,1,0:T(8,128)(2,1)} %all-gather.5.cloned.1.call-done, s32[24,128]{1,0:T(8,128)S(1)} %copy-done.4, bf16[1,256,512]{2,1,0:T(8,128)(2,1)S(1)} %copy-done.5), kind=kOutput, calls=%fused_computation.28 | convolution fusion | flops 1614151680 | bytes 8400896 | tf_op jit(solution)/shard_map/jkw,jkr->wr/dot_general | solution.py:60
  104.8 0.3 convolution_convert_fusion.17
  105.4 1.9 collective-permute-start
  107.5 28.2 %all_gather.24 = bf16[1,256,256]{2,1,0:T(8,128)(2,1)S(1)} all-gather(bf16[1,32,256]{2,1,0:T(8,128)(2,1)S(1)} %copy-done.2), channel_id=1, replica_groups=mesh['leaf'=16,'load'=8] {'load'}, dimensions={1}, use_global_device_ids=true | all-gather | bytes 147456 | tf_op jit(solution)/shard_map/all_gather | solution.py:64
  135.7 28.2 %all_gather.25 = bf16[1,256,256]{2,1,0:T(8,128)(2,1)S(1)} all-gather(bf16[1,32,256]{2,1,0:T(8,128)(2,1)S(1)} %copy-done.3), channel_id=1, replica_groups=mesh['leaf'=16,'load'=8] {'load'}, dimensions={1}, use_global_device_ids=true | all-gather | bytes 147456 | tf_op jit(solution)/shard_map/all_gather | solution.py:65
  163.9 0.3 convolution_convert_fusion.15
  164.1 0.3 fusion.46
  164.4 1.9 collective-permute-start.2
  166.3 2.4 collective-permute-start.1
  168.7 1.4 collective-permute-done.2
  170.2 7.4 %collective-permute-done.1 = bf16[256,512]{0,1:T(8,128)(2,1)S(1)} collective-permute-done((bf16[256,512]{0,1:T(8,128)(2,1)S(1)}, bf16[256,512]{0,1:T(8,128)(2,1)S(1)}, u32[]{:S(2)}, u32[]{:S(2)}) %collective-permute-start.1) | collective-permute-done | bytes 262176 | tf_op jit(solution)/shard_map/ppermute | solution.py:10
  177.6 0.3 convolution_convert_fusion.13
  177.9 0.3 fusion.48
  178.2 1.9 collective-permute-start.4
  180.1 3.9 %collective-permute-start.3 = (bf16[256,512]{0,1:T(8,128)(2,1)S(1)}, bf16[256,512]{0,1:T(8,128)(2,1)S(1)}, u32[]{:S(2)}, u32[]{:S(2)}) collective-permute-start(bf16[256,512]{0,1:T(8,128)(2,1)S(1)} %fusion.48), channel_id=1, source_target_pairs={{0,16},{8,24},{16,32},{24,40},{32,48},{40,56},{48,64},{56,72},{64,... | collective-permute-start | bytes 786440 | tf_op jit(solution)/shard_map/ppermute | solution.py:10
  184.0 2.4 collective-permute-done.4
  186.4 6.8 %collective-permute-done.3 = bf16[256,512]{0,1:T(8,128)(2,1)S(1)} collective-permute-done((bf16[256,512]{0,1:T(8,128)(2,1)S(1)}, bf16[256,512]{0,1:T(8,128)(2,1)S(1)}, u32[]{:S(2)}, u32[]{:S(2)}) %collective-permute-start.3) | collective-permute-done | bytes 262176 | tf_op jit(solution)/shard_map/ppermute | solution.py:10
  193.2 0.3 convolution_convert_fusion.11
  193.4 0.3 fusion.50
  193.7 1.9 collective-permute-start.6
  195.7 5.4 %collective-permute-start.5 = (bf16[256,512]{0,1:T(8,128)(2,1)S(1)}, bf16[256,512]{0,1:T(8,128)(2,1)S(1)}, u32[]{:S(2)}, u32[]{:S(2)}) collective-permute-start(bf16[256,512]{0,1:T(8,128)(2,1)S(1)} %fusion.50), channel_id=1, source_target_pairs={{0,32},{8,40},{16,48},{24,56},{32,64},{40,72},{48,80},{56,88},{64,... | collective-permute-start | bytes 786440 | tf_op jit(solution)/shard_map/ppermute | solution.py:10
  201.1 8.3 %collective-permute-done.6 = bf16[256,512]{0,1:T(8,128)(2,1)S(1)} collective-permute-done((bf16[256,512]{0,1:T(8,128)(2,1)S(1)}, bf16[256,512]{0,1:T(8,128)(2,1)S(1)}, u32[]{:S(2)}, u32[]{:S(2)}) %collective-permute-start.6) | collective-permute-done | bytes 262176 | tf_op jit(solution)/shard_map/ppermute | solution.py:10
  209.4 0.3 convolution_convert_fusion.9
  209.7 0.3 fusion.52
  209.9 1.3 collective-permute-start.8
  211.3 1.3 collective-permute-start.7
  212.6 2.6 collective-permute-done.8
  215.1 5.9 %collective-permute-done.7 = bf16[256,512]{0,1:T(8,128)(2,1)S(1)} collective-permute-done((bf16[256,512]{0,1:T(8,128)(2,1)S(1)}, bf16[256,512]{0,1:T(8,128)(2,1)S(1)}, u32[]{:S(2)}, u32[]{:S(2)}) %collective-permute-start.7) | collective-permute-done | bytes 262176 | tf_op jit(solution)/shard_map/ppermute | solution.py:10
  221.0 0.3 fusion.55
  221.3 0.4 fusion.65
  221.8 1.3 collective-permute-start.10
  223.1 6.1 %collective-permute-start.9 = (bf16[256,512]{0,1:T(8,128)(2,1)S(1)}, bf16[256,512]{0,1:T(8,128)(2,1)S(1)}, u32[]{:S(2)}, u32[]{:S(2)}) collective-permute-start(bf16[256,512]{0,1:T(8,128)(2,1)S(1)} %fusion.65), channel_id=1, source_target_pairs={{64,0},{72,8},{80,16},{88,24},{96,32},{104,40},{112,48},{120,56},{... | collective-permute-start | bytes 786440 | tf_op jit(solution)/shard_map/ppermute | solution.py:10
  229.2 2.3 collective-permute-done.10
  231.6 1.5 collective-permute-done.9
  233.0 0.4 fusion.63
  233.4 1.9 collective-permute-start.12
  235.4 7.8 %collective-permute-start.11 = (bf16[256,512]{0,1:T(8,128)(2,1)S(1)}, bf16[256,512]{0,1:T(8,128)(2,1)S(1)}, u32[]{:S(2)}, u32[]{:S(2)}) collective-permute-start(bf16[256,512]{0,1:T(8,128)(2,1)S(1)} %fusion.63), channel_id=1, source_target_pairs={{32,0},{40,8},{48,16},{56,24},{64,32},{72,40},{80,48},{88,56},{96,... | collective-permute-start | bytes 786440 | tf_op jit(solution)/shard_map/ppermute | solution.py:10
  243.2 2.5 collective-permute-done.12
  245.7 2.2 collective-permute-done.11
  247.9 0.4 fusion.62
  248.3 6.2 %collective-permute-start.14 = (bf16[256,512]{0,1:T(8,128)(2,1)S(1)}, bf16[256,512]{0,1:T(8,128)(2,1)S(1)}, u32[]{:S(2)}, u32[]{:S(2)}) collective-permute-start(bf16[256,512]{0,1:T(8,128)(2,1)S(1)} %fusion.62), channel_id=1, source_target_pairs={{0,16},{8,24},{16,32},{24,40},{32,48},{40,56},{48,64},{56,72},{64,... | collective-permute-start | bytes 786440 | tf_op jit(solution)/shard_map/ppermute | solution.py:10
  254.6 5.6 %collective-permute-start.13 = (bf16[256,512]{0,1:T(8,128)(2,1)S(1)}, bf16[256,512]{0,1:T(8,128)(2,1)S(1)}, u32[]{:S(2)}, u32[]{:S(2)}) collective-permute-start(bf16[256,512]{0,1:T(8,128)(2,1)S(1)} %fusion.62), channel_id=1, source_target_pairs={{16,0},{24,8},{32,16},{40,24},{48,32},{56,40},{64,48},{72,56},{80,... | collective-permute-start | bytes 786440 | tf_op jit(solution)/shard_map/ppermute | solution.py:10
  260.2 2.4 collective-permute-done.14
  262.6 1.5 collective-permute-done.13
  264.1 0.4 fusion.61
  264.5 1.9 collective-permute-start.16
  266.4 7.3 %collective-permute-start.15 = (bf16[256,512]{0,1:T(8,128)(2,1)S(1)}, bf16[256,512]{0,1:T(8,128)(2,1)S(1)}, u32[]{:S(2)}, u32[]{:S(2)}) collective-permute-start(bf16[256,512]{0,1:T(8,128)(2,1)S(1)} %fusion.61), channel_id=1, source_target_pairs={{8,0},{16,8},{24,16},{32,24},{40,32},{48,40},{56,48},{64,56},{72,6... | collective-permute-start | bytes 786440 | tf_op jit(solution)/shard_map/ppermute | solution.py:10
  273.7 2.1 collective-permute-done.16
  275.8 1.8 collective-permute-done.15
  277.5 0.4 fusion.60
  277.9 2.1 collective-permute-start.17
  280.1 0.8 copy.18
  280.9 8.5 %collective-permute-done.17 = bf16[256,512]{0,1:T(8,128)(2,1)S(1)} collective-permute-done((bf16[256,512]{0,1:T(8,128)(2,1)S(1)}, bf16[256,512]{0,1:T(8,128)(2,1)S(1)}, u32[]{:S(2)}, u32[]{:S(2)}) %collective-permute-start.17) | collective-permute-done | bytes 262176 | tf_op jit(solution)/shard_map/ppermute | solution.py:10
  289.4 1.1 convolution_convert_fusion.1
  290.5 2.2 fusion.12
  292.7 1.8 copy.17
  294.5 9.6 %convert_bitcast_fusion = bf16[24,256,512]{1,2,0:T(8,128)(2,1)} fusion(bf16[24,256,256]{2,1,0:T(8,128)(2,1)} %all-gather.3.cloned.1.call-done, bf16[24,256,512]{2,1,0:T(8,128)(2,1)} %convolution_convert_fusion, bf16[24,128,256]{2,1,0:T(8,128)(2,1)} %all-gather.5.cloned.1.call-done, bf16[24,128,512]{2,1,0:T(8,128)(2,1)S(1)} %fusion.12), kind=kOutput, calls=%fused_computation.3 | convolution fusion | flops 2428502016 | bytes 20447232 | tf_op jit(solution)/shard_map/jnw,jnr->jwr/dot_general | solution.py:129
  304.1 8.6 %copy.16 = bf16[24,256,512]{2,1,0:T(8,128)(2,1)} copy(bf16[24,256,512]{1,2,0:T(8,128)(2,1)} %convert_bitcast_fusion) | data formatting | bytes 12582912
  (19 shorter events, 0.5 us)
Async XLA Ops:
  7.2 214.2 %copy-start = (bf16[256,512]{1,0:T(8,128)(2,1)S(1)}, bf16[256,512]{1,0:T(8,128)(2,1)}, u32[]{:S(2)}) copy-start(bf16[256,512]{1,0:T(8,128)(2,1)} %param.14) | copy-start | bytes 786436
  7.2 58.8 %all-gather.3.cloned.1.call-start = ((), (), s32[]{:S(2)}) async-start(), calls=%async_computation | async-start | bytes 3538944 | tf_op jit(solution)/shard_map/all_gather | solution.py:131
  7.9 90.5 %all-gather.5.cloned.1.call-start = ((), (), s32[]{:S(2)}) async-start(), calls=%async_computation.1 | async-start | bytes 1769472 | tf_op jit(solution)/shard_map/all_gather | solution.py:123
  66.0 32.4 %copy-start.4 = (s32[24,128]{1,0:T(8,128)S(1)}, s32[24,128]{1,0:T(8,128)}, u32[]{:S(2)}) copy-start(s32[24,128]{1,0:T(8,128)} %param.17) | copy-start | bytes 36868
  66.0 32.4 %copy-start.5 = (bf16[1,256,512]{2,1,0:T(8,128)(2,1)S(1)}, bf16[1,256,512]{2,1,0:T(8,128)(2,1)}, u32[]{:S(2)}) copy-start(bf16[1,256,512]{2,1,0:T(8,128)(2,1)} %param.12) | copy-start | bytes 786436
  74.4 33.0 %copy-start.1 = (bf16[1,256,512]{2,1,0:T(8,128)(2,1)S(1)}, bf16[1,256,512]{2,1,0:T(8,128)(2,1)}, u32[]{:S(2)}) copy-start(bf16[1,256,512]{2,1,0:T(8,128)(2,1)} %param.13) | copy-start | bytes 786436
  74.4 33.1 %copy-start.2 = (bf16[1,32,256]{2,1,0:T(8,128)(2,1)S(1)}, bf16[1,32,256]{2,1,0:T(8,128)(2,1)}, u32[]{:S(2)}) copy-start(bf16[1,32,256]{2,1,0:T(8,128)(2,1)} %param.20) | copy-start | bytes 49156
  74.4 61.3 %copy-start.3 = (bf16[1,32,256]{2,1,0:T(8,128)(2,1)S(1)}, bf16[1,32,256]{2,1,0:T(8,128)(2,1)}, u32[]{:S(2)}) copy-start(bf16[1,32,256]{2,1,0:T(8,128)(2,1)} %param.21) | copy-start | bytes 49156
  105.4 58.5 %collective-permute-start = (bf16[256,512]{0,1:T(8,128)(2,1)S(1)}, bf16[256,512]{0,1:T(8,128)(2,1)S(1)}, u32[]{:S(2)}, u32[]{:S(2)}) collective-permute-start(bf16[256,512]{0,1:T(8,128)(2,1)S(1)} %fusion.44), channel_id=1, source_target_pairs={{8,0},{16,8},{24,16},{32,24},{40,32},{48,40},{56,48},{64,56},{72,6... | collective-permute-start | bytes 786440 | tf_op jit(solution)/shard_map/ppermute | solution.py:10
  164.4 5.8 %collective-permute-start.2 = (bf16[256,512]{0,1:T(8,128)(2,1)S(1)}, bf16[256,512]{0,1:T(8,128)(2,1)S(1)}, u32[]{:S(2)}, u32[]{:S(2)}) collective-permute-start(bf16[256,512]{0,1:T(8,128)(2,1)S(1)} %fusion.46), channel_id=1, source_target_pairs={{8,0},{16,8},{24,16},{32,24},{40,32},{48,40},{56,48},{64,56},{72,6... | collective-permute-start | bytes 786440 | tf_op jit(solution)/shard_map/ppermute | solution.py:10
  166.3 11.3 %collective-permute-start.1 = (bf16[256,512]{0,1:T(8,128)(2,1)S(1)}, bf16[256,512]{0,1:T(8,128)(2,1)S(1)}, u32[]{:S(2)}, u32[]{:S(2)}) collective-permute-start(bf16[256,512]{0,1:T(8,128)(2,1)S(1)} %fusion.46), channel_id=1, source_target_pairs={{0,8},{8,16},{16,24},{24,32},{32,40},{40,48},{48,56},{56,64},{64,7... | collective-permute-start | bytes 786440 | tf_op jit(solution)/shard_map/ppermute | solution.py:10
  178.2 8.3 %collective-permute-start.4 = (bf16[256,512]{0,1:T(8,128)(2,1)S(1)}, bf16[256,512]{0,1:T(8,128)(2,1)S(1)}, u32[]{:S(2)}, u32[]{:S(2)}) collective-permute-start(bf16[256,512]{0,1:T(8,128)(2,1)S(1)} %fusion.48), channel_id=1, source_target_pairs={{16,0},{24,8},{32,16},{40,24},{48,32},{56,40},{64,48},{72,56},{80,... | collective-permute-start | bytes 786440 | tf_op jit(solution)/shard_map/ppermute | solution.py:10
  180.1 13.1 %collective-permute-start.3 = (bf16[256,512]{0,1:T(8,128)(2,1)S(1)}, bf16[256,512]{0,1:T(8,128)(2,1)S(1)}, u32[]{:S(2)}, u32[]{:S(2)}) collective-permute-start(bf16[256,512]{0,1:T(8,128)(2,1)S(1)} %fusion.48), channel_id=1, source_target_pairs={{0,16},{8,24},{16,32},{24,40},{32,48},{40,56},{48,64},{56,72},{64,... | collective-permute-start | bytes 786440 | tf_op jit(solution)/shard_map/ppermute | solution.py:10
  193.7 15.7 %collective-permute-start.6 = (bf16[256,512]{0,1:T(8,128)(2,1)S(1)}, bf16[256,512]{0,1:T(8,128)(2,1)S(1)}, u32[]{:S(2)}, u32[]{:S(2)}) collective-permute-start(bf16[256,512]{0,1:T(8,128)(2,1)S(1)} %fusion.50), channel_id=1, source_target_pairs={{32,0},{40,8},{48,16},{56,24},{64,32},{72,40},{80,48},{88,56},{96,... | collective-permute-start | bytes 786440 | tf_op jit(solution)/shard_map/ppermute | solution.py:10
  195.7 13.7 %collective-permute-start.5 = (bf16[256,512]{0,1:T(8,128)(2,1)S(1)}, bf16[256,512]{0,1:T(8,128)(2,1)S(1)}, u32[]{:S(2)}, u32[]{:S(2)}) collective-permute-start(bf16[256,512]{0,1:T(8,128)(2,1)S(1)} %fusion.50), channel_id=1, source_target_pairs={{0,32},{8,40},{16,48},{24,56},{32,64},{40,72},{48,80},{56,88},{64,... | collective-permute-start | bytes 786440 | tf_op jit(solution)/shard_map/ppermute | solution.py:10
  209.9 5.2 %collective-permute-start.8 = (bf16[256,512]{0,1:T(8,128)(2,1)S(1)}, bf16[256,512]{0,1:T(8,128)(2,1)S(1)}, u32[]{:S(2)}, u32[]{:S(2)}) collective-permute-start(bf16[256,512]{0,1:T(8,128)(2,1)S(1)} %fusion.52), channel_id=1, source_target_pairs={{64,0},{72,8},{80,16},{88,24},{96,32},{104,40},{112,48},{120,56},{... | collective-permute-start | bytes 786440 | tf_op jit(solution)/shard_map/ppermute | solution.py:10
  211.3 9.8 %collective-permute-start.7 = (bf16[256,512]{0,1:T(8,128)(2,1)S(1)}, bf16[256,512]{0,1:T(8,128)(2,1)S(1)}, u32[]{:S(2)}, u32[]{:S(2)}) collective-permute-start(bf16[256,512]{0,1:T(8,128)(2,1)S(1)} %fusion.52), channel_id=1, source_target_pairs={{0,64},{8,72},{16,80},{24,88},{32,96},{40,104},{48,112},{56,120},{... | collective-permute-start | bytes 786440 | tf_op jit(solution)/shard_map/ppermute | solution.py:10
  221.8 9.8 %collective-permute-start.10 = (bf16[256,512]{0,1:T(8,128)(2,1)S(1)}, bf16[256,512]{0,1:T(8,128)(2,1)S(1)}, u32[]{:S(2)}, u32[]{:S(2)}) collective-permute-start(bf16[256,512]{0,1:T(8,128)(2,1)S(1)} %fusion.65), channel_id=1, source_target_pairs={{0,64},{8,72},{16,80},{24,88},{32,96},{40,104},{48,112},{56,120},{... | collective-permute-start | bytes 786440 | tf_op jit(solution)/shard_map/ppermute | solution.py:10
  223.1 9.9 %collective-permute-start.9 = (bf16[256,512]{0,1:T(8,128)(2,1)S(1)}, bf16[256,512]{0,1:T(8,128)(2,1)S(1)}, u32[]{:S(2)}, u32[]{:S(2)}) collective-permute-start(bf16[256,512]{0,1:T(8,128)(2,1)S(1)} %fusion.65), channel_id=1, source_target_pairs={{64,0},{72,8},{80,16},{88,24},{96,32},{104,40},{112,48},{120,56},{... | collective-permute-start | bytes 786440 | tf_op jit(solution)/shard_map/ppermute | solution.py:10
  233.4 12.3 %collective-permute-start.12 = (bf16[256,512]{0,1:T(8,128)(2,1)S(1)}, bf16[256,512]{0,1:T(8,128)(2,1)S(1)}, u32[]{:S(2)}, u32[]{:S(2)}) collective-permute-start(bf16[256,512]{0,1:T(8,128)(2,1)S(1)} %fusion.63), channel_id=1, source_target_pairs={{0,32},{8,40},{16,48},{24,56},{32,64},{40,72},{48,80},{56,88},{64,... | collective-permute-start | bytes 786440 | tf_op jit(solution)/shard_map/ppermute | solution.py:10
  235.4 12.6 %collective-permute-start.11 = (bf16[256,512]{0,1:T(8,128)(2,1)S(1)}, bf16[256,512]{0,1:T(8,128)(2,1)S(1)}, u32[]{:S(2)}, u32[]{:S(2)}) collective-permute-start(bf16[256,512]{0,1:T(8,128)(2,1)S(1)} %fusion.63), channel_id=1, source_target_pairs={{32,0},{40,8},{48,16},{56,24},{64,32},{72,40},{80,48},{88,56},{96,... | collective-permute-start | bytes 786440 | tf_op jit(solution)/shard_map/ppermute | solution.py:10
  248.3 14.2 %collective-permute-start.14 = (bf16[256,512]{0,1:T(8,128)(2,1)S(1)}, bf16[256,512]{0,1:T(8,128)(2,1)S(1)}, u32[]{:S(2)}, u32[]{:S(2)}) collective-permute-start(bf16[256,512]{0,1:T(8,128)(2,1)S(1)} %fusion.62), channel_id=1, source_target_pairs={{0,16},{8,24},{16,32},{24,40},{32,48},{40,56},{48,64},{56,72},{64,... | collective-permute-start | bytes 786440 | tf_op jit(solution)/shard_map/ppermute | solution.py:10
  254.6 9.5 %collective-permute-start.13 = (bf16[256,512]{0,1:T(8,128)(2,1)S(1)}, bf16[256,512]{0,1:T(8,128)(2,1)S(1)}, u32[]{:S(2)}, u32[]{:S(2)}) collective-permute-start(bf16[256,512]{0,1:T(8,128)(2,1)S(1)} %fusion.62), channel_id=1, source_target_pairs={{16,0},{24,8},{32,16},{40,24},{48,32},{56,40},{64,48},{72,56},{80,... | collective-permute-start | bytes 786440 | tf_op jit(solution)/shard_map/ppermute | solution.py:10
  264.5 11.3 %collective-permute-start.16 = (bf16[256,512]{0,1:T(8,128)(2,1)S(1)}, bf16[256,512]{0,1:T(8,128)(2,1)S(1)}, u32[]{:S(2)}, u32[]{:S(2)}) collective-permute-start(bf16[256,512]{0,1:T(8,128)(2,1)S(1)} %fusion.61), channel_id=1, source_target_pairs={{0,8},{8,16},{16,24},{24,32},{32,40},{40,48},{48,56},{56,64},{64,7... | collective-permute-start | bytes 786440 | tf_op jit(solution)/shard_map/ppermute | solution.py:10
  266.4 11.1 %collective-permute-start.15 = (bf16[256,512]{0,1:T(8,128)(2,1)S(1)}, bf16[256,512]{0,1:T(8,128)(2,1)S(1)}, u32[]{:S(2)}, u32[]{:S(2)}) collective-permute-start(bf16[256,512]{0,1:T(8,128)(2,1)S(1)} %fusion.61), channel_id=1, source_target_pairs={{8,0},{16,8},{24,16},{32,24},{40,32},{48,40},{56,48},{64,56},{72,6... | collective-permute-start | bytes 786440 | tf_op jit(solution)/shard_map/ppermute | solution.py:10
  277.9 11.5 %collective-permute-start.17 = (bf16[256,512]{0,1:T(8,128)(2,1)S(1)}, bf16[256,512]{0,1:T(8,128)(2,1)S(1)}, u32[]{:S(2)}, u32[]{:S(2)}) collective-permute-start(bf16[256,512]{0,1:T(8,128)(2,1)S(1)} %fusion.60), channel_id=1, source_target_pairs={{0,8},{8,16},{16,24},{24,32},{32,40},{40,48},{48,56},{56,64},{64,7... | collective-permute-start | bytes 786440 | tf_op jit(solution)/shard_map/ppermute | solution.py:10
Sparse Core Ops, SparseCore 0:
  9.7 46.5 all-gather.2
  57.9 40.5 all-gather.4
where the time goes:
time: 320 us
  blocking collectives  114 us (36%)
  waiting for transfers between devices  84.9 us (27%)
  starting transfers between devices  62.3 us (19%)
  matrix products  32.6 us (10%)
  between operations  14.6 us (5%)
  local copies, waits for them, and re-layouts  11.4 us (4%)
    ppermute x18, starting transfers between devices, from_behind(): lax.ppermute(value, axis, [(source, source + steps) for source in range(l...  62.3 us
    ppermute x18, waiting for transfers between devices, from_behind(): lax.ppermute(value, axis, [(source, source + steps) for source in range(l...  59.5 us
    all_gather x1, blocking collectives, local(): lax.all_gather(root_inverse, 'load', axis=1, tiled=True)  28.8 us
    all_gather x1, blocking collectives, local(): lax.all_gather(root_coupling, 'load', axis=1, tiled=True)  28.5 us
    all_gather x1, blocking collectives, local(): lax.all_gather(sep_inverse, 'load', axis=1, tiled=True)  28.2 us
    all_gather x1, blocking collectives, local(): lax.all_gather(sep_coupling, 'load', axis=1, tiled=True)  28.2 us
    all_gather x1, waiting for transfers between devices, local(): lax.all_gather(leaf_update, 'load', axis=1, tiled=True)  24 us
    unnamed x16, local copies, waits for them, and re-layouts  11.4 us
  transfers between devices with their start and end apart: 20, of which 17 were waited for; matrix products, arithmetic and copies ran while one was open for 3% of the time, Pallas kernels for 0%

commit v1 on v0

v1 whole, which is shorter than its diff:
```python
import functools

import jax
import jax.numpy as jnp
from jax import lax
from jax.experimental import pallas as pl
from jax.experimental.pallas import tpu as pltpu
from jax.sharding import PartitionSpec as P

BF = jnp.bfloat16
F32 = jnp.float32


def mm(a, b):
    return jnp.dot(a, b, preferred_element_type=F32)


def mmt(a, b):
    return lax.dot_general(a, b, (((0,), (0,)), ((), ())), preferred_element_type=F32)


def sub(rhs, inflow):
    return (rhs.astype(F32) - inflow).astype(BF)


def f32sum(a, b):
    return a.astype(F32) + b.astype(F32)


def y_shift(s):
    return [(x * 4 + y, x * 4 + (y + s) % 4) for x in range(2) for y in range(4)]


def z_shift(s):
    return [
        (x * 8 + z * 2 + c, x * 8 + ((z + s) % 4) * 2 + c)
        for x in range(2)
        for z in range(4)
        for c in range(2)
    ]


X_LO = [(i, (i + 4) % 8) for i in range(8)]
X_HI = [(i, (i + 8) % 16) for i in range(16)]
CORE = [(i, i ^ 1) for i in range(16)]


def up(v):
    return lax.ppermute(v, "load", y_shift(1))


def down(v):
    return lax.ppermute(v, "load", y_shift(3))


def across(v):
    return lax.ppermute(v, "load", X_LO)


def other_core(v):
    return lax.ppermute(v, "leaf", CORE)


def other_half(v):
    return lax.ppermute(v, "leaf", X_HI)


def along_z(v, s):
    return lax.ppermute(v, "leaf", z_shift(s))


VMEM = pl.BlockSpec(memory_space=pltpu.VMEM)
SMEM = pl.BlockSpec(memory_space=pltpu.SMEM)


def spec(block, index):
    return pl.BlockSpec(block, index)


def shape(dims, dtype=BF):
    return jax.ShapeDtypeStruct(dims, dtype)


def small_kernel(offs, *refs):
    blocks, (root_ref, sep_ref, full) = refs[:8], refs[8:]
    for k, block in enumerate(blocks):
        rows = block[...].reshape(144, 256)
        at = pl.multiple_of(offs[k] * 32, 32)
        for m in range(4):
            full[m, pl.ds(at, 32), :] = rows[32 * m : 32 * m + 32]
    for m, out in ((0, root_ref), (2, sep_ref)):
        inv, cpl = full[m], full[m + 1]
        out[0] = mm(cpl, inv).astype(BF)
        out[1] = mmt(inv, inv).astype(BF)


def small_blocks(offs, blocks):
    head = spec((3, 48, 256), lambda i: (0, 0, 0))
    return pl.pallas_call(
        small_kernel,
        grid=(1,),
        in_specs=[SMEM] + [head] * 8,
        out_specs=[spec((2, 256, 256), lambda i: (0, 0, 0))] * 2,
        out_shape=[shape((2, 256, 256))] * 2,
        scratch_shapes=[pltpu.VMEM((4, 256, 256), BF)],
        cost_estimate=pl.CostEstimate(flops=4 * 2**25, bytes_accessed=2**20, transcendentals=0),
    )(offs, *blocks)


STEP = 4


def forward_kernel(split, offs, *refs):
    blocks = refs[:9]
    rhs, rows, before, m_ref, inv_ref, total, inv, upd = refs[9:]
    step = pl.program_id(0)

    @pl.when(step == 0)
    def _():
        total[...] = before[...]

    at = [offs[k] for k in range(8)]

    def place(i, k, rows48):
        inv[i, pl.ds(pl.multiple_of(at[k] * 32, 32), 32), :] = rows48[:32]
        upd[i, pl.ds(pl.multiple_of(at[k] * 16, 16), 16), :] = rows48[32:]

    for i in range(STEP):
        for k in range(7):
            place(i, k, blocks[k][i])

    @pl.when(step < split)
    def _():
        for i in range(STEP):
            place(i, 7, blocks[7][i])

    @pl.when(step >= split)
    def _():
        for i in range(STEP):
            place(i, 7, blocks[8][i])

    inv_ref[...] = inv[...]
    parts = []
    for i in range(STEP):
        s = mm(upd[i], inv[i]).astype(BF)
        hot = (lax.broadcasted_iota(jnp.int32, (256, 128), 0) == rows[i]).astype(BF)
        m = mm(hot, s).astype(BF)
        m_ref[i] = m
        parts.append(m)
    total[...] += mm(jnp.concatenate(parts, axis=1), rhs[...].reshape(STEP * 256, 512))


def leaves_forward(offs, blocks, skips, rest, rhs, first, rows, before):
    count = 12
    split = 8 // STEP
    specs = []
    for skip in skips:
        specs.append(skip)
    lead = [
        spec((pl.Element(STEP), pl.Element(48), pl.Element(256)), lambda i, s=s: (i * STEP + s, 0, 0))
        for s in skips
    ]
    lead.append(spec((STEP, 48, 256), lambda i: (jnp.minimum(i, split - 1), 0, 0)))
    lead.append(spec((STEP, 48, 256), lambda i: (jnp.maximum(i - split, 0), 0, 0)))
    return pl.pallas_call(
        functools.partial(forward_kernel, split),
        grid=(count // STEP,),
        in_specs=[SMEM]
        + lead
        + [
            spec((STEP, 256, 512), lambda i: (i + first // STEP, 0, 0)),
            spec((STEP, 1, 128), lambda i: (i + first // STEP, 0, 0)),
            spec((256, 512), lambda i: (0, 0)),
        ],
        out_specs=[
            spec((STEP, 256, 256), lambda i: (i, 0, 0)),
            spec((STEP, 256, 256), lambda i: (i, 0, 0)),
            spec((256, 512), lambda i: (0, 0)),
        ],
        out_shape=[shape((count, 256, 256)), shape((count, 256, 256)), shape((256, 512), F32)],
        scratch_shapes=[pltpu.VMEM((STEP, 256, 256), BF), pltpu.VMEM((STEP, 128, 256), BF)],
        cost_estimate=pl.CostEstimate(flops=2**31, bytes_accessed=12 * 2**20, transcendentals=0),
    )(offs, *blocks, *rest, rhs, rows, before)


def prepare_kernel(inv, m, out):
    for i in range(STEP):
        out[i, :, :256] = mmt(inv[i], inv[i]).astype(BF)
        out[i, :, 256:] = -(m[i].T)


def prepare(inv, m):
    count = inv.shape[0]
    block = spec((STEP, 256, 256), lambda i: (i, 0, 0))
    return pl.pallas_call(
        prepare_kernel,
        grid=(count // STEP,),
        in_specs=[block, block],
        out_specs=spec((STEP, 256, 512), lambda i: (i, 0, 0)),
        out_shape=shape((count, 256, 512)),
        cost_estimate=pl.CostEstimate(flops=2**29, bytes_accessed=6 * 2**20, transcendentals=0),
    )(inv, m)


def root_kernel(place, rhs, total, mats, r_ref, keep, send):
    r = sub(rhs[0], total[...])
    r_ref[...] = r
    flow = mm(mats[0], r).astype(BF)

    @pl.when(place[0] == 0)
    def _():
        keep[...] = flow[:, :256]
        send[...] = flow[:, 256:]

    @pl.when(place[0] == 1)
    def _():
        keep[...] = flow[:, 256:]
        send[...] = flow[:, :256]


def level_one_kernel(rhs, mine, theirs, mats, r_ref, flow):
    r = sub(rhs[...], f32sum(mine[...], theirs[...]))
    r_ref[...] = r
    flow[...] = mm(mats[0], r).astype(BF)


def middle_kernel(place, f0, f1, f2, f3, rhs, a, r_out, flow, flows):
    z = place[1]
    for k, f in enumerate((f0, f1, f2, f3)):
        flows[lax.rem(z - k + 4, 4)] = f[...]
    i0, i1, i2 = place[2], place[3], place[4]
    r0 = sub(rhs[i0], f32sum(flows[0], flows[1]))
    r2 = sub(rhs[i2], f32sum(flows[2], flows[3]))
    g0 = mm(a[i0], r0).astype(BF)
    g2 = mm(a[i2], r2).astype(BF)
    r1 = sub(rhs[i1], f32sum(g0, g2))
    flow[...] = mm(a[i1], r1).astype(BF)
    r_out[0] = r0
    r_out[1] = r1
    r_out[2] = r2


def top_kernel(place, mine, theirs, rhs, a, g, rs, r_even, even, above, out, ans):
    i0, i1, i2, i3 = place[2], place[3], place[4], place[5]
    i7, i15 = place[6], place[7]
    r7 = sub(rhs[i7], f32sum(mine[...], theirs[...]))
    f7 = mm(a[i7], r7).astype(BF)
    r15 = sub(rhs[i15], f7.astype(F32))
    x15 = (mm(g[i15], r15) - mmt(a[i15], above[...])).astype(BF)
    x7 = (mm(g[i7], r7) - mmt(a[i7], x15)).astype(BF)
    x1 = (mm(g[i1], rs[1]) - mmt(a[i1], x7)).astype(BF)
    x0 = (mm(g[i0], rs[0]) - mmt(a[i0], x1)).astype(BF)
    x2 = (mm(g[i2], rs[2]) - mmt(a[i2], x1)).astype(BF)
    ans[0] = x0
    ans[1] = x1
    ans[2] = x2
    ans[3] = jnp.where(place[8] == 0, x7, x15)
    parent = ans[place[9]]
    out[0] = (mm(even[1], r_even[...]) - mmt(even[0], parent)).astype(BF)
    out[1] = ans[place[1]]


def call(kernel, outs, *args, scratch=(), flops=2**26):
    specs = [SMEM if a.dtype == jnp.int32 else VMEM for a in args]
    return pl.pallas_call(
        kernel,
        in_specs=specs,
        out_specs=[VMEM] * len(outs),
        out_shape=[shape(o) for o in outs],
        scratch_shapes=list(scratch),
        cost_estimate=pl.CostEstimate(flops=flops, bytes_accessed=2**20, transcendentals=0),
    )(*args)


def backward_kernel(place, r, mats, mine, theirs, rhs, gm, leaf_out, root_out, sep_out, answer):
    @pl.when(pl.program_id(0) == 0)
    def _():
        core = place[0]
        first = jnp.where(core == 0, mine[...], theirs[...])
        second = jnp.where(core == 0, theirs[...], mine[...])
        parent = jnp.concatenate([first[0], second[0]], axis=1)
        value = (mm(mats[1], r[...]) - mmt(mats[0], parent)).astype(BF)
        answer[...] = value
        root_out[0] = value
        odd = jnp.concatenate([first[1], second[1]], axis=1)
        sep_out[0] = jnp.where(core == 0, parent, odd)

    for i in range(rhs.shape[0]):
        leaf_out[i] = (mm(gm[i, :, :256], rhs[i]) + mm(gm[i, :, 256:], answer[...])).astype(BF)


def backward(place, r, mats, mine, theirs, rhs, gm):
    step = 4
    whole = lambda *dims: spec(dims, lambda i: (0,) * len(dims))
    return pl.pallas_call(
        backward_kernel,
        grid=(24 // step,),
        in_specs=[
            SMEM,
            whole(256, 512),
            whole(2, 256, 256),
            whole(2, 256, 256),
            whole(2, 256, 256),
            spec((step, 256, 512), lambda i: (i, 0, 0)),
            spec((step, 256, 512), lambda i: (i, 0, 0)),
        ],
        out_specs=[
            spec((step, 256, 512), lambda i: (i, 0, 0)),
            whole(1, 256, 512),
            whole(1, 256, 512),
        ],
        out_shape=[shape((24, 256, 512)), shape((1, 256, 512)), shape((1, 256, 512))],
        scratch_shapes=[pltpu.VMEM((256, 512), BF)],
        cost_estimate=pl.CostEstimate(flops=2**32, bytes_accessed=18 * 2**20, transcendentals=0),
    )(place, r, mats, mine, theirs, rhs, gm)


def local(
    rhs_leaves,
    rhs_roots,
    rhs_seps,
    above_solution,
    leaf_inverse,
    leaf_update,
    leaf_rows,
    root_inverse,
    root_coupling,
    sep_inverse,
    sep_coupling,
):
    position = lax.axis_index("leaf")
    core, z, x_hi = position % 2, (position // 2) % 4, position // 8
    load = lax.axis_index("load")
    x, y = load // 4, load % 4
    rel = [(x, y), (x, y + 3), (x, y + 1), (x, y + 2), (1 - x, y), (1 - x, y + 3), (1 - x, y + 1), (1 - x, y + 2)]
    offs = jnp.stack([a * 4 + b % 4 for a, b in rel]).astype(jnp.int32)
    index = [(z + 4 - j) % 4 for j in range(4)]
    i7 = jnp.where(x_hi == 0, index[3], 4)
    i15 = jnp.where(x_hi == 0, 4, index[3])
    place = jnp.stack([core, z, *index, i7, i15, x_hi, (z // 2) * 2]).astype(jnp.int32)

    pad = jnp.zeros((16, 256), BF)
    small = jnp.concatenate(
        [root_inverse[0], root_coupling[0], sep_inverse[0], sep_coupling[0], pad], axis=0
    ).reshape(3, 48, 256)
    both = jnp.concatenate([leaf_inverse, leaf_update], axis=1)
    w1 = jnp.concatenate([small, both[:12]], axis=0)
    w2 = both[12:]
    a1, b1, c1 = up(w1), down(w1), across(w1)
    a2, b2, c2 = up(w2), down(w2), across(w2)
    d1, bm1, am1 = up(a1), down(c1), across(a1)
    e2, am2, bm2 = down(b2), up(c2), across(b2)
    s_opp = across(d1[:3])
    g1, k1 = up(am1[3:11]), across(d1[11:])
    g2, k2 = down(bm2[:8]), across(e2[8:])
    blocks1 = [w1, a1, b1, d1, c1, am1, bm1]
    blocks2 = [w2, a2, b2, e2, c2, am2, bm2]

    own_half = lax.dynamic_slice(rhs_seps[0], (0, core * 256), (256, 256))
    far_half = lax.dynamic_slice(rhs_seps[0], (0, (1 - core) * 256), (256, 256))
    got = other_core(far_half)
    rhs_even = jnp.where(core == 0, own_half, got)
    rhs_odd = jnp.where(core == 0, got, own_half)
    rhs_z = [rhs_odd] + [along_z(rhs_odd, s) for s in (1, 2, 3)]
    rhs_z = jnp.stack(rhs_z)
    rhs_hi = other_half(lax.dynamic_index_in_dim(rhs_z, index[3], 0, False))
    rhs_tree = jnp.concatenate([rhs_z, rhs_hi[None]], axis=0)
    above = lax.dynamic_slice(above_solution, (0, core * 256), (256, 256))

    root_mats, sep_mats = small_blocks(offs, blocks1 + [s_opp])
    sep_got = other_core(sep_mats)
    even = jnp.where(core == 0, sep_mats, sep_got)
    odd = jnp.where(core == 0, sep_got[0], sep_mats[1])
    odd_z = jnp.stack([odd] + [along_z(odd, s) for s in (1, 2, 3)])
    odd_hi = other_half(lax.dynamic_index_in_dim(odd_z, index[3], 0, False))
    mine = jnp.concatenate([odd_z, odd_hi[None]], axis=0)
    theirs = other_core(mine)
    mats_a = jnp.where(core == 0, mine, theirs)
    mats_g = jnp.where(core == 0, theirs, mine)

    rows = leaf_rows.reshape(24, 1, 128)
    nothing = jnp.zeros((256, 512), F32)
    m1, inv1, total = leaves_forward(
        offs, blocks1, [3] * 7, [g1, k1], rhs_leaves, 0, rows, nothing
    )
    m2, inv2, total = leaves_forward(
        offs, blocks2, [0] * 7, [g2, k2], rhs_leaves, 12, rows, total
    )
    gm = jnp.concatenate([prepare(inv1, m1), prepare(inv2, m2)], axis=0)

    r_root, keep, send = call(
        root_kernel, [(256, 512), (256, 256), (256, 256)], place, rhs_roots, total, root_mats
    )
    r_even, flow = call(
        level_one_kernel, [(256, 256), (256, 256)], rhs_even, keep, other_core(send), even
    )
    flows = [flow] + [along_z(flow, s) for s in (1, 2, 3)]
    rs, flow = call(
        middle_kernel,
        [(3, 256, 256), (256, 256)],
        place,
        *flows,
        rhs_tree,
        mats_a,
        scratch=[pltpu.VMEM((4, 256, 256), BF)],
    )
    (answers,) = call(
        top_kernel,
        [(2, 256, 256)],
        place,
        flow,
        other_half(flow),
        rhs_tree,
        mats_a,
        mats_g,
        rs,
        r_even,
        even,
        above,
        scratch=[pltpu.VMEM((4, 256, 256), BF)],
    )
    leaf, root, sep = backward(
        place, r_root, root_mats, answers, other_core(answers), rhs_leaves, gm
    )
    return leaf, root, sep


def solution(mesh):
    rows = P("leaf", "load", None)
    columns = P("leaf", None, "load")
    in_specs = (columns, columns, columns, P(None, "load"), rows, rows, P("leaf", None)) + (rows,) * 4
    return jax.shard_map(
        local, mesh=mesh, in_specs=in_specs, out_specs=(columns,) * 3, check_vma=False
    )
```

time: 320 us -> 152 us (0.47)
  the two profiles are of different devices: /device:TPU:4 before, /device:TPU:1 now
where the time goes in v1:
time: 152 us; the launch traced here: 151 us
  Pallas kernels  47.2 us (31%)
  starting transfers between devices  45.7 us (30%)
  waiting for transfers between devices  28.1 us (18%)
  local copies, waits for them, and re-layouts  18.7 us (12%)
  other arithmetic  10.5 us (7%)
    ppermute x9, starting transfers between devices, along_z(): return lax.ppermute(v, 'leaf', z_shift(s))  15.3 us
    pallas_call x2, Pallas kernels, leaves_forward(): pl.pallas_call(functools.partial(forward_kernel, split), grid=(count // S...  13.5 us
    pallas_call x4, Pallas kernels, call(): pl.pallas_call(kernel, in_specs=specs, out_specs=[VMEM] * len(outs), out_...  11.1 us
    pallas_call x1, Pallas kernels, backward(): pl.pallas_call(backward_kernel, grid=(24 // step,), in_specs=[SMEM, whole...  10.7 us
    unnamed x63, local copies, waits for them, and re-layouts  9.94 us
    pallas_call x2, Pallas kernels, prepare(): pl.pallas_call(prepare_kernel, grid=(count // STEP,), in_specs=[block, bl...  9.7 us
    ppermute x9, waiting for transfers between devices, along_z(): return lax.ppermute(v, 'leaf', z_shift(s))  8.98 us
    ppermute x5, waiting for transfers between devices, up(): return lax.ppermute(v, 'load', y_shift(1))  8.75 us
  transfers between devices with their start and end apart: 34, of which 11 were waited for; matrix products, arithmetic and copies ran while one was open for 13% of the time, Pallas kernels for 20%

profile of v1, /device:TPU:1, one launch (start us, length us, event | category | flops | bytes accessed | tf_op | source)
XLA Modules:
  0.0 151.2 jit_solution(224034516184541974)
XLA Ops:
  0.7 0.8 constant_dynamic-update-slice_fusion.6
  1.4 0.7 constant_dynamic-update-slice_fusion.5
  2.2 0.7 constant_dynamic-update-slice_fusion.4
  2.9 0.7 constant_dynamic-update-slice_fusion.3
  3.6 1.0 constant_dynamic-update-slice_fusion.1
  4.6 0.9 constant_dynamic-update-slice_fusion
  5.6 0.8 fusion.8
  6.4 2.2 %collective-permute-start.8 = (bf16[15,48,256]{2,1,0:T(8,128)(2,1)S(1)}, bf16[15,48,256]{2,1,0:T(8,128)(2,1)S(1)}, u32[]{:S(2)}, u32[]{:S(2)}) collective-permute-start(bf16[15,48,256]{2,1,0:T(8,128)(2,1)S(1)} %pad_maximum_fusion.1.refs_0_), channel_id=1, source_target_pairs={{0,1},{1,2},{2,3},{3,0},{4,5},{5,6},{6,7},{7,4},{8,9},{9,10},{10,1... | collective-permute-start | bytes 1105928 | tf_op jit(solution)/shard_map/ppermute | solution.py:49
  8.6 1.2 collective-permute-start.11
  9.8 1.3 collective-permute-start.17
  11.1 1.4 collective-permute-start.9
  12.5 0.7 stack.107.offs
  13.8 4.3 %collective-permute-done.8.refs_1_ = bf16[15,48,256]{2,1,0:T(8,128)(2,1)S(1)} collective-permute-done((bf16[15,48,256]{2,1,0:T(8,128)(2,1)S(1)}, bf16[15,48,256]{2,1,0:T(8,128)(2,1)S(1)}, u32[]{:S(2)}, u32[]{:S(2)}) %collective-permute-start.8) | collective-permute-done | bytes 368672 | tf_op jit(solution)/shard_map/ppermute | solution.py:49
  18.2 1.6 %collective-permute-start.23 = (bf16[256,256]{1,0:T(8,128)(2,1)S(1)}, bf16[256,256]{1,0:T(8,128)(2,1)S(1)}, u32[]{:S(2)}, u32[]{:S(2)}) collective-permute-start(bf16[256,256]{1,0:T(8,128)(2,1)S(1)} %get-tuple-element.36), channel_id=1, source_target_pairs={{0,16},{8,24},{16,32},{24,40},{32,48},{40,56},{48,0},{56,8},{64,80... | collective-permute-start | bytes 393224 | tf_op jit(solution)/shard_map/ppermute | solution.py:69
  19.8 1.2 collective-permute-start.12
  21.1 2.7 %collective-permute-start.13 = (bf16[15,48,256]{2,1,0:T(8,128)(2,1)S(1)}, bf16[15,48,256]{2,1,0:T(8,128)(2,1)S(1)}, u32[]{:S(2)}, u32[]{:S(2)}) collective-permute-start(bf16[15,48,256]{2,1,0:T(8,128)(2,1)S(1)} %collective-permute-done.11.refs_4_), channel_id=1, source_target_pairs={{0,3},{1,0},{2,1},{3,2},{4,7},{5,4},{6,5},{7,6},{8,11},{9,8},{10,9... | collective-permute-start | bytes 1105928 | tf_op jit(solution)/shard_map/ppermute | solution.py:53
  23.8 1.6 %bitcast_select_fusion.1.rhs = bf16[256,256]{1,0:T(8,128)(2,1)} fusion(bf16[256,256]{1,0:T(8,128)(2,1)} %copy-done.14, pred[]{:T(512)S(6)} %eq.29, bf16[1,256,512]{2,1,0:T(8,128)(2,1)} %param.13, s32[]{:T(128)S(6)} %select_n.148), kind=kLoop, calls=%fused_computation.25 | loop fusion | flops 65536 | bytes 393221 | tf_op jit(solution)/shard_map/jit(_where)/select_n | solution.py:362
  25.4 2.2 %collective-permute-start.25 = (bf16[256,256]{1,0:T(8,128)(2,1)S(1)}, bf16[256,256]{1,0:T(8,128)(2,1)S(1)}, u32[]{:S(2)}, u32[]{:S(2)}) collective-permute-start(bf16[256,256]{1,0:T(8,128)(2,1)S(1)} %get-tuple-element.36), channel_id=1, source_target_pairs={{0,48},{8,56},{16,0},{24,8},{32,16},{40,24},{48,32},{56,40},{64,11... | collective-permute-start | bytes 393224 | tf_op jit(solution)/shard_map/ppermute | solution.py:69
  28.1 3.4 %collective-permute-start.24 = (bf16[256,256]{1,0:T(8,128)(2,1)S(1)}, bf16[256,256]{1,0:T(8,128)(2,1)S(1)}, u32[]{:S(2)}, u32[]{:S(2)}) collective-permute-start(bf16[256,256]{1,0:T(8,128)(2,1)S(1)} %get-tuple-element.36), channel_id=1, source_target_pairs={{0,32},{8,40},{16,48},{24,56},{32,0},{40,8},{48,16},{56,24},{64,96... | collective-permute-start | bytes 393224 | tf_op jit(solution)/shard_map/ppermute | solution.py:69
  31.7 2.1 %collective-permute-done.24 = bf16[256,256]{1,0:T(8,128)(2,1)S(1)} collective-permute-done((bf16[256,256]{1,0:T(8,128)(2,1)S(1)}, bf16[256,256]{1,0:T(8,128)(2,1)S(1)}, u32[]{:S(2)}, u32[]{:S(2)}) %collective-permute-start.24) | collective-permute-done | bytes 131104 | tf_op jit(solution)/shard_map/ppermute | solution.py:69
  33.8 1.2 collective-permute-start.16
  35.0 0.8 fusion.7
  36.1 2.7 %collective-permute-start.26 = (bf16[256,256]{1,0:T(8,128)(2,1)}, bf16[256,256]{1,0:T(8,128)(2,1)}, u32[]{:S(2)}, u32[]{:S(2)}) collective-permute-start(bf16[256,256]{1,0:T(8,128)(2,1)} %fusion.7), channel_id=1, source_target_pairs={{0,64},{8,72},{16,80},{24,88},{32,96},{40,104},{48,112},{56,120},{... | collective-permute-start | bytes 393224 | tf_op jit(solution)/shard_map/ppermute | solution.py:65
  39.6 2.2 %shard_map.132 = (bf16[2,256,256]{2,1,0:T(8,128)(2,1)}, bf16[2,256,256]{2,1,0:T(8,128)(2,1)}) custom-call(s32[8]{0:T(128)} %stack.107.offs, bf16[15,48,256]{2,1,0:T(8,128)(2,1)} %copy-done.2, bf16[15,48,256]{2,1,0:T(8,128)(2,1)} %copy-done.6, bf16[15,48,256]{2,1,0:T(8,128)(2,1)} %copy-done.8, bf16[15,48,256]{2,1,0:T(8,128)(2,1)} %copy-done.5, ...), custom_call_target="tpu_custom_call" | custom-call | flops 134217728 | bytes 1048576 | tf_op jit(solution)/shard_map/pallas_call | solution.py:99
  41.8 4.1 %collective-permute-start.19 = (bf16[2,256,256]{2,1,0:T(8,128)(2,1)}, bf16[2,256,256]{2,1,0:T(8,128)(2,1)S(1)}, u32[]{:S(2)}, u32[]{:S(2)}) collective-permute-start(bf16[2,256,256]{2,1,0:T(8,128)(2,1)} %get-tuple-element.24), channel_id=1, source_target_pairs={{0,8},{8,0},{16,24},{24,16},{32,40},{40,32},{48,56},{56,48},{64,72... | collective-permute-start | bytes 786440 | tf_op jit(solution)/shard_map/ppermute | solution.py:61
  45.9 0.9 constant_dynamic-update-slice_fusion.8
  47.2 0.9 constant_dynamic-update-slice_fusion.7
  48.1 1.1 collective-permute-start.2
  49.2 0.9 constant_dynamic-update-slice_fusion.14
  50.1 2.7 %collective-permute-start.29 = (bf16[256,256]{1,0:T(8,128)(2,1)S(1)}, bf16[256,256]{1,0:T(8,128)(2,1)S(1)}, u32[]{:S(2)}, u32[]{:S(2)}) collective-permute-start(bf16[256,256]{1,0:T(8,128)(2,1)S(1)} %bitcast.57), channel_id=1, source_target_pairs={{0,48},{8,56},{16,0},{24,8},{32,16},{40,24},{48,32},{56,40},{64,11... | collective-permute-start | bytes 393224 | tf_op jit(solution)/shard_map/ppermute | solution.py:69
  52.8 2.9 %collective-permute-done.5.refs_6_ = bf16[12,48,256]{2,1,0:T(8,128)(2,1)S(1)} collective-permute-done((bf16[12,48,256]{2,1,0:T(8,128)(2,1)}, bf16[12,48,256]{2,1,0:T(8,128)(2,1)S(1)}, u32[]{:S(2)}, u32[]{:S(2)}) %collective-permute-start.5) | collective-permute-done | bytes 294944 | tf_op jit(solution)/shard_map/ppermute | solution.py:57
  55.7 1.3 collective-permute-start.27
  57.0 0.9 bitcast_dynamic-update-slice_fusion.1.rhs
  58.0 0.8 slice.37
  59.5 0.9 slice.40
  60.4 0.9 slice.41
  61.3 2.7 %collective-permute-start.6 = (bf16[8,48,256]{2,1,0:T(8,128)(2,1)}, bf16[8,48,256]{2,1,0:T(8,128)(2,1)}, u32[]{:S(2)}, u32[]{:S(2)}) collective-permute-start(bf16[8,48,256]{2,1,0:T(8,128)(2,1)} %slice.37), channel_id=1, source_target_pairs={{0,3},{1,0},{2,1},{3,2},{4,7},{5,4},{6,5},{7,6},{8,11},{9,8},{10,9... | collective-permute-start | bytes 589832 | tf_op jit(solution)/shard_map/ppermute | solution.py:53
  64.2 2.1 %collective-permute-start.30 = (bf16[256,256]{1,0:T(8,128)(2,1)S(1)}, bf16[256,256]{1,0:T(8,128)(2,1)S(1)}, u32[]{:S(2)}, u32[]{:S(2)}) collective-permute-start(bf16[256,256]{1,0:T(8,128)(2,1)S(1)} %fusion.3), channel_id=1, source_target_pairs={{0,64},{8,72},{16,80},{24,88},{32,96},{40,104},{48,112},{56,120},{... | collective-permute-start | bytes 393224 | tf_op jit(solution)/shard_map/ppermute | solution.py:65
  66.3 3.3 %collective-permute-done.30 = bf16[256,256]{1,0:T(8,128)(2,1)S(1)} collective-permute-done((bf16[256,256]{1,0:T(8,128)(2,1)S(1)}, bf16[256,256]{1,0:T(8,128)(2,1)S(1)}, u32[]{:S(2)}, u32[]{:S(2)}) %collective-permute-start.30) | collective-permute-done | bytes 131104 | tf_op jit(solution)/shard_map/ppermute | solution.py:65
  70.2 3.2 %collective-permute-done.15.refs_8_ = bf16[4,48,256]{2,1,0:T(8,128)(2,1)S(1)} collective-permute-done((bf16[4,48,256]{2,1,0:T(8,128)(2,1)S(1)}, bf16[4,48,256]{2,1,0:T(8,128)(2,1)S(1)}, u32[]{:S(2)}, u32[]{:S(2)}) %collective-permute-start.15) | collective-permute-done | bytes 98336 | tf_op jit(solution)/shard_map/ppermute | solution.py:57
  74.1 4.0 %collective-permute-done.14.refs_7_ = bf16[8,48,256]{2,1,0:T(8,128)(2,1)S(1)} collective-permute-done((bf16[8,48,256]{2,1,0:T(8,128)(2,1)S(1)}, bf16[8,48,256]{2,1,0:T(8,128)(2,1)S(1)}, u32[]{:S(2)}, u32[]{:S(2)}) %collective-permute-start.14) | collective-permute-done | bytes 196640 | tf_op jit(solution)/shard_map/ppermute | solution.py:49
  78.1 0.7 copy-done.18
  78.8 2.0 %collective-permute-start.31 = (bf16[5,256,256]{2,1,0:T(8,128)(2,1)S(1)}, bf16[5,256,256]{2,1,0:T(8,128)(2,1)S(1)}, u32[]{:S(2)}, u32[]{:S(2)}) collective-permute-start(bf16[5,256,256]{2,1,0:T(8,128)(2,1)S(1)} %bitcast_dynamic-update-slice_fusion), channel_id=1, source_target_pairs={{0,8},{8,0},{16,24},{24,16},{32,40},{40,32},{48,56},{56,48},{64,72... | collective-permute-start | bytes 1966088 | tf_op jit(solution)/shard_map/ppermute | solution.py:61
  80.8 0.9 broadcast_in_dim.13.refs_11_
  81.7 6.7 %shard_map.130 = (bf16[12,256,256]{2,1,0:T(8,128)(2,1)}, bf16[12,256,256]{2,1,0:T(8,128)(2,1)}, f32[256,512]{1,0:T(8,128)}) custom-call(s32[8]{0:T(128)} %stack.107.offs, bf16[15,48,256]{2,1,0:T(8,128)(2,1)} %copy-done.2, bf16[15,48,256]{2,1,0:T(8,128)(2,1)} %copy-done.6, bf16[15,48,256]{2,1,0:T(8,128)(2,1)} %copy-done.8, bf16[15,48,256]{2,1,0:T(8,128)(2,1)} %copy-done.5, ...), custom_call_target="tpu_custom_call" | custom-call | flops 2147483648 | bytes 12582912 | tf_op jit(solution)/shard_map/pallas_call | solution.py:165
  89.2 6.8 %shard_map.131 = (bf16[12,256,256]{2,1,0:T(8,128)(2,1)}, bf16[12,256,256]{2,1,0:T(8,128)(2,1)}, f32[256,512]{1,0:T(8,128)}) custom-call(s32[8]{0:T(128)} %stack.107.offs, bf16[12,48,256]{2,1,0:T(8,128)(2,1)} %get-tuple-element.40.refs_0_, bf16[12,48,256]{2,1,0:T(8,128)(2,1)} %copy-done.17, bf16[12,48,256]{2,1,0:T(8,128)(2,1)} %collective-permute-done.1.refs_2_, ...), custom_call_target="tpu_custom_call" | custom-call | flops 2147483648 | bytes 12582912 | tf_op jit(solution)/shard_map/pallas_call | solution.py:165
  96.0 2.2 %shard_map.133 = (bf16[256,512]{1,0:T(8,128)(2,1)}, bf16[256,256]{1,0:T(8,128)(2,1)}, bf16[256,256]{1,0:T(8,128)(2,1)}) custom-call(s32[10]{0:T(128)} %stack.98.place, bf16[1,256,512]{2,1,0:T(8,128)(2,1)} %rhs.2, f32[256,512]{1,0:T(8,128)} %get-tuple-element.19.total, bf16[2,256,256]{2,1,0:T(8,128)(2,1)} %get-tuple-element.20.mats), custom_call_target="tpu_custom_call" | custom-call | flops 67108864 | bytes 1048576 | tf_op jit(solution)/shard_map/pallas_call | solution.py:265
  98.2 0.7 broadcast_select_fusion.2.mats.even
  99.0 0.8 collective-permute-done.18.theirs
  100.4 2.0 %shard_map.134 = (bf16[256,256]{1,0:T(8,128)(2,1)}, bf16[256,256]{1,0:T(8,128)(2,1)}) custom-call(bf16[256,256]{1,0:T(8,128)(2,1)} %bitcast_select_fusion.1.rhs, bf16[256,256]{1,0:T(8,128)(2,1)} %get-tuple-element.22.mine, bf16[256,256]{1,0:T(8,128)(2,1)} %copy-done.20, bf16[2,256,256]{2,1,0:T(8,128)(2,1)} %broadcast_select_fusion.2.mats.even), custom_call_target="tpu_custom_call" | custom-call | flops 67108864 | bytes 1048576 | tf_op jit(solution)/shard_map/pallas_call | solution.py:265
  102.4 2.2 %collective-permute-start.22 = (bf16[256,256]{1,0:T(8,128)(2,1)}, bf16[256,256]{1,0:T(8,128)(2,1)S(1)}, u32[]{:S(2)}, u32[]{:S(2)}) collective-permute-start(bf16[256,256]{1,0:T(8,128)(2,1)} %get-tuple-element.25.f0), channel_id=1, source_target_pairs={{0,48},{8,56},{16,0},{24,8},{32,16},{40,24},{48,32},{56,40},{64,11... | collective-permute-start | bytes 393224 | tf_op jit(solution)/shard_map/ppermute | solution.py:69
  104.7 1.2 collective-permute-start.21
  105.9 0.7 collective-permute-start.20
  106.6 1.2 broadcast_select_fusion
  108.0 3.1 %collective-permute-done.21.f2 = bf16[256,256]{1,0:T(8,128)(2,1)S(1)} collective-permute-done((bf16[256,256]{1,0:T(8,128)(2,1)}, bf16[256,256]{1,0:T(8,128)(2,1)S(1)}, u32[]{:S(2)}, u32[]{:S(2)}) %collective-permute-start.21) | collective-permute-done | bytes 131104 | tf_op jit(solution)/shard_map/ppermute | solution.py:69
  111.0 3.6 %collective-permute-done.20.f1 = bf16[256,256]{1,0:T(8,128)(2,1)S(1)} collective-permute-done((bf16[256,256]{1,0:T(8,128)(2,1)}, bf16[256,256]{1,0:T(8,128)(2,1)S(1)}, u32[]{:S(2)}, u32[]{:S(2)}) %collective-permute-start.20) | collective-permute-done | bytes 131104 | tf_op jit(solution)/shard_map/ppermute | solution.py:69
  115.3 2.8 %shard_map.135 = (bf16[3,256,256]{2,1,0:T(8,128)(2,1)}, bf16[256,256]{1,0:T(8,128)(2,1)}) custom-call(s32[10]{0:T(128)} %stack.98.place, bf16[256,256]{1,0:T(8,128)(2,1)} %get-tuple-element.25.f0, bf16[256,256]{1,0:T(8,128)(2,1)} %copy-done.23, bf16[256,256]{1,0:T(8,128)(2,1)} %copy-done.22, bf16[256,256]{1,0:T(8,128)(2,1)} %copy-done.21, ...), custom_call_target="tpu_custom_call" | custom-call | flops 67108864 | bytes 1048576 | tf_op jit(solution)/shard_map/pallas_call | solution.py:265
  118.0 1.5 %collective-permute-start.32 = (bf16[256,256]{1,0:T(8,128)(2,1)}, bf16[256,256]{1,0:T(8,128)(2,1)S(1)}, u32[]{:S(2)}, u32[]{:S(2)}) collective-permute-start(bf16[256,256]{1,0:T(8,128)(2,1)} %get-tuple-element.26.mine), channel_id=1, source_target_pairs={{0,64},{8,72},{16,80},{24,88},{32,96},{40,104},{48,112},{56,120},{... | collective-permute-start | bytes 393224 | tf_op jit(solution)/shard_map/ppermute | solution.py:65
  120.2 4.9 %shard_map.138 = bf16[12,256,512]{2,1,0:T(8,128)(2,1)} custom-call(bf16[12,256,256]{2,1,0:T(8,128)(2,1)} %get-tuple-element.31.inv, bf16[12,256,256]{2,1,0:T(8,128)(2,1)} %get-tuple-element.32.m), custom_call_target="tpu_custom_call" | custom-call | flops 536870912 | bytes 6291456 | tf_op jit(solution)/shard_map/pallas_call | solution.py:195
  125.1 4.8 %shard_map.137 = bf16[12,256,512]{2,1,0:T(8,128)(2,1)} custom-call(bf16[12,256,256]{2,1,0:T(8,128)(2,1)} %get-tuple-element.29.inv, bf16[12,256,256]{2,1,0:T(8,128)(2,1)} %get-tuple-element.30.m), custom_call_target="tpu_custom_call" | custom-call | flops 536870912 | bytes 6291456 | tf_op jit(solution)/shard_map/pallas_call | solution.py:195
  130.6 4.1 %shard_map.136.mine = bf16[2,256,256]{2,1,0:T(8,128)(2,1)} custom-call(s32[10]{0:T(128)} %stack.98.place, bf16[256,256]{1,0:T(8,128)(2,1)} %get-tuple-element.26.mine, bf16[256,256]{1,0:T(8,128)(2,1)} %copy-done.19, bf16[5,256,256]{2,1,0:T(8,128)(2,1)} %copy-done.3, bf16[5,256,256]{2,1,0:T(8,128)(2,1)} %get-tuple-element.38.a, ...), custom_call_target="tpu_custom_call" | custom-call | flops 67108864 | bytes 1048576 | tf_op jit(solution)/shard_map/pallas_call | solution.py:265
  134.7 0.8 collective-permute-start.33
  135.5 5.1 %pad_maximum_fusion.gm = bf16[24,256,512]{2,1,0:T(8,128)(2,1)} fusion(bf16[12,256,512]{2,1,0:T(8,128)(2,1)S(1)} %copy-done.1, bf16[12,256,512]{2,1,0:T(8,128)(2,1)} %shard_map.137), kind=kLoop, calls=%fused_computation | loop fusion | flops 3145728 | bytes 12582912 | tf_op jit(solution)/shard_map/concatenate | solution.py:389
  140.6 10.7 %shard_map.139 = (bf16[24,256,512]{2,1,0:T(8,128)(2,1)}, bf16[1,256,512]{2,1,0:T(8,128)(2,1)}, bf16[1,256,512]{2,1,0:T(8,128)(2,1)}) custom-call(s32[10]{0:T(128)} %stack.98.place, bf16[256,512]{1,0:T(8,128)(2,1)} %get-tuple-element.21.r, bf16[2,256,256]{2,1,0:T(8,128)(2,1)} %get-tuple-element.20.mats, bf16[2,256,256]{2,1,0:T(8,128)(2,1)} %shard_map.136.mine, ...), custom_call_target="tpu_custom_call" | custom-call | flops 4294967296 | bytes 18874368 | tf_op jit(solution)/shard_map/pallas_call | solution.py:295
  (101 shorter events, 8.5 us)
Async XLA Ops:
  0.6 118.9 %copy-start = (bf16[256,512]{1,0:T(8,128)(2,1)S(1)}, bf16[256,512]{1,0:T(8,128)(2,1)}, u32[]{:S(2)}) copy-start(bf16[256,512]{1,0:T(8,128)(2,1)} %param.14) | copy-start | bytes 786436
  0.6 9.1 %copy-start.11 = (bf16[1,256,512]{2,1,0:T(8,128)(2,1)S(1)}, bf16[1,256,512]{2,1,0:T(8,128)(2,1)}, u32[]{:S(2)}) copy-start(bf16[1,256,512]{2,1,0:T(8,128)(2,1)} %param.13) | copy-start | bytes 786436
  6.4 32.5 %copy-start.2 = (bf16[15,48,256]{2,1,0:T(8,128)(2,1)}, bf16[15,48,256]{2,1,0:T(8,128)(2,1)S(1)}, u32[]{:S(2)}) copy-start(bf16[15,48,256]{2,1,0:T(8,128)(2,1)S(1)} %pad_maximum_fusion.1.refs_0_) | copy-start | bytes 1105924
  6.4 11.8 %collective-permute-start.8 = (bf16[15,48,256]{2,1,0:T(8,128)(2,1)S(1)}, bf16[15,48,256]{2,1,0:T(8,128)(2,1)S(1)}, u32[]{:S(2)}, u32[]{:S(2)}) collective-permute-start(bf16[15,48,256]{2,1,0:T(8,128)(2,1)S(1)} %pad_maximum_fusion.1.refs_0_), channel_id=1, source_target_pairs={{0,1},{1,2},{2,3},{3,0},{4,5},{5,6},{6,7},{7,4},{8,9},{9,10},{10,1... | collective-permute-start | bytes 1105928 | tf_op jit(solution)/shard_map/ppermute | solution.py:49
  8.6 12.5 %collective-permute-start.11 = (bf16[15,48,256]{2,1,0:T(8,128)(2,1)S(1)}, bf16[15,48,256]{2,1,0:T(8,128)(2,1)S(1)}, u32[]{:S(2)}, u32[]{:S(2)}) collective-permute-start(bf16[15,48,256]{2,1,0:T(8,128)(2,1)S(1)} %pad_maximum_fusion.1.refs_0_), channel_id=1, source_target_pairs={{0,4},{1,5},{2,6},{3,7},{4,0},{5,1},{6,2},{7,3},{8,12},{9,13},{10,... | collective-permute-start | bytes 1105928 | tf_op jit(solution)/shard_map/ppermute | solution.py:57
  9.8 8.4 %collective-permute-start.17 = (bf16[256,256]{1,0:T(8,128)(2,1)S(1)}, bf16[256,256]{1,0:T(8,128)(2,1)S(1)}, u32[]{:S(2)}, u32[]{:S(2)}) collective-permute-start(bf16[256,256]{1,0:T(8,128)(2,1)S(1)} %dynamic-slice_bitcast_fusion), channel_id=1, source_target_pairs={{0,8},{8,0},{16,24},{24,16},{32,40},{40,32},{48,56},{56,48},{64,72... | collective-permute-start | bytes 393224 | tf_op jit(solution)/shard_map/ppermute | solution.py:61
  11.1 24.7 %collective-permute-start.9 = (bf16[15,48,256]{2,1,0:T(8,128)(2,1)S(1)}, bf16[15,48,256]{2,1,0:T(8,128)(2,1)S(1)}, u32[]{:S(2)}, u32[]{:S(2)}) collective-permute-start(bf16[15,48,256]{2,1,0:T(8,128)(2,1)S(1)} %pad_maximum_fusion.1.refs_0_), channel_id=1, source_target_pairs={{0,3},{1,0},{2,1},{3,2},{4,7},{5,4},{6,5},{7,6},{8,11},{9,8},{10,9... | collective-permute-start | bytes 1105928 | tf_op jit(solution)/shard_map/ppermute | solution.py:53
  18.2 20.7 %copy-start.6 = (bf16[15,48,256]{2,1,0:T(8,128)(2,1)}, bf16[15,48,256]{2,1,0:T(8,128)(2,1)S(1)}, u32[]{:S(2)}) copy-start(bf16[15,48,256]{2,1,0:T(8,128)(2,1)S(1)} %collective-permute-done.8.refs_1_) | copy-start | bytes 1105924
  18.2 9.9 %collective-permute-start.10 = (bf16[15,48,256]{2,1,0:T(8,128)(2,1)S(1)}, bf16[15,48,256]{2,1,0:T(8,128)(2,1)S(1)}, u32[]{:S(2)}, u32[]{:S(2)}) collective-permute-start(bf16[15,48,256]{2,1,0:T(8,128)(2,1)S(1)} %collective-permute-done.8.refs_1_), channel_id=1, source_target_pairs={{0,1},{1,2},{2,3},{3,0},{4,5},{5,6},{6,7},{7,4},{8,9},{9,10},{10,1... | collective-permute-start | bytes 1105928 | tf_op jit(solution)/shard_map/ppermute | solution.py:49
  18.2 2.9 %copy-start.14 = (bf16[256,256]{1,0:T(8,128)(2,1)}, bf16[256,256]{1,0:T(8,128)(2,1)S(1)}, u32[]{:S(2)}) copy-start(bf16[256,256]{1,0:T(8,128)(2,1)S(1)} %collective-permute-done.17) | copy-start | bytes 393220
  18.2 7.2 %collective-permute-start.23 = (bf16[256,256]{1,0:T(8,128)(2,1)S(1)}, bf16[256,256]{1,0:T(8,128)(2,1)S(1)}, u32[]{:S(2)}, u32[]{:S(2)}) collective-permute-start(bf16[256,256]{1,0:T(8,128)(2,1)S(1)} %get-tuple-element.36), channel_id=1, source_target_pairs={{0,16},{8,24},{16,32},{24,40},{32,48},{40,56},{48,0},{56,8},{64,80... | collective-permute-start | bytes 393224 | tf_op jit(solution)/shard_map/ppermute | solution.py:69
  19.8 19.0 %collective-permute-start.12 = (bf16[15,48,256]{2,1,0:T(8,128)(2,1)S(1)}, bf16[15,48,256]{2,1,0:T(8,128)(2,1)S(1)}, u32[]{:S(2)}, u32[]{:S(2)}) collective-permute-start(bf16[15,48,256]{2,1,0:T(8,128)(2,1)S(1)} %collective-permute-done.8.refs_1_), channel_id=1, source_target_pairs={{0,4},{1,5},{2,6},{3,7},{4,0},{5,1},{6,2},{7,3},{8,12},{9,13},{10,... | collective-permute-start | bytes 1105928 | tf_op jit(solution)/shard_map/ppermute | solution.py:57
  21.1 17.8 %copy-start.7 = (bf16[15,48,256]{2,1,0:T(8,128)(2,1)}, bf16[15,48,256]{2,1,0:T(8,128)(2,1)S(1)}, u32[]{:S(2)}) copy-start(bf16[15,48,256]{2,1,0:T(8,128)(2,1)S(1)} %collective-permute-done.11.refs_4_) | copy-start | bytes 1105924
  21.1 15.0 %collective-permute-start.13 = (bf16[15,48,256]{2,1,0:T(8,128)(2,1)S(1)}, bf16[15,48,256]{2,1,0:T(8,128)(2,1)S(1)}, u32[]{:S(2)}, u32[]{:S(2)}) collective-permute-start(bf16[15,48,256]{2,1,0:T(8,128)(2,1)S(1)} %collective-permute-done.11.refs_4_), channel_id=1, source_target_pairs={{0,3},{1,0},{2,1},{3,2},{4,7},{5,4},{6,5},{7,6},{8,11},{9,8},{10,9... | collective-permute-start | bytes 1105928 | tf_op jit(solution)/shard_map/ppermute | solution.py:53
  25.4 6.1 %collective-permute-start.25 = (bf16[256,256]{1,0:T(8,128)(2,1)S(1)}, bf16[256,256]{1,0:T(8,128)(2,1)S(1)}, u32[]{:S(2)}, u32[]{:S(2)}) collective-permute-start(bf16[256,256]{1,0:T(8,128)(2,1)S(1)} %get-tuple-element.36), channel_id=1, source_target_pairs={{0,48},{8,56},{16,0},{24,8},{32,16},{40,24},{48,32},{56,40},{64,11... | collective-permute-start | bytes 393224 | tf_op jit(solution)/shard_map/ppermute | solution.py:69
  28.1 10.8 %copy-start.5 = (bf16[15,48,256]{2,1,0:T(8,128)(2,1)}, bf16[15,48,256]{2,1,0:T(8,128)(2,1)S(1)}, u32[]{:S(2)}) copy-start(bf16[15,48,256]{2,1,0:T(8,128)(2,1)S(1)} %collective-permute-done.10.refs_3_) | copy-start | bytes 1105924
  28.1 5.8 %collective-permute-start.24 = (bf16[256,256]{1,0:T(8,128)(2,1)S(1)}, bf16[256,256]{1,0:T(8,128)(2,1)S(1)}, u32[]{:S(2)}, u32[]{:S(2)}) collective-permute-start(bf16[256,256]{1,0:T(8,128)(2,1)S(1)} %get-tuple-element.36), channel_id=1, source_target_pairs={{0,32},{8,40},{16,48},{24,56},{32,0},{40,8},{48,16},{56,24},{64,96... | collective-permute-start | bytes 393224 | tf_op jit(solution)/shard_map/ppermute | solution.py:69
  31.5 7.3 %copy-start.15 = (bf16[256,256]{1,0:T(8,128)(2,1)}, bf16[256,256]{1,0:T(8,128)(2,1)S(1)}, u32[]{:S(2)}) copy-start(bf16[256,256]{1,0:T(8,128)(2,1)S(1)} %collective-permute-done.25) | copy-start | bytes 393220
  31.5 15.3 %collective-permute-start.1 = (bf16[12,48,256]{2,1,0:T(8,128)(2,1)}, bf16[12,48,256]{2,1,0:T(8,128)(2,1)}, u32[]{:S(2)}, u32[]{:S(2)}) collective-permute-start(bf16[12,48,256]{2,1,0:T(8,128)(2,1)} %get-tuple-element.40.refs_0_), channel_id=1, source_target_pairs={{0,3},{1,0},{2,1},{3,2},{4,7},{5,4},{6,5},{7,6},{8,11},{9,8},{10,9... | collective-permute-start | bytes 884744 | tf_op jit(solution)/shard_map/ppermute | solution.py:53
  33.8 5.0 %copy-start.16 = (bf16[256,256]{1,0:T(8,128)(2,1)}, bf16[256,256]{1,0:T(8,128)(2,1)S(1)}, u32[]{:S(2)}) copy-start(bf16[256,256]{1,0:T(8,128)(2,1)S(1)} %collective-permute-done.24) | copy-start | bytes 393220
  33.8 5.0 %collective-permute-start.16 = (bf16[3,48,256]{2,1,0:T(8,128)(2,1)S(1)}, bf16[3,48,256]{2,1,0:T(8,128)(2,1)}, u32[]{:S(2)}, u32[]{:S(2)}) collective-permute-start(bf16[3,48,256]{2,1,0:T(8,128)(2,1)S(1)} %slice.42), channel_id=1, source_target_pairs={{0,4},{1,5},{2,6},{3,7},{4,0},{5,1},{6,2},{7,3},{8,12},{9,13},{10,... | collective-permute-start | bytes 221192 | tf_op jit(solution)/shard_map/ppermute | solution.py:57
  35.8 3.1 %copy-start.8 = (bf16[15,48,256]{2,1,0:T(8,128)(2,1)}, bf16[15,48,256]{2,1,0:T(8,128)(2,1)S(1)}, u32[]{:S(2)}) copy-start(bf16[15,48,256]{2,1,0:T(8,128)(2,1)S(1)} %collective-permute-done.9.refs_2_) | copy-start | bytes 1105924
  35.8 22.9 %collective-permute-start.3 = (bf16[12,48,256]{2,1,0:T(8,128)(2,1)}, bf16[12,48,256]{2,1,0:T(8,128)(2,1)}, u32[]{:S(2)}, u32[]{:S(2)}) collective-permute-start(bf16[12,48,256]{2,1,0:T(8,128)(2,1)} %get-tuple-element.40.refs_0_), channel_id=1, source_target_pairs={{0,4},{1,5},{2,6},{3,7},{4,0},{5,1},{6,2},{7,3},{8,12},{9,13},{10,... | collective-permute-start | bytes 884744 | tf_op jit(solution)/shard_map/ppermute | solution.py:57
  36.1 2.8 %copy-start.9 = (bf16[15,48,256]{2,1,0:T(8,128)(2,1)}, bf16[15,48,256]{2,1,0:T(8,128)(2,1)S(1)}, u32[]{:S(2)}) copy-start(bf16[15,48,256]{2,1,0:T(8,128)(2,1)S(1)} %collective-permute-done.13.refs_6_) | copy-start | bytes 1105924
  36.1 16.7 %collective-permute-start.26 = (bf16[256,256]{1,0:T(8,128)(2,1)}, bf16[256,256]{1,0:T(8,128)(2,1)}, u32[]{:S(2)}, u32[]{:S(2)}) collective-permute-start(bf16[256,256]{1,0:T(8,128)(2,1)} %fusion.7), channel_id=1, source_target_pairs={{0,64},{8,72},{16,80},{24,88},{32,96},{40,104},{48,112},{56,120},{... | collective-permute-start | bytes 393224 | tf_op jit(solution)/shard_map/ppermute | solution.py:65
  38.8 0.7 copy-start.4
  41.8 7.4 %collective-permute-start.19 = (bf16[2,256,256]{2,1,0:T(8,128)(2,1)}, bf16[2,256,256]{2,1,0:T(8,128)(2,1)S(1)}, u32[]{:S(2)}, u32[]{:S(2)}) collective-permute-start(bf16[2,256,256]{2,1,0:T(8,128)(2,1)} %get-tuple-element.24), channel_id=1, source_target_pairs={{0,8},{8,0},{16,24},{24,16},{32,40},{40,32},{48,56},{56,48},{64,72... | collective-permute-start | bytes 786440 | tf_op jit(solution)/shard_map/ppermute | solution.py:61
  46.8 8.9 %collective-permute-start.5 = (bf16[12,48,256]{2,1,0:T(8,128)(2,1)}, bf16[12,48,256]{2,1,0:T(8,128)(2,1)S(1)}, u32[]{:S(2)}, u32[]{:S(2)}) collective-permute-start(bf16[12,48,256]{2,1,0:T(8,128)(2,1)} %collective-permute-done.1.refs_2_), channel_id=1, source_target_pairs={{0,4},{1,5},{2,6},{3,7},{4,0},{5,1},{6,2},{7,3},{8,12},{9,13},{10,... | collective-permute-start | bytes 884744 | tf_op jit(solution)/shard_map/ppermute | solution.py:57
  48.1 10.6 %collective-permute-start.2 = (bf16[12,48,256]{2,1,0:T(8,128)(2,1)}, bf16[12,48,256]{2,1,0:T(8,128)(2,1)S(1)}, u32[]{:S(2)}, u32[]{:S(2)}) collective-permute-start(bf16[12,48,256]{2,1,0:T(8,128)(2,1)} %collective-permute-done.1.refs_2_), channel_id=1, source_target_pairs={{0,3},{1,0},{2,1},{3,2},{4,7},{5,4},{6,5},{7,6},{8,11},{9,8},{10,9... | collective-permute-start | bytes 884744 | tf_op jit(solution)/shard_map/ppermute | solution.py:53
  50.1 11.2 %collective-permute-start.29 = (bf16[256,256]{1,0:T(8,128)(2,1)S(1)}, bf16[256,256]{1,0:T(8,128)(2,1)S(1)}, u32[]{:S(2)}, u32[]{:S(2)}) collective-permute-start(bf16[256,256]{1,0:T(8,128)(2,1)S(1)} %bitcast.57), channel_id=1, source_target_pairs={{0,48},{8,56},{16,0},{24,8},{32,16},{40,24},{48,32},{56,40},{64,11... | collective-permute-start | bytes 393224 | tf_op jit(solution)/shard_map/ppermute | solution.py:69
  52.8 11.3 %collective-permute-start.28 = (bf16[256,256]{1,0:T(8,128)(2,1)S(1)}, bf16[256,256]{1,0:T(8,128)(2,1)S(1)}, u32[]{:S(2)}, u32[]{:S(2)}) collective-permute-start(bf16[256,256]{1,0:T(8,128)(2,1)S(1)} %bitcast.58), channel_id=1, source_target_pairs={{0,32},{8,40},{16,48},{24,56},{32,0},{40,8},{48,16},{56,24},{64,96... | collective-permute-start | bytes 393224 | tf_op jit(solution)/shard_map/ppermute | solution.py:69
  55.7 32.7 %copy-start.10 = (bf16[12,48,256]{2,1,0:T(8,128)(2,1)}, bf16[12,48,256]{2,1,0:T(8,128)(2,1)S(1)}, u32[]{:S(2)}) copy-start(bf16[12,48,256]{2,1,0:T(8,128)(2,1)S(1)} %collective-permute-done.5.refs_6_) | copy-start | bytes 884740
  55.7 8.3 %collective-permute-start.27 = (bf16[256,256]{1,0:T(8,128)(2,1)S(1)}, bf16[256,256]{1,0:T(8,128)(2,1)S(1)}, u32[]{:S(2)}, u32[]{:S(2)}) collective-permute-start(bf16[256,256]{1,0:T(8,128)(2,1)S(1)} %bitcast.59), channel_id=1, source_target_pairs={{0,16},{8,24},{16,32},{24,40},{32,48},{40,56},{48,0},{56,8},{64,80... | collective-permute-start | bytes 393224 | tf_op jit(solution)/shard_map/ppermute | solution.py:69
  57.9 30.5 %copy-start.3 = (bf16[5,256,256]{2,1,0:T(8,128)(2,1)}, bf16[5,256,256]{2,1,0:T(8,128)(2,1)S(1)}, u32[]{:S(2)}) copy-start(bf16[5,256,256]{2,1,0:T(8,128)(2,1)S(1)} %bitcast_dynamic-update-slice_fusion.1.rhs) | copy-start | bytes 1966084
  58.7 29.7 %collective-permute-start = (bf16[12,48,256]{2,1,0:T(8,128)(2,1)}, bf16[12,48,256]{2,1,0:T(8,128)(2,1)S(1)}, u32[]{:S(2)}, u32[]{:S(2)}) collective-permute-start(bf16[12,48,256]{2,1,0:T(8,128)(2,1)} %get-tuple-element.40.refs_0_), channel_id=1, source_target_pairs={{0,1},{1,2},{2,3},{3,0},{4,5},{5,6},{6,7},{7,4},{8,9},{9,10},{10,1... | collective-permute-start | bytes 884744 | tf_op jit(solution)/shard_map/ppermute | solution.py:49
  58.7 29.7 %copy-start.13 = (bf16[12,48,256]{2,1,0:T(8,128)(2,1)}, bf16[12,48,256]{2,1,0:T(8,128)(2,1)S(1)}, u32[]{:S(2)}) copy-start(bf16[12,48,256]{2,1,0:T(8,128)(2,1)S(1)} %collective-permute-done.2.refs_3_) | copy-start | bytes 884740
  58.7 29.7 %collective-permute-start.4 = (bf16[12,48,256]{2,1,0:T(8,128)(2,1)}, bf16[12,48,256]{2,1,0:T(8,128)(2,1)}, u32[]{:S(2)}, u32[]{:S(2)}) collective-permute-start(bf16[12,48,256]{2,1,0:T(8,128)(2,1)} %collective-permute-done.3.refs_4_), channel_id=1, source_target_pairs={{0,1},{1,2},{2,3},{3,0},{4,5},{5,6},{6,7},{7,4},{8,9},{9,10},{10,1... | collective-permute-start | bytes 884744 | tf_op jit(solution)/shard_map/ppermute | solution.py:49
  61.3 27.2 %collective-permute-start.6 = (bf16[8,48,256]{2,1,0:T(8,128)(2,1)}, bf16[8,48,256]{2,1,0:T(8,128)(2,1)}, u32[]{:S(2)}, u32[]{:S(2)}) collective-permute-start(bf16[8,48,256]{2,1,0:T(8,128)(2,1)} %slice.37), channel_id=1, source_target_pairs={{0,3},{1,0},{2,1},{3,2},{4,7},{5,4},{6,5},{7,6},{8,11},{9,8},{10,9... | collective-permute-start | bytes 589832 | tf_op jit(solution)/shard_map/ppermute | solution.py:53
  64.1 14.0 %collective-permute-start.14 = (bf16[8,48,256]{2,1,0:T(8,128)(2,1)S(1)}, bf16[8,48,256]{2,1,0:T(8,128)(2,1)S(1)}, u32[]{:S(2)}, u32[]{:S(2)}) collective-permute-start(bf16[8,48,256]{2,1,0:T(8,128)(2,1)S(1)} %slice.40), channel_id=1, source_target_pairs={{0,1},{1,2},{2,3},{3,0},{4,5},{5,6},{6,7},{7,4},{8,9},{9,10},{10,1... | collective-permute-start | bytes 589832 | tf_op jit(solution)/shard_map/ppermute | solution.py:49
  64.2 5.4 %collective-permute-start.30 = (bf16[256,256]{1,0:T(8,128)(2,1)S(1)}, bf16[256,256]{1,0:T(8,128)(2,1)S(1)}, u32[]{:S(2)}, u32[]{:S(2)}) collective-permute-start(bf16[256,256]{1,0:T(8,128)(2,1)S(1)} %fusion.3), channel_id=1, source_target_pairs={{0,64},{8,72},{16,80},{24,88},{32,96},{40,104},{48,112},{56,120},{... | collective-permute-start | bytes 393224 | tf_op jit(solution)/shard_map/ppermute | solution.py:65
  69.6 3.9 %collective-permute-start.15 = (bf16[4,48,256]{2,1,0:T(8,128)(2,1)S(1)}, bf16[4,48,256]{2,1,0:T(8,128)(2,1)S(1)}, u32[]{:S(2)}, u32[]{:S(2)}) collective-permute-start(bf16[4,48,256]{2,1,0:T(8,128)(2,1)S(1)} %slice.41), channel_id=1, source_target_pairs={{0,4},{1,5},{2,6},{3,7},{4,0},{5,1},{6,2},{7,3},{8,12},{9,13},{10,... | collective-permute-start | bytes 294920 | tf_op jit(solution)/shard_map/ppermute | solution.py:57
  73.5 0.6 copy-start.25
  73.5 15.0 %collective-permute-start.7 = (bf16[4,48,256]{2,1,0:T(8,128)(2,1)}, bf16[4,48,256]{2,1,0:T(8,128)(2,1)S(1)}, u32[]{:S(2)}, u32[]{:S(2)}) collective-permute-start(bf16[4,48,256]{2,1,0:T(8,128)(2,1)} %slice.38), channel_id=1, source_target_pairs={{0,4},{1,5},{2,6},{3,7},{4,0},{5,1},{6,2},{7,3},{8,12},{9,13},{10,... | collective-permute-start | bytes 294920 | tf_op jit(solution)/shard_map/ppermute | solution.py:57
  78.1 0.7 copy-start.18
  78.8 27.8 %collective-permute-start.31 = (bf16[5,256,256]{2,1,0:T(8,128)(2,1)S(1)}, bf16[5,256,256]{2,1,0:T(8,128)(2,1)S(1)}, u32[]{:S(2)}, u32[]{:S(2)}) collective-permute-start(bf16[5,256,256]{2,1,0:T(8,128)(2,1)S(1)} %bitcast_dynamic-update-slice_fusion), channel_id=1, source_target_pairs={{0,8},{8,0},{16,24},{24,16},{32,40},{40,32},{48,56},{56,48},{64,72... | collective-permute-start | bytes 1966088 | tf_op jit(solution)/shard_map/ppermute | solution.py:61
  88.4 0.7 copy-start.17
  88.5 0.7 copy-start.24
  89.2 9.0 %copy-start.12 = (bf16[2,256,256]{2,1,0:T(8,128)(2,1)S(1)}, bf16[2,256,256]{2,1,0:T(8,128)(2,1)}, u32[]{:S(2)}) copy-start(bf16[2,256,256]{2,1,0:T(8,128)(2,1)} %get-tuple-element.24) | copy-start | bytes 786436
  98.2 1.6 %collective-permute-start.18 = (bf16[256,256]{1,0:T(8,128)(2,1)}, bf16[256,256]{1,0:T(8,128)(2,1)S(1)}, u32[]{:S(2)}, u32[]{:S(2)}) collective-permute-start(bf16[256,256]{1,0:T(8,128)(2,1)} %get-tuple-element.23), channel_id=1, source_target_pairs={{0,8},{8,0},{16,24},{24,16},{32,40},{40,32},{48,56},{56,48},{64,72... | collective-permute-start | bytes 393224 | tf_op jit(solution)/shard_map/ppermute | solution.py:61
  99.8 0.7 copy-start.20
  102.4 5.5 %collective-permute-start.22 = (bf16[256,256]{1,0:T(8,128)(2,1)}, bf16[256,256]{1,0:T(8,128)(2,1)S(1)}, u32[]{:S(2)}, u32[]{:S(2)}) collective-permute-start(bf16[256,256]{1,0:T(8,128)(2,1)} %get-tuple-element.25.f0), channel_id=1, source_target_pairs={{0,48},{8,56},{16,0},{24,8},{32,16},{40,24},{48,32},{56,40},{64,11... | collective-permute-start | bytes 393224 | tf_op jit(solution)/shard_map/ppermute | solution.py:69
  104.7 6.3 %collective-permute-start.21 = (bf16[256,256]{1,0:T(8,128)(2,1)}, bf16[256,256]{1,0:T(8,128)(2,1)S(1)}, u32[]{:S(2)}, u32[]{:S(2)}) collective-permute-start(bf16[256,256]{1,0:T(8,128)(2,1)} %get-tuple-element.25.f0), channel_id=1, source_target_pairs={{0,32},{8,40},{16,48},{24,56},{32,0},{40,8},{48,16},{56,24},{64,96... | collective-permute-start | bytes 393224 | tf_op jit(solution)/shard_map/ppermute | solution.py:69
  105.9 8.7 %collective-permute-start.20 = (bf16[256,256]{1,0:T(8,128)(2,1)}, bf16[256,256]{1,0:T(8,128)(2,1)S(1)}, u32[]{:S(2)}, u32[]{:S(2)}) collective-permute-start(bf16[256,256]{1,0:T(8,128)(2,1)} %get-tuple-element.25.f0), channel_id=1, source_target_pairs={{0,16},{8,24},{16,32},{24,40},{32,48},{40,56},{48,0},{56,8},{64,80... | collective-permute-start | bytes 393224 | tf_op jit(solution)/shard_map/ppermute | solution.py:69
  108.0 6.7 %copy-start.21 = (bf16[256,256]{1,0:T(8,128)(2,1)}, bf16[256,256]{1,0:T(8,128)(2,1)S(1)}, u32[]{:S(2)}) copy-start(bf16[256,256]{1,0:T(8,128)(2,1)S(1)} %collective-permute-done.22.f3) | copy-start | bytes 393220
  111.0 3.6 %copy-start.22 = (bf16[256,256]{1,0:T(8,128)(2,1)}, bf16[256,256]{1,0:T(8,128)(2,1)S(1)}, u32[]{:S(2)}) copy-start(bf16[256,256]{1,0:T(8,128)(2,1)S(1)} %collective-permute-done.21.f2) | copy-start | bytes 393220
  114.6 0.7 copy-start.23
  118.0 11.9 %collective-permute-start.32 = (bf16[256,256]{1,0:T(8,128)(2,1)}, bf16[256,256]{1,0:T(8,128)(2,1)S(1)}, u32[]{:S(2)}, u32[]{:S(2)}) collective-permute-start(bf16[256,256]{1,0:T(8,128)(2,1)} %get-tuple-element.26.mine), channel_id=1, source_target_pairs={{0,64},{8,72},{16,80},{24,88},{32,96},{40,104},{48,112},{56,120},{... | collective-permute-start | bytes 393224 | tf_op jit(solution)/shard_map/ppermute | solution.py:65
  129.9 5.6 %copy-start.1 = (bf16[12,256,512]{2,1,0:T(8,128)(2,1)S(1)}, bf16[12,256,512]{2,1,0:T(8,128)(2,1)}, u32[]{:S(2)}) copy-start(bf16[12,256,512]{2,1,0:T(8,128)(2,1)} %shard_map.138) | copy-start | bytes 9437188
  129.9 0.7 copy-start.19
  134.7 5.8 %collective-permute-start.33 = (bf16[2,256,256]{2,1,0:T(8,128)(2,1)}, bf16[2,256,256]{2,1,0:T(8,128)(2,1)}, u32[]{:S(2)}, u32[]{:S(2)}) collective-permute-start(bf16[2,256,256]{2,1,0:T(8,128)(2,1)} %shard_map.136.mine), channel_id=1, source_target_pairs={{0,8},{8,0},{16,24},{24,16},{32,40},{40,32},{48,56},{56,48},{64,72... | collective-permute-start | bytes 786440 | tf_op jit(solution)/shard_map/ppermute | solution.py:61

commit v2 on v0

v2 whole, which is shorter than its diff:
```python
import functools

import jax
import jax.numpy as jnp
from jax import lax
from jax.experimental import pallas as pl
from jax.experimental.pallas import tpu as pltpu
from jax.sharding import PartitionSpec as P

BF = jnp.bfloat16
F32 = jnp.float32

ODD = range(1, 16, 2)


def mm(a, b):
    return jnp.dot(a, b, preferred_element_type=F32)


def mmt(a, b):
    return lax.dot_general(a, b, (((0,), (0,)), ((), ())), preferred_element_type=F32)


def sub(rhs, inflow):
    return (rhs.astype(F32) - inflow).astype(BF)


def f32sum(a, b):
    return a.astype(F32) + b.astype(F32)


def y_shift(s):
    return [(x * 4 + y, x * 4 + (y + s) % 4) for x in range(2) for y in range(4)]


def z_shift(s, places):
    return [(x * 8 + z * 2 + 1, x * 8 + ((z + s) % 4) * 2 + 1) for x in range(2) for z in places]


X_LO = [(i, (i + 4) % 8) for i in range(8)]
X_HI = [(p, (p + 8) % 16) for p in ODD]
PAIR = [(p, p ^ 2) for p in ODD]
MIRROR = [(p, (p // 8) * 8 + (3 - (p // 2) % 4) * 2 + 1) for p in ODD]
TO_ODD = [(p - 1, p) for p in ODD]
TO_EVEN = [(p, p - 1) for p in ODD]


def up(v):
    return lax.ppermute(v, "load", y_shift(1))


def down(v):
    return lax.ppermute(v, "load", y_shift(3))


def across(v):
    return lax.ppermute(v, "load", X_LO)


def among(v, pairs):
    return lax.ppermute(v, "leaf", pairs)


def shape(dims, dtype=BF):
    return jax.ShapeDtypeStruct(dims, dtype)


VMEM = pl.BlockSpec(memory_space=pltpu.VMEM)
ANY = pl.BlockSpec(memory_space=pl.ANY)


def call(kernel, outs, *args, scratch=(), flops=2**26, limit=8, size=2**20, **specs):
    return pl.pallas_call(
        kernel,
        in_specs=specs.get("in_specs", [VMEM] * len(args)),
        out_specs=specs.get("out_specs", [VMEM] * len(outs)),
        out_shape=[o if isinstance(o, jax.ShapeDtypeStruct) else shape(o) for o in outs],
        scratch_shapes=list(scratch),
        compiler_params=pltpu.CompilerParams(vmem_limit_bytes=limit * 2**20),
        cost_estimate=pl.CostEstimate(flops=flops, bytes_accessed=size, transcendentals=0),
    )(*args)


ORIGINS = [(0, 0), (0, 3), (0, 1), (1, 0), (0, 2), (1, 3), (1, 1), (1, 2)]


def origin(slot):
    load = lax.axis_index("load")
    dx, dy = ORIGINS[slot]
    return lax.rem(load // 4 + dx, 2) * 4 + lax.rem(load + dy, 4)


def leaf_place():
    position = lax.axis_index("leaf")
    return lax.rem(position, 2), lax.rem(position // 2, 4), position // 8


def pack_kernel(*refs):
    smalls, (inv, upd, out, small, sems) = refs[:4], refs[4:]
    pairs = [(inv, out.at[:, pl.ds(0, 32)]), (upd, out.at[:, pl.ds(32, 16)])]
    for n, ref in enumerate(smalls):
        for to in range(8):
            pairs.append((ref.at[0], small.at[to, pl.ds(32 * n, 32)]))
    copies = [pltpu.make_async_copy(a, b, sems.at[n]) for n, (a, b) in enumerate(pairs)]
    for copy in copies:
        copy.start()
    for copy in copies:
        copy.wait()


def small_kernel(rows, rhs, root_ref, pack):
    full = [
        jnp.concatenate([rows[d, 32 * m : 32 * m + 32, :] for d in range(8)], axis=0)
        for m in range(4)
    ]
    for m, out in ((0, root_ref), (2, pack)):
        inv, cpl = full[m], full[m + 1]
        out[0] = mm(cpl, inv).astype(BF)
        out[1] = mmt(inv, inv).astype(BF)
    pack[2] = rhs[0, :, :256]
    pack[3] = rhs[0, :, 256:]


HALF = 12


def forward_kernel(*refs):
    common, last = refs[:7], refs[7:9]
    rhs, rows, m_ref, inv, total, upd = refs[9:]
    for n in range(2):
        first = n * HALF
        for slot in range(8):
            if slot < 7:
                rows48 = common[slot][pl.ds(first, HALF)]
            else:
                rows48 = last[n][...]
            at = origin(slot)
            inv[pl.ds(first, HALF), pl.ds(pl.multiple_of(at * 32, 32), 32), :] = rows48[:, :32]
            upd[:, pl.ds(pl.multiple_of(at * 16, 16), 16), :] = rows48[:, 32:]
        flows = [mm(upd[i], inv[first + i]).astype(BF) for i in range(HALF)]
        parts = []
        for i in range(HALF):
            hot = lax.broadcasted_iota(jnp.int32, (256, 128), 0) == rows[first + i]
            m = mm(hot.astype(BF), flows[i]).astype(BF)
            m_ref[first + i] = m
            parts.append(m)
        new = mm(
            jnp.concatenate(parts, axis=1), rhs[pl.ds(first, HALF)].reshape(HALF * 256, 512)
        )
        total[...] = new if n == 0 else total[...] + new


def leaves_forward(blocks, rhs, rows):
    return call(
        forward_kernel,
        [(24, 256, 256), (24, 256, 256), shape((256, 512), F32)],
        *blocks,
        rhs,
        rows,
        scratch=[
            pltpu.VMEM((HALF, 128, 256), BF),
        ],
        flops=2**32,
        size=2**24,
        limit=16,
    )


def prepare_kernel(first, inv, m, rhs, base, mt):
    count = base.shape[0]
    squares = [mmt(inv[first + i], inv[first + i]).astype(BF) for i in range(count)]
    for i in range(count):
        mt[i] = -(m[first + i].T)
    for i in range(count):
        base[i] = mm(squares[i], rhs[first + i]).astype(BF)


def prepare(first, count, inv, m, rhs):
    return call(
        functools.partial(prepare_kernel, first),
        [(count, 256, 512), (count, 256, 256)],
        inv,
        m,
        rhs,
        flops=count * 2**27,
    )


def root_kernel(rhs, total, mats, r_ref, flow):
    r = sub(rhs[0], total[...])
    r_ref[...] = r
    flow[...] = mm(mats[0], r).astype(BF)


def halves(pack):
    return jnp.concatenate([pack[2], pack[3]], axis=1)


def first_kernel(pack, mine, theirs, r_ref, flow, mats):
    r = sub(halves(pack), f32sum(mine[...], theirs[...]))
    r_ref[...] = r
    flow[...] = mm(pack[0], r).astype(BF)
    mats[0] = pack[0].T
    mats[1] = pack[1]


def middle_kernel(*refs):
    packs, flows, (r_ref, flow, mats) = refs[:4], refs[4:8], refs[8:]
    z = leaf_place()[1]
    for k in range(4):

        @pl.when(z == k)
        def _():
            p = [packs[(k - j) % 4] for j in range(4)]
            f = [flows[(k - j) % 4] for j in range(4)]
            r = [None] * 3
            out = [None] * 3
            for j in (0, 2):
                r[j] = sub(halves(p[j]), f32sum(f[j][...], f[j + 1][...]))
                out[j] = mm(p[j][0], r[j]).astype(BF)
            r[1] = sub(halves(p[1]), f32sum(out[0], out[2]))
            flow[...] = mm(p[1][0], r[1]).astype(BF)
            for n, j in enumerate((k // 2 * 2, 1)):
                r_ref[n] = r[j]
                mats[n, 0] = p[j][0].T
                mats[n, 1] = p[j][1]


def choose_kernel(own, s1, s2, s3, out):
    z = leaf_place()[1]
    for k, ref in enumerate((s1, s2, s3, own)):

        @pl.when(z == k)
        def _():
            out[...] = ref[...]


def top_kernel(mine, theirs, top, far, t0, t, r0, r, above, even, odd, p3, p4):
    _, z, x_hi = leaf_place()

    @pl.when(x_hi == 0)
    def _():
        p3[...] = top[...]
        p4[...] = far[...]

    @pl.when(x_hi == 1)
    def _():
        p3[...] = far[...]
        p4[...] = top[...]

    r3 = sub(halves(p3), f32sum(mine[...], theirs[...]))
    r4 = sub(halves(p4), mm(p3[0], r3).astype(BF).astype(F32))
    x4 = (mm(p4[1], r4) - mmt(p4[0], above[...])).astype(BF)
    x3 = (mm(p3[1], r3) - mmt(p3[0], x4)).astype(BF)
    x2 = (mm(t[1, 1], r[1]) - mm(t[1, 0], x3)).astype(BF)
    x1 = (mm(t[0, 1], r[0]) - mm(t[0, 0], x2)).astype(BF)
    even[...] = (mm(t0[1], r0[...]) - mm(t0[0], x1)).astype(BF)

    @pl.when(z % 2 == 0)
    def _():
        odd[...] = x1

    @pl.when(z == 1)
    def _():
        odd[...] = x2

    @pl.when(z == 3)
    def _():
        odd[...] = jnp.where(x_hi == 0, x3, x4)


PIECE = 2


def backward_kernel(parts, r, mats, even, odd, got, *refs):
    bases, mts = refs[:parts], refs[parts : 2 * parts]
    leaf_out, root_out, sep_out, small, held, sems, small_sems = refs[2 * parts :]
    core = leaf_place()[0]
    parent = jnp.where(core == 0, got[...], even[...])
    small[0] = (mm(mats[1], r[...]) - mmt(mats[0], parent)).astype(BF)
    small[1] = jnp.where(core == 0, got[...], odd[...])
    copies = [
        pltpu.make_async_copy(small.at[n], ref.at[0], small_sems.at[n])
        for n, ref in enumerate((root_out, sep_out))
    ]
    for copy in copies:
        copy.start()
    count = 24 // PIECE
    for step in range(count):
        part, at = divmod(step, count // parts)
        here = pl.ds(at * PIECE, PIECE)
        moved = mm(mts[part][here].reshape(PIECE * 256, 256), small[0])
        held[step] = (bases[part][here].astype(F32) + moved.reshape(PIECE, 256, 512)).astype(BF)
        copy = pltpu.make_async_copy(
            held.at[step], leaf_out.at[pl.ds(step * PIECE, PIECE)], sems.at[step]
        )
        copy.start()
        copies.append(copy)
    for copy in copies:
        copy.wait()


def backward(r, mats, even, odd, got, bases, mts):
    return call(
        functools.partial(backward_kernel, len(bases)),
        [(24, 256, 512), (1, 256, 512), (1, 256, 512)],
        r,
        mats,
        even,
        odd,
        got,
        *bases,
        *mts,
        scratch=[
            pltpu.VMEM((2, 256, 512), BF),
            pltpu.VMEM((24 // PIECE, PIECE, 256, 512), BF),
            pltpu.SemaphoreType.DMA((24 // PIECE,)),
            pltpu.SemaphoreType.DMA((2,)),
        ],
        out_specs=[ANY] * 3,
        flops=2**31,
        size=2**24,
        limit=14,
    )


def local(
    rhs_leaves,
    rhs_roots,
    rhs_seps,
    above_solution,
    leaf_inverse,
    leaf_update,
    leaf_rows,
    root_inverse,
    root_coupling,
    sep_inverse,
    sep_coupling,
):
    w, small = call(
        pack_kernel,
        [(24, 48, 256), (8, 128, 256)],
        root_inverse,
        root_coupling,
        sep_inverse,
        sep_coupling,
        leaf_inverse,
        leaf_update,
        scratch=[pltpu.SemaphoreType.DMA((34,))],
        limit=56,
        in_specs=[ANY] * 6,
    )
    small = lax.all_to_all(small, "load", 0, 0)
    a, b, c, small = lax.optimization_barrier((up(w), down(w), across(w), small))
    d, e, f = lax.optimization_barrier((up(a), across(a), down(c)))
    blocks = (w, a, b, c, d, e, f)
    root_mats, pack = call(small_kernel, [(2, 256, 256), (4, 256, 256)], small, rhs_seps)

    over_z = lambda v: [among(v, z_shift(k, range(4))) for k in (1, 2, 3)]
    packs = over_z(pack)
    g, h = up(e[:HALF]), down(f[HALF:])
    (top,) = call(choose_kernel, [(4, 256, 256)], pack, *packs)
    far = among(top, X_HI)
    g, h, even_pack = lax.optimization_barrier((g, h, among(pack, TO_ODD)))

    m, inv, total = leaves_forward(
        (*blocks, g, h), rhs_leaves, leaf_rows.reshape(24, 1, 128)
    )

    r_root, flow = call(root_kernel, [(256, 512)] * 2, rhs_roots, total, root_mats)
    theirs, far = lax.optimization_barrier((among(flow, TO_ODD), far))
    r0, flow, t0 = call(
        first_kernel,
        [(256, 512), (256, 512), (2, 256, 256)],
        even_pack,
        flow,
        theirs,
    )
    flows = over_z(flow)
    held, flow = lax.optimization_barrier((inv, flow))
    parts = [prepare(8 * n, 8, held, m, rhs_leaves) for n in range(2)]
    flows, parts = lax.optimization_barrier((flows, parts))
    r, flow, t = call(
        middle_kernel,
        [(2, 256, 512), (256, 512), (2, 2, 256, 256)],
        pack,
        *packs,
        flow,
        *flows,
    )
    theirs = among(flow, X_HI)
    held, flow = lax.optimization_barrier((held, flow))
    parts.append(prepare(16, 8, held, m, rhs_leaves))
    theirs, parts = lax.optimization_barrier((theirs, parts))
    even, odd = call(
        top_kernel,
        [(256, 512)] * 2,
        flow,
        theirs,
        top,
        far,
        t0,
        t,
        r0,
        r,
        above_solution,
        scratch=[pltpu.VMEM((4, 256, 256), BF)] * 2,
    )
    return tuple(
        backward(
            r_root,
            root_mats,
            even,
            odd,
            among(even, TO_EVEN),
            [p[0] for p in parts],
            [p[1] for p in parts],
        )
    )


def solution(mesh):
    rows = P("leaf", "load", None)
    columns = P("leaf", None, "load")
    in_specs = (columns, columns, columns, P(None, "load"), rows, rows, P("leaf", None)) + (rows,) * 4
    return jax.shard_map(
        local, mesh=mesh, in_specs=in_specs, out_specs=(columns,) * 3, check_vma=False
    )
```

time: 320 us -> 101 us (0.32)
  the two profiles are of different devices: /device:TPU:4 before, /device:TPU:1 now
where the time goes in v2:
time: 101 us
  starting transfers between devices  43.3 us (43%)
  blocking collectives  19.9 us (20%)
  waiting for transfers between devices  17.7 us (18%)
  Pallas kernels  15.8 us (16%)
  local copies, waits for them, and re-layouts  2.77 us (3%)
  between operations  1.08 us (1%)
    ppermute x11, starting transfers between devices, among(): return lax.ppermute(v, 'leaf', pairs)  33.6 us
    all_to_all x1, blocking collectives, local(): small = lax.all_to_all(small, 'load', 0, 0)  19.9 us
    ppermute x11, waiting for transfers between devices, among(): return lax.ppermute(v, 'leaf', pairs)  16.1 us
    pallas_call x12, Pallas kernels, call(): pl.pallas_call(kernel, in_specs=specs.get('in_specs', [VMEM] * len(args))...  15.8 us
    ppermute x3, starting transfers between devices, down(): return lax.ppermute(v, 'load', y_shift(3))  7.08 us
    unnamed x12, local copies, waits for them, and re-layouts  2.73 us
    ppermute x2, starting transfers between devices, across(): return lax.ppermute(v, 'load', X_LO)  2.22 us
  transfers between devices with their start and end apart: 19, of which 8 were waited for; matrix products, arithmetic and copies ran while one was open for 0% of the time, Pallas kernels for 7%

profile of v2, /device:TPU:1, one launch (start us, length us, event | category | flops | bytes accessed | tf_op | source)
XLA Modules:
  0.0 100.6 jit_solution(9580386427884114362)
XLA Ops:
  0.6 0.0 copy-start
  0.6 2.7 %shard_map.130 = (bf16[24,48,256]{2,1,0:T(8,128)(2,1)}, bf16[8,128,256]{2,1,0:T(8,128)(2,1)}) custom-call(bf16[1,32,256]{2,1,0:T(8,128)(2,1)} %refs_0_.1, bf16[1,32,256]{2,1,0:T(8,128)(2,1)} %refs_1_.1, bf16[1,32,256]{2,1,0:T(8,128)(2,1)} %refs_2_.1, bf16[1,32,256]{2,1,0:T(8,128)(2,1)} %refs_3_.1, bf16[24,32,256]{2,1,0:T(8,128)(2,1)} %refs_4_.1, ...), custom_call_target="tpu_custom_call" | custom-call | flops 67108864 | bytes 1048576 | tf_op jit(solution)/shard_map/pallas_call | solution.py:73
  3.4 2.1 %collective-permute-start.2 = (bf16[24,48,256]{2,1,0:T(8,128)(2,1)}, bf16[24,48,256]{2,1,0:T(8,128)(2,1)S(1)}, u32[]{:S(2)}, u32[]{:S(2)}) collective-permute-start(bf16[24,48,256]{2,1,0:T(8,128)(2,1)} %get-tuple-element.56.refs_0_), channel_id=1, source_target_pairs={{0,4},{1,5},{2,6},{3,7},{4,0},{5,1},{6,2},{7,3},{8,12},{9,13},{10,... | collective-permute-start | bytes 1769480 | tf_op jit(solution)/shard_map/ppermute | solution.py:57
  5.5 2.7 %collective-permute-start.1 = (bf16[24,48,256]{2,1,0:T(8,128)(2,1)}, bf16[24,48,256]{2,1,0:T(8,128)(2,1)S(1)}, u32[]{:S(2)}, u32[]{:S(2)}) collective-permute-start(bf16[24,48,256]{2,1,0:T(8,128)(2,1)} %get-tuple-element.56.refs_0_), channel_id=1, source_target_pairs={{0,3},{1,0},{2,1},{3,2},{4,7},{5,4},{6,5},{7,6},{8,11},{9,8},{10,9... | collective-permute-start | bytes 1769480 | tf_op jit(solution)/shard_map/ppermute | solution.py:53
  8.2 0.0 collective-permute-start
  8.2 19.9 %all_to_all.5.rows = bf16[8,128,256]{2,1,0:T(8,128)(2,1)S(1)} all-to-all(bf16[8,128,256]{2,1,0:T(8,128)(2,1)} %get-tuple-element.57), channel_id=1, replica_groups=mesh['leaf'=16,'load'=8] {'load'}, dimensions={0} | all-to-all | bytes 1048576 | tf_op jit(solution)/shard_map/all_to_all | solution.py:353
  28.1 0.0 collective-permute-done.2.refs_3_
  28.1 0.0 collective-permute-done.1.refs_2_
  28.1 0.0 collective-permute-done.refs_1_
  28.2 1.1 %collective-permute-start.5 = (bf16[24,48,256]{2,1,0:T(8,128)(2,1)S(1)}, bf16[24,48,256]{2,1,0:T(8,128)(2,1)S(1)}, u32[]{:S(2)}, u32[]{:S(2)}) collective-permute-start(bf16[24,48,256]{2,1,0:T(8,128)(2,1)S(1)} %collective-permute-done.2.refs_3_), channel_id=1, source_target_pairs={{0,3},{1,0},{2,1},{3,2},{4,7},{5,4},{6,5},{7,6},{8,11},{9,8},{10,9... | collective-permute-start | bytes 1769480 | tf_op jit(solution)/shard_map/ppermute | solution.py:53
  29.2 0.1 collective-permute-start.4
  29.3 0.4 collective-permute-start.3
  29.7 0.0 copy-start.1
  29.7 0.9 copy-done.1
  30.6 0.3 shard_map.131
  31.0 5.7 %collective-permute-start.12 = (bf16[4,256,256]{2,1,0:T(8,128)(2,1)S(1)}, bf16[4,256,256]{2,1,0:T(8,128)(2,1)S(1)}, u32[]{:S(2)}, u32[]{:S(2)}) collective-permute-start(bf16[4,256,256]{2,1,0:T(8,128)(2,1)S(1)} %get-tuple-element.65.own.refs_0_), channel_id=1, source_target_pairs={{8,56},{24,8},{40,24},{56,40},{72,120},{88,72},{104,88},{120,104},... | collective-permute-start | bytes 1572872 | tf_op jit(solution)/shard_map/ppermute | solution.py:61
  36.6 1.9 %collective-permute-start.11 = (bf16[4,256,256]{2,1,0:T(8,128)(2,1)S(1)}, bf16[4,256,256]{2,1,0:T(8,128)(2,1)S(1)}, u32[]{:S(2)}, u32[]{:S(2)}) collective-permute-start(bf16[4,256,256]{2,1,0:T(8,128)(2,1)S(1)} %get-tuple-element.65.own.refs_0_), channel_id=1, source_target_pairs={{8,40},{24,56},{40,8},{56,24},{72,104},{88,120},{104,72},{120,88},... | collective-permute-start | bytes 1572872 | tf_op jit(solution)/shard_map/ppermute | solution.py:61
  38.6 1.6 %collective-permute-done.5.refs_6_ = bf16[24,48,256]{2,1,0:T(8,128)(2,1)S(1)} collective-permute-done((bf16[24,48,256]{2,1,0:T(8,128)(2,1)S(1)}, bf16[24,48,256]{2,1,0:T(8,128)(2,1)S(1)}, u32[]{:S(2)}, u32[]{:S(2)}) %collective-permute-start.5) | collective-permute-done | bytes 589856 | tf_op jit(solution)/shard_map/ppermute | solution.py:53
  40.2 3.5 %collective-permute-start.10 = (bf16[4,256,256]{2,1,0:T(8,128)(2,1)S(1)}, bf16[4,256,256]{2,1,0:T(8,128)(2,1)S(1)}, u32[]{:S(2)}, u32[]{:S(2)}) collective-permute-start(bf16[4,256,256]{2,1,0:T(8,128)(2,1)S(1)} %get-tuple-element.65.own.refs_0_), channel_id=1, source_target_pairs={{8,24},{24,40},{40,56},{56,8},{72,88},{88,104},{104,120},{120,72},... | collective-permute-start | bytes 1572872 | tf_op jit(solution)/shard_map/ppermute | solution.py:61
  43.7 0.0 collective-permute-done.4.refs_5_
  43.7 1.3 %collective-permute-start.8 = (bf16[4,256,256]{2,1,0:T(8,128)(2,1)S(1)}, bf16[4,256,256]{2,1,0:T(8,128)(2,1)S(1)}, u32[]{:S(2)}, u32[]{:S(2)}) collective-permute-start(bf16[4,256,256]{2,1,0:T(8,128)(2,1)S(1)} %get-tuple-element.65.own.refs_0_), channel_id=1, source_target_pairs={{0,8},{16,24},{32,40},{48,56},{64,72},{80,88},{96,104},{112,120},{... | collective-permute-start | bytes 1572872 | tf_op jit(solution)/shard_map/ppermute | solution.py:61
  45.0 0.0 collective-permute-done.3.refs_4_
  45.1 3.3 %collective-permute-start.7 = (bf16[12,48,256]{2,1,0:T(8,128)(2,1)S(1)}, bf16[12,48,256]{2,1,0:T(8,128)(2,1)S(1)}, u32[]{:S(2)}, u32[]{:S(2)}) collective-permute-start(bf16[12,48,256]{2,1,0:T(8,128)(2,1)S(1)} %slice.7), channel_id=1, source_target_pairs={{0,3},{1,0},{2,1},{3,2},{4,7},{5,4},{6,5},{7,6},{8,11},{9,8},{10,9... | collective-permute-start | bytes 884744 | tf_op jit(solution)/shard_map/ppermute | solution.py:53
  48.4 0.0 collective-permute-done.12.s3.refs_3_
  48.4 0.0 collective-permute-start.6
  48.4 0.0 collective-permute-done.11.s2.refs_2_
  48.4 5.2 %collective-permute-done.10.s1.refs_1_ = bf16[4,256,256]{2,1,0:T(8,128)(2,1)S(1)} collective-permute-done((bf16[4,256,256]{2,1,0:T(8,128)(2,1)S(1)}, bf16[4,256,256]{2,1,0:T(8,128)(2,1)S(1)}, u32[]{:S(2)}, u32[]{:S(2)}) %collective-permute-start.10) | collective-permute-done | bytes 524320 | tf_op jit(solution)/shard_map/ppermute | solution.py:61
  53.7 4.4 %collective-permute-start.13 = (bf16[4,256,256]{2,1,0:T(8,128)(2,1)S(1)}, bf16[4,256,256]{2,1,0:T(8,128)(2,1)S(1)}, u32[]{:S(2)}, u32[]{:S(2)}) collective-permute-start(bf16[4,256,256]{2,1,0:T(8,128)(2,1)S(1)} %shard_map.134.top), channel_id=1, source_target_pairs={{8,72},{24,88},{40,104},{56,120},{72,8},{88,24},{104,40},{120,56},... | collective-permute-start | bytes 1572872 | tf_op jit(solution)/shard_map/ppermute | solution.py:61
  58.2 0.0 collective-permute-done.8.pack
  58.2 0.0 collective-permute-done.7.refs_8_
  58.2 0.0 collective-permute-done.6.refs_7_
  58.2 0.0 copy-done
  58.2 0.0 copy-start.4
  58.2 1.1 %copy-done.4 = bf16[24,48,256]{2,1,0:T(8,128)(2,1)S(1)} copy-done((bf16[24,48,256]{2,1,0:T(8,128)(2,1)S(1)}, bf16[24,48,256]{2,1,0:T(8,128)(2,1)}, u32[]{:S(2)}) %copy-start.4) | copy-done | bytes 589848
  59.3 0.0 copy-start.5
  59.3 0.7 copy-done.5
  60.0 0.0 copy-start.2
  60.0 3.3 %shard_map.132 = (bf16[24,256,256]{2,1,0:T(8,128)(2,1)S(1)}, bf16[24,256,256]{2,1,0:T(8,128)(2,1)S(1)}, f32[256,512]{1,0:T(8,128)S(1)}) custom-call(bf16[24,48,256]{2,1,0:T(8,128)(2,1)S(1)} %copy-done.4, bf16[24,48,256]{2,1,0:T(8,128)(2,1)S(1)} %collective-permute-done.refs_1_, bf16[24,48,256]{2,1,0:T(8,128)(2,1)S(1)} %collective-permute-done.1.refs_2_, ...), custom_call_target="tpu_custom_call" | custom-call | flops 4294967296 | bytes 16777216 | tf_op jit(solution)/shard_map/pallas_call | solution.py:73
  63.3 0.0 copy-done.2
  63.3 0.2 shard_map.133
  63.5 1.3 %collective-permute-start.9 = (bf16[256,512]{1,0:T(8,128)(2,1)S(1)}, bf16[256,512]{1,0:T(8,128)(2,1)S(1)}, u32[]{:S(2)}, u32[]{:S(2)}) collective-permute-start(bf16[256,512]{1,0:T(8,128)(2,1)S(1)} %get-tuple-element.73.mine), channel_id=1, source_target_pairs={{0,8},{16,24},{32,40},{48,56},{64,72},{80,88},{96,104},{112,120},{... | collective-permute-start | bytes 786440 | tf_op jit(solution)/shard_map/ppermute | solution.py:61
  64.8 0.3 collective-permute-done.13.far
  65.2 1.8 %collective-permute-done.9.theirs = bf16[256,512]{1,0:T(8,128)(2,1)S(1)} collective-permute-done((bf16[256,512]{1,0:T(8,128)(2,1)S(1)}, bf16[256,512]{1,0:T(8,128)(2,1)S(1)}, u32[]{:S(2)}, u32[]{:S(2)}) %collective-permute-start.9) | collective-permute-done | bytes 262176 | tf_op jit(solution)/shard_map/ppermute | solution.py:61
  67.0 0.3 shard_map.135
  67.3 4.7 %collective-permute-start.16 = (bf16[256,512]{1,0:T(8,128)(2,1)S(1)}, bf16[256,512]{1,0:T(8,128)(2,1)S(1)}, u32[]{:S(2)}, u32[]{:S(2)}) collective-permute-start(bf16[256,512]{1,0:T(8,128)(2,1)S(1)} %get-tuple-element.77.refs_4_), channel_id=1, source_target_pairs={{8,56},{24,8},{40,24},{56,40},{72,120},{88,72},{104,88},{120,104},... | collective-permute-start | bytes 786440 | tf_op jit(solution)/shard_map/ppermute | solution.py:61
  71.9 2.3 %collective-permute-start.15 = (bf16[256,512]{1,0:T(8,128)(2,1)S(1)}, bf16[256,512]{1,0:T(8,128)(2,1)S(1)}, u32[]{:S(2)}, u32[]{:S(2)}) collective-permute-start(bf16[256,512]{1,0:T(8,128)(2,1)S(1)} %get-tuple-element.77.refs_4_), channel_id=1, source_target_pairs={{8,40},{24,56},{40,8},{56,24},{72,104},{88,120},{104,72},{120,88},... | collective-permute-start | bytes 786440 | tf_op jit(solution)/shard_map/ppermute | solution.py:61
  74.2 2.6 %collective-permute-start.14 = (bf16[256,512]{1,0:T(8,128)(2,1)S(1)}, bf16[256,512]{1,0:T(8,128)(2,1)S(1)}, u32[]{:S(2)}, u32[]{:S(2)}) collective-permute-start(bf16[256,512]{1,0:T(8,128)(2,1)S(1)} %get-tuple-element.77.refs_4_), channel_id=1, source_target_pairs={{8,24},{24,40},{40,56},{56,8},{72,88},{88,104},{104,120},{120,72},... | collective-permute-start | bytes 786440 | tf_op jit(solution)/shard_map/ppermute | solution.py:61
  76.8 1.0 %shard_map.137 = (bf16[8,256,512]{2,1,0:T(8,128)(2,1)S(1)}, bf16[8,256,256]{2,1,0:T(8,128)(2,1)S(1)}) custom-call(bf16[24,256,256]{2,1,0:T(8,128)(2,1)S(1)} %get-tuple-element.92.inv, bf16[24,256,256]{2,1,0:T(8,128)(2,1)S(1)} %get-tuple-element.78.m, bf16[24,256,512]{2,1,0:T(8,128)(2,1)S(1)} %copy-done), custom_call_target="tpu_custom_call" | custom-call | flops 1073741824 | bytes 1048576 | tf_op jit(solution)/shard_map/pallas_call | solution.py:73
  77.9 1.0 %shard_map.136 = (bf16[8,256,512]{2,1,0:T(8,128)(2,1)S(1)}, bf16[8,256,256]{2,1,0:T(8,128)(2,1)S(1)}) custom-call(bf16[24,256,256]{2,1,0:T(8,128)(2,1)S(1)} %get-tuple-element.92.inv, bf16[24,256,256]{2,1,0:T(8,128)(2,1)S(1)} %get-tuple-element.78.m, bf16[24,256,512]{2,1,0:T(8,128)(2,1)S(1)} %copy-done), custom_call_target="tpu_custom_call" | custom-call | flops 1073741824 | bytes 1048576 | tf_op jit(solution)/shard_map/pallas_call | solution.py:73
  78.9 0.0 collective-permute-done.16.refs_7_
  78.9 1.7 %collective-permute-done.15.refs_6_ = bf16[256,512]{1,0:T(8,128)(2,1)S(1)} collective-permute-done((bf16[256,512]{1,0:T(8,128)(2,1)S(1)}, bf16[256,512]{1,0:T(8,128)(2,1)S(1)}, u32[]{:S(2)}, u32[]{:S(2)}) %collective-permute-start.15) | collective-permute-done | bytes 262176 | tf_op jit(solution)/shard_map/ppermute | solution.py:61
  80.6 2.7 %collective-permute-done.14.refs_5_ = bf16[256,512]{1,0:T(8,128)(2,1)S(1)} collective-permute-done((bf16[256,512]{1,0:T(8,128)(2,1)S(1)}, bf16[256,512]{1,0:T(8,128)(2,1)S(1)}, u32[]{:S(2)}, u32[]{:S(2)}) %collective-permute-start.14) | collective-permute-done | bytes 262176 | tf_op jit(solution)/shard_map/ppermute | solution.py:61
  83.4 0.8 shard_map.138
  84.2 0.0 copy-start.3
  84.2 4.6 %collective-permute-start.17 = (bf16[256,512]{1,0:T(8,128)(2,1)S(1)}, bf16[256,512]{1,0:T(8,128)(2,1)S(1)}, u32[]{:S(2)}, u32[]{:S(2)}) collective-permute-start(bf16[256,512]{1,0:T(8,128)(2,1)S(1)} %get-tuple-element.87.mine), channel_id=1, source_target_pairs={{8,72},{24,88},{40,104},{56,120},{72,8},{88,24},{104,40},{120,56},... | collective-permute-start | bytes 786440 | tf_op jit(solution)/shard_map/ppermute | solution.py:61
  88.8 1.0 %shard_map.139 = (bf16[8,256,512]{2,1,0:T(8,128)(2,1)S(1)}, bf16[8,256,256]{2,1,0:T(8,128)(2,1)S(1)}) custom-call(bf16[24,256,256]{2,1,0:T(8,128)(2,1)S(1)} %get-tuple-element.92.inv, bf16[24,256,256]{2,1,0:T(8,128)(2,1)S(1)} %get-tuple-element.78.m, bf16[24,256,512]{2,1,0:T(8,128)(2,1)S(1)} %copy-done), custom_call_target="tpu_custom_call" | custom-call | flops 1073741824 | bytes 1048576 | tf_op jit(solution)/shard_map/pallas_call | solution.py:73
  89.9 3.1 %collective-permute-done.17.theirs = bf16[256,512]{1,0:T(8,128)(2,1)S(1)} collective-permute-done((bf16[256,512]{1,0:T(8,128)(2,1)S(1)}, bf16[256,512]{1,0:T(8,128)(2,1)S(1)}, u32[]{:S(2)}, u32[]{:S(2)}) %collective-permute-start.17) | collective-permute-done | bytes 262176 | tf_op jit(solution)/shard_map/ppermute | solution.py:61
  93.0 0.0 copy-done.3
  93.0 1.5 %shard_map.140 = (bf16[256,512]{1,0:T(8,128)(2,1)S(1)}, bf16[256,512]{1,0:T(8,128)(2,1)S(1)}) custom-call(bf16[256,512]{1,0:T(8,128)(2,1)S(1)} %get-tuple-element.87.mine, bf16[256,512]{1,0:T(8,128)(2,1)S(1)} %collective-permute-done.17.theirs, bf16[4,256,256]{2,1,0:T(8,128)(2,1)S(1)} %shard_map.134.top, ...), custom_call_target="tpu_custom_call" | custom-call | flops 67108864 | bytes 1048576 | tf_op jit(solution)/shard_map/pallas_call | solution.py:73
  94.5 1.3 %collective-permute-start.18 = (bf16[256,512]{1,0:T(8,128)(2,1)S(1)}, bf16[256,512]{1,0:T(8,128)(2,1)S(1)}, u32[]{:S(2)}, u32[]{:S(2)}) collective-permute-start(bf16[256,512]{1,0:T(8,128)(2,1)S(1)} %get-tuple-element.101.even), channel_id=1, source_target_pairs={{8,0},{24,16},{40,32},{56,48},{72,64},{88,80},{104,96},{120,112},{... | collective-permute-start | bytes 786440 | tf_op jit(solution)/shard_map/ppermute | solution.py:61
  95.8 1.1 %collective-permute-done.18.got = bf16[256,512]{1,0:T(8,128)(2,1)S(1)} collective-permute-done((bf16[256,512]{1,0:T(8,128)(2,1)S(1)}, bf16[256,512]{1,0:T(8,128)(2,1)S(1)}, u32[]{:S(2)}, u32[]{:S(2)}) %collective-permute-start.18) | collective-permute-done | bytes 262176 | tf_op jit(solution)/shard_map/ppermute | solution.py:61
  96.9 3.5 %shard_map.141 = (bf16[24,256,512]{2,1,0:T(8,128)(2,1)}, bf16[1,256,512]{2,1,0:T(8,128)(2,1)}, bf16[1,256,512]{2,1,0:T(8,128)(2,1)}) custom-call(bf16[256,512]{1,0:T(8,128)(2,1)S(1)} %get-tuple-element.70.r, bf16[2,256,256]{2,1,0:T(8,128)(2,1)S(1)} %get-tuple-element.69.mats, bf16[256,512]{1,0:T(8,128)(2,1)S(1)} %get-tuple-element.101.even, ...), custom_call_target="tpu_custom_call" | custom-call | flops 2147483648 | bytes 16777216 | tf_op jit(solution)/shard_map/pallas_call | solution.py:73
  (3 shorter events, 0.1 us)
Async XLA Ops:
  0.6 57.6 %copy-start = (bf16[24,256,512]{2,1,0:T(8,128)(2,1)S(1)}, bf16[24,256,512]{2,1,0:T(8,128)(2,1)}, u32[]{:S(2)}) copy-start(bf16[24,256,512]{2,1,0:T(8,128)(2,1)} %rhs.9) | copy-start | bytes 18874372
  3.4 24.8 %collective-permute-start.2 = (bf16[24,48,256]{2,1,0:T(8,128)(2,1)}, bf16[24,48,256]{2,1,0:T(8,128)(2,1)S(1)}, u32[]{:S(2)}, u32[]{:S(2)}) collective-permute-start(bf16[24,48,256]{2,1,0:T(8,128)(2,1)} %get-tuple-element.56.refs_0_), channel_id=1, source_target_pairs={{0,4},{1,5},{2,6},{3,7},{4,0},{5,1},{6,2},{7,3},{8,12},{9,13},{10,... | collective-permute-start | bytes 1769480 | tf_op jit(solution)/shard_map/ppermute | solution.py:57
  5.5 22.7 %collective-permute-start.1 = (bf16[24,48,256]{2,1,0:T(8,128)(2,1)}, bf16[24,48,256]{2,1,0:T(8,128)(2,1)S(1)}, u32[]{:S(2)}, u32[]{:S(2)}) collective-permute-start(bf16[24,48,256]{2,1,0:T(8,128)(2,1)} %get-tuple-element.56.refs_0_), channel_id=1, source_target_pairs={{0,3},{1,0},{2,1},{3,2},{4,7},{5,4},{6,5},{7,6},{8,11},{9,8},{10,9... | collective-permute-start | bytes 1769480 | tf_op jit(solution)/shard_map/ppermute | solution.py:53
  8.2 19.9 %collective-permute-start = (bf16[24,48,256]{2,1,0:T(8,128)(2,1)}, bf16[24,48,256]{2,1,0:T(8,128)(2,1)S(1)}, u32[]{:S(2)}, u32[]{:S(2)}) collective-permute-start(bf16[24,48,256]{2,1,0:T(8,128)(2,1)} %get-tuple-element.56.refs_0_), channel_id=1, source_target_pairs={{0,1},{1,2},{2,3},{3,0},{4,5},{5,6},{6,7},{7,4},{8,9},{9,10},{10,1... | collective-permute-start | bytes 1769480 | tf_op jit(solution)/shard_map/ppermute | solution.py:49
  28.2 12.0 %collective-permute-start.5 = (bf16[24,48,256]{2,1,0:T(8,128)(2,1)S(1)}, bf16[24,48,256]{2,1,0:T(8,128)(2,1)S(1)}, u32[]{:S(2)}, u32[]{:S(2)}) collective-permute-start(bf16[24,48,256]{2,1,0:T(8,128)(2,1)S(1)} %collective-permute-done.2.refs_3_), channel_id=1, source_target_pairs={{0,3},{1,0},{2,1},{3,2},{4,7},{5,4},{6,5},{7,6},{8,11},{9,8},{10,9... | collective-permute-start | bytes 1769480 | tf_op jit(solution)/shard_map/ppermute | solution.py:53
  29.2 14.5 %collective-permute-start.4 = (bf16[24,48,256]{2,1,0:T(8,128)(2,1)S(1)}, bf16[24,48,256]{2,1,0:T(8,128)(2,1)S(1)}, u32[]{:S(2)}, u32[]{:S(2)}) collective-permute-start(bf16[24,48,256]{2,1,0:T(8,128)(2,1)S(1)} %collective-permute-done.refs_1_), channel_id=1, source_target_pairs={{0,4},{1,5},{2,6},{3,7},{4,0},{5,1},{6,2},{7,3},{8,12},{9,13},{10,... | collective-permute-start | bytes 1769480 | tf_op jit(solution)/shard_map/ppermute | solution.py:57
  29.3 15.7 %collective-permute-start.3 = (bf16[24,48,256]{2,1,0:T(8,128)(2,1)S(1)}, bf16[24,48,256]{2,1,0:T(8,128)(2,1)S(1)}, u32[]{:S(2)}, u32[]{:S(2)}) collective-permute-start(bf16[24,48,256]{2,1,0:T(8,128)(2,1)S(1)} %collective-permute-done.refs_1_), channel_id=1, source_target_pairs={{0,1},{1,2},{2,3},{3,0},{4,5},{5,6},{6,7},{7,4},{8,9},{9,10},{10,1... | collective-permute-start | bytes 1769480 | tf_op jit(solution)/shard_map/ppermute | solution.py:49
  29.7 0.9 copy-start.1
  31.0 17.4 %collective-permute-start.12 = (bf16[4,256,256]{2,1,0:T(8,128)(2,1)S(1)}, bf16[4,256,256]{2,1,0:T(8,128)(2,1)S(1)}, u32[]{:S(2)}, u32[]{:S(2)}) collective-permute-start(bf16[4,256,256]{2,1,0:T(8,128)(2,1)S(1)} %get-tuple-element.65.own.refs_0_), channel_id=1, source_target_pairs={{8,56},{24,8},{40,24},{56,40},{72,120},{88,72},{104,88},{120,104},... | collective-permute-start | bytes 1572872 | tf_op jit(solution)/shard_map/ppermute | solution.py:61
  36.6 11.8 %collective-permute-start.11 = (bf16[4,256,256]{2,1,0:T(8,128)(2,1)S(1)}, bf16[4,256,256]{2,1,0:T(8,128)(2,1)S(1)}, u32[]{:S(2)}, u32[]{:S(2)}) collective-permute-start(bf16[4,256,256]{2,1,0:T(8,128)(2,1)S(1)} %get-tuple-element.65.own.refs_0_), channel_id=1, source_target_pairs={{8,40},{24,56},{40,8},{56,24},{72,104},{88,120},{104,72},{120,88},... | collective-permute-start | bytes 1572872 | tf_op jit(solution)/shard_map/ppermute | solution.py:61
  40.2 13.5 %collective-permute-start.10 = (bf16[4,256,256]{2,1,0:T(8,128)(2,1)S(1)}, bf16[4,256,256]{2,1,0:T(8,128)(2,1)S(1)}, u32[]{:S(2)}, u32[]{:S(2)}) collective-permute-start(bf16[4,256,256]{2,1,0:T(8,128)(2,1)S(1)} %get-tuple-element.65.own.refs_0_), channel_id=1, source_target_pairs={{8,24},{24,40},{40,56},{56,8},{72,88},{88,104},{104,120},{120,72},... | collective-permute-start | bytes 1572872 | tf_op jit(solution)/shard_map/ppermute | solution.py:61
  43.7 14.4 %collective-permute-start.8 = (bf16[4,256,256]{2,1,0:T(8,128)(2,1)S(1)}, bf16[4,256,256]{2,1,0:T(8,128)(2,1)S(1)}, u32[]{:S(2)}, u32[]{:S(2)}) collective-permute-start(bf16[4,256,256]{2,1,0:T(8,128)(2,1)S(1)} %get-tuple-element.65.own.refs_0_), channel_id=1, source_target_pairs={{0,8},{16,24},{32,40},{48,56},{64,72},{80,88},{96,104},{112,120},{... | collective-permute-start | bytes 1572872 | tf_op jit(solution)/shard_map/ppermute | solution.py:61
  45.1 13.1 %collective-permute-start.7 = (bf16[12,48,256]{2,1,0:T(8,128)(2,1)S(1)}, bf16[12,48,256]{2,1,0:T(8,128)(2,1)S(1)}, u32[]{:S(2)}, u32[]{:S(2)}) collective-permute-start(bf16[12,48,256]{2,1,0:T(8,128)(2,1)S(1)} %slice.7), channel_id=1, source_target_pairs={{0,3},{1,0},{2,1},{3,2},{4,7},{5,4},{6,5},{7,6},{8,11},{9,8},{10,9... | collective-permute-start | bytes 884744 | tf_op jit(solution)/shard_map/ppermute | solution.py:53
  48.4 9.8 %collective-permute-start.6 = (bf16[12,48,256]{2,1,0:T(8,128)(2,1)S(1)}, bf16[12,48,256]{2,1,0:T(8,128)(2,1)S(1)}, u32[]{:S(2)}, u32[]{:S(2)}) collective-permute-start(bf16[12,48,256]{2,1,0:T(8,128)(2,1)S(1)} %slice.6), channel_id=1, source_target_pairs={{0,1},{1,2},{2,3},{3,0},{4,5},{5,6},{6,7},{7,4},{8,9},{9,10},{10,1... | collective-permute-start | bytes 884744 | tf_op jit(solution)/shard_map/ppermute | solution.py:49
  53.7 11.4 %collective-permute-start.13 = (bf16[4,256,256]{2,1,0:T(8,128)(2,1)S(1)}, bf16[4,256,256]{2,1,0:T(8,128)(2,1)S(1)}, u32[]{:S(2)}, u32[]{:S(2)}) collective-permute-start(bf16[4,256,256]{2,1,0:T(8,128)(2,1)S(1)} %shard_map.134.top), channel_id=1, source_target_pairs={{8,72},{24,88},{40,104},{56,120},{72,8},{88,24},{104,40},{120,56},... | collective-permute-start | bytes 1572872 | tf_op jit(solution)/shard_map/ppermute | solution.py:61
  58.2 1.1 %copy-start.4 = (bf16[24,48,256]{2,1,0:T(8,128)(2,1)S(1)}, bf16[24,48,256]{2,1,0:T(8,128)(2,1)}, u32[]{:S(2)}) copy-start(bf16[24,48,256]{2,1,0:T(8,128)(2,1)} %get-tuple-element.56.refs_0_) | copy-start | bytes 1769476
  59.3 0.7 copy-start.5
  60.0 3.3 %copy-start.2 = (bf16[1,256,512]{2,1,0:T(8,128)(2,1)S(1)}, bf16[1,256,512]{2,1,0:T(8,128)(2,1)}, u32[]{:S(2)}) copy-start(bf16[1,256,512]{2,1,0:T(8,128)(2,1)} %rhs.6) | copy-start | bytes 786436
  63.5 3.4 %collective-permute-start.9 = (bf16[256,512]{1,0:T(8,128)(2,1)S(1)}, bf16[256,512]{1,0:T(8,128)(2,1)S(1)}, u32[]{:S(2)}, u32[]{:S(2)}) collective-permute-start(bf16[256,512]{1,0:T(8,128)(2,1)S(1)} %get-tuple-element.73.mine), channel_id=1, source_target_pairs={{0,8},{16,24},{32,40},{48,56},{64,72},{80,88},{96,104},{112,120},{... | collective-permute-start | bytes 786440 | tf_op jit(solution)/shard_map/ppermute | solution.py:61
  67.3 11.7 %collective-permute-start.16 = (bf16[256,512]{1,0:T(8,128)(2,1)S(1)}, bf16[256,512]{1,0:T(8,128)(2,1)S(1)}, u32[]{:S(2)}, u32[]{:S(2)}) collective-permute-start(bf16[256,512]{1,0:T(8,128)(2,1)S(1)} %get-tuple-element.77.refs_4_), channel_id=1, source_target_pairs={{8,56},{24,8},{40,24},{56,40},{72,120},{88,72},{104,88},{120,104},... | collective-permute-start | bytes 786440 | tf_op jit(solution)/shard_map/ppermute | solution.py:61
  71.9 8.7 %collective-permute-start.15 = (bf16[256,512]{1,0:T(8,128)(2,1)S(1)}, bf16[256,512]{1,0:T(8,128)(2,1)S(1)}, u32[]{:S(2)}, u32[]{:S(2)}) collective-permute-start(bf16[256,512]{1,0:T(8,128)(2,1)S(1)} %get-tuple-element.77.refs_4_), channel_id=1, source_target_pairs={{8,40},{24,56},{40,8},{56,24},{72,104},{88,120},{104,72},{120,88},... | collective-permute-start | bytes 786440 | tf_op jit(solution)/shard_map/ppermute | solution.py:61
  74.2 9.2 %collective-permute-start.14 = (bf16[256,512]{1,0:T(8,128)(2,1)S(1)}, bf16[256,512]{1,0:T(8,128)(2,1)S(1)}, u32[]{:S(2)}, u32[]{:S(2)}) collective-permute-start(bf16[256,512]{1,0:T(8,128)(2,1)S(1)} %get-tuple-element.77.refs_4_), channel_id=1, source_target_pairs={{8,24},{24,40},{40,56},{56,8},{72,88},{88,104},{104,120},{120,72},... | collective-permute-start | bytes 786440 | tf_op jit(solution)/shard_map/ppermute | solution.py:61
  84.2 8.8 %copy-start.3 = (bf16[256,512]{1,0:T(8,128)(2,1)S(1)}, bf16[256,512]{1,0:T(8,128)(2,1)}, u32[]{:S(2)}) copy-start(bf16[256,512]{1,0:T(8,128)(2,1)} %above.1) | copy-start | bytes 786436
  84.2 8.8 %collective-permute-start.17 = (bf16[256,512]{1,0:T(8,128)(2,1)S(1)}, bf16[256,512]{1,0:T(8,128)(2,1)S(1)}, u32[]{:S(2)}, u32[]{:S(2)}) collective-permute-start(bf16[256,512]{1,0:T(8,128)(2,1)S(1)} %get-tuple-element.87.mine), channel_id=1, source_target_pairs={{8,72},{24,88},{40,104},{56,120},{72,8},{88,24},{104,40},{120,56},... | collective-permute-start | bytes 786440 | tf_op jit(solution)/shard_map/ppermute | solution.py:61
  94.5 2.4 %collective-permute-start.18 = (bf16[256,512]{1,0:T(8,128)(2,1)S(1)}, bf16[256,512]{1,0:T(8,128)(2,1)S(1)}, u32[]{:S(2)}, u32[]{:S(2)}) collective-permute-start(bf16[256,512]{1,0:T(8,128)(2,1)S(1)} %get-tuple-element.101.even), channel_id=1, source_target_pairs={{8,0},{24,16},{40,32},{56,48},{72,64},{88,80},{104,96},{120,112},{... | collective-permute-start | bytes 786440 | tf_op jit(solution)/shard_map/ppermute | solution.py:61

commit v3 on v2

--- a/solution.py
+++ b/solution.py
@@ -10,8 +10,6 @@
 BF = jnp.bfloat16
 F32 = jnp.float32
 
-ODD = range(1, 16, 2)
-
 
 def mm(a, b):
     return jnp.dot(a, b, preferred_element_type=F32)
@@ -33,16 +31,18 @@
     return [(x * 4 + y, x * 4 + (y + s) % 4) for x in range(2) for y in range(4)]
 
 
-def z_shift(s, places):
-    return [(x * 8 + z * 2 + 1, x * 8 + ((z + s) % 4) * 2 + 1) for x in range(2) for z in places]
-
-
-X_LO = [(i, (i + 4) % 8) for i in range(8)]
-X_HI = [(p, (p + 8) % 16) for p in ODD]
-PAIR = [(p, p ^ 2) for p in ODD]
-MIRROR = [(p, (p // 8) * 8 + (3 - (p // 2) % 4) * 2 + 1) for p in ODD]
-TO_ODD = [(p - 1, p) for p in ODD]
-TO_EVEN = [(p, p - 1) for p in ODD]
+def z_shift(s):
+    return [
+        (x * 8 + z * 2 + c, x * 8 + (z + s) % 4 * 2 + c)
+        for x in range(2)
+        for z in range(4)
+        for c in range(2)
+    ]
+
+
+X_LO = [(p, (p + 4) % 8) for p in range(8)]
+X_HI = [(p, (p + 8) % 16) for p in range(16)]
+CORES = [(p, p ^ 1) for p in range(16)]
 
 
 def up(v):
@@ -108,17 +108,56 @@
         copy.wait()
 
 
-def small_kernel(rows, rhs, root_ref, pack):
+def by_core(whole, keep, send):
+    core = leaf_place()[0]
+    for c in range(2):
+
+        @pl.when(core == c)
+        def _():
+            keep[...] = whole[:, 256 * c : 256 * c + 256]
+            send[...] = whole[:, 256 - 256 * c : 512 - 256 * c]
+
+
+def small_kernel(rows, rhs, leaves, root_ref, keep, send):
+    del leaves
     full = [
         jnp.concatenate([rows[d, 32 * m : 32 * m + 32, :] for d in range(8)], axis=0)
         for m in range(4)
     ]
-    for m, out in ((0, root_ref), (2, pack)):
+    for m, outs in ((0, (root_ref,)), (2, (keep, send))):
         inv, cpl = full[m], full[m + 1]
-        out[0] = mm(cpl, inv).astype(BF)
-        out[1] = mmt(inv, inv).astype(BF)
-    pack[2] = rhs[0, :, :256]
-    pack[3] = rhs[0, :, 256:]
+        for n, value in enumerate((mm(cpl, inv).astype(BF), mmt(inv, inv).astype(BF))):
+            for out in outs:
+                out[n] = value
+    by_core(rhs[0], keep.at[2], send.at[2])
+
+
+def sides_kernel(own, got, even, odd, part):
+    core = leaf_place()[0]
+    for c, (a, b) in enumerate(((own, got), (got, own))):
+
+        @pl.when(core == c)
+        def _():
+            even[...] = a[...]
+            odd[...] = b[...]
+            part[0] = b[c]
+            part[1] = b[2]
+
+
+def joined(core, mine, theirs):
+    a = jnp.where(core == 0, mine[0], theirs[0])
+    g = jnp.where(core == 0, theirs[0], mine[0])
+    return a, g, mine[1]
+
+
+def stage_kernel(*refs):
+    n = len(refs) // 2
+    ins, outs, sems = refs[:n], refs[n:-1], refs[-1]
+    copies = [pltpu.make_async_copy(a, b, sems.at[n]) for n, (a, b) in enumerate(zip(ins, outs))]
+    for copy in copies:
+        copy.start()
+    for copy in copies:
+        copy.wait()
 
 
 HALF = 12
@@ -160,7 +199,7 @@
         scratch=[
             pltpu.VMEM((HALF, 128, 256), BF),
         ],
-        flops=2**32,
+        flops=2**20,
         size=2**24,
         limit=16,
     )
@@ -186,39 +225,38 @@
     )
 
 
-def root_kernel(rhs, total, mats, r_ref, flow):
+def root_kernel(rhs, total, mats, r_ref, keep, send):
     r = sub(rhs[0], total[...])
     r_ref[...] = r
-    flow[...] = mm(mats[0], r).astype(BF)
-
-
-def halves(pack):
-    return jnp.concatenate([pack[2], pack[3]], axis=1)
+    by_core(mm(mats[0], r).astype(BF), keep, send)
 
 
 def first_kernel(pack, mine, theirs, r_ref, flow, mats):
-    r = sub(halves(pack), f32sum(mine[...], theirs[...]))
+    r = sub(pack[2], f32sum(mine[...], theirs[...]))
     r_ref[...] = r
     flow[...] = mm(pack[0], r).astype(BF)
     mats[0] = pack[0].T
     mats[1] = pack[1]
 
 
-def middle_kernel(*refs):
-    packs, flows, (r_ref, flow, mats) = refs[:4], refs[4:8], refs[8:]
-    z = leaf_place()[1]
+def middle_kernel(odd, *refs):
+    mine, theirs, flows, (r_ref, flow, mats) = refs[:3], refs[3:6], refs[6:10], refs[10:]
+    core, z, _ = leaf_place()
     for k in range(4):
 
         @pl.when(z == k)
         def _():
-            p = [packs[(k - j) % 4] for j in range(4)]
+            p = []
+            for j in range(4):
+                n = (k - j) % 4
+                p.append(joined(core, mine[n - 1], theirs[n - 1]) if n else odd)
             f = [flows[(k - j) % 4] for j in range(4)]
             r = [None] * 3
             out = [None] * 3
             for j in (0, 2):
-                r[j] = sub(halves(p[j]), f32sum(f[j][...], f[j + 1][...]))
+                r[j] = sub(p[j][2], f32sum(f[j][...], f[j + 1][...]))
                 out[j] = mm(p[j][0], r[j]).astype(BF)
-            r[1] = sub(halves(p[1]), f32sum(out[0], out[2]))
+            r[1] = sub(p[1][2], f32sum(out[0], out[2]))
             flow[...] = mm(p[1][0], r[1]).astype(BF)
             for n, j in enumerate((k // 2 * 2, 1)):
                 r_ref[n] = r[j]
@@ -226,59 +264,68 @@
                 mats[n, 1] = p[j][1]
 
 
-def choose_kernel(own, s1, s2, s3, out):
-    z = leaf_place()[1]
-    for k, ref in enumerate((s1, s2, s3, own)):
+def choose_kernel(odd, part, *refs):
+    mine, theirs, (top, carried) = refs[:3], refs[3:6], refs[6:]
+    core, z, _ = leaf_place()
+
+    @pl.when(z == 3)
+    def _():
+        top[...] = odd[...]
+        carried[...] = part[...]
+
+    for k in range(3):
 
         @pl.when(z == k)
         def _():
-            out[...] = ref[...]
-
-
-def top_kernel(mine, theirs, top, far, t0, t, r0, r, above, even, odd, p3, p4):
-    _, z, x_hi = leaf_place()
-
-    @pl.when(x_hi == 0)
-    def _():
-        p3[...] = top[...]
-        p4[...] = far[...]
-
-    @pl.when(x_hi == 1)
-    def _():
-        p3[...] = far[...]
-        p4[...] = top[...]
-
-    r3 = sub(halves(p3), f32sum(mine[...], theirs[...]))
-    r4 = sub(halves(p4), mm(p3[0], r3).astype(BF).astype(F32))
-    x4 = (mm(p4[1], r4) - mmt(p4[0], above[...])).astype(BF)
+            for n, value in enumerate(joined(core, mine[k], theirs[k])):
+                top[n] = value
+            carried[...] = mine[k][...]
+
+
+def top_kernel(mine, theirs, top, far, far2, t0, t, r0, r, above, out, p3, p4):
+    core, z, x_hi = leaf_place()
+    above = above[:, pl.ds(pl.multiple_of(core * 256, 256), 256)]
+    for h, (a, b) in enumerate(((p3, p4), (p4, p3))):
+
+        @pl.when(x_hi == h)
+        def _():
+            a[...] = top[...]
+            for n, value in enumerate(joined(core, far, far2)):
+                b[n] = value
+
+    r3 = sub(p3[2], f32sum(mine[...], theirs[...]))
+    r4 = sub(p4[2], mm(p3[0], r3).astype(BF).astype(F32))
+    x4 = (mm(p4[1], r4) - mmt(p4[0], above)).astype(BF)
     x3 = (mm(p3[1], r3) - mmt(p3[0], x4)).astype(BF)
     x2 = (mm(t[1, 1], r[1]) - mm(t[1, 0], x3)).astype(BF)
     x1 = (mm(t[0, 1], r[0]) - mm(t[0, 0], x2)).astype(BF)
-    even[...] = (mm(t0[1], r0[...]) - mm(t0[0], x1)).astype(BF)
+    out[0] = (mm(t0[1], r0[...]) - mm(t0[0], x1)).astype(BF)
 
     @pl.when(z % 2 == 0)
     def _():
-        odd[...] = x1
+        out[1] = x1
 
     @pl.when(z == 1)
     def _():
-        odd[...] = x2
+        out[1] = x2
 
     @pl.when(z == 3)
     def _():
-        odd[...] = jnp.where(x_hi == 0, x3, x4)
+        out[1] = jnp.where(x_hi == 0, x3, x4)
 
 
 PIECE = 2
 
 
-def backward_kernel(parts, r, mats, even, odd, got, *refs):
+def backward_kernel(parts, r, mats, own, got, *refs):
     bases, mts = refs[:parts], refs[parts : 2 * parts]
     leaf_out, root_out, sep_out, small, held, sems, small_sems = refs[2 * parts :]
     core = leaf_place()[0]
-    parent = jnp.where(core == 0, got[...], even[...])
+    left = jnp.where(core == 0, own[...], got[...])
+    right = jnp.where(core == 0, got[...], own[...])
+    parent = jnp.concatenate([left[0], right[0]], axis=1)
     small[0] = (mm(mats[1], r[...]) - mmt(mats[0], parent)).astype(BF)
-    small[1] = jnp.where(core == 0, got[...], odd[...])
+    small[1] = jnp.where(core == 0, parent, jnp.concatenate([left[1], right[1]], axis=1))
     copies = [
         pltpu.make_async_copy(small.at[n], ref.at[0], small_sems.at[n])
         for n, ref in enumerate((root_out, sep_out))
@@ -300,14 +347,13 @@
         copy.wait()
 
 
-def backward(r, mats, even, odd, got, bases, mts):
+def backward(r, mats, own, got, bases, mts):
     return call(
         functools.partial(backward_kernel, len(bases)),
         [(24, 256, 512), (1, 256, 512), (1, 256, 512)],
         r,
         mats,
-        even,
-        odd,
+        own,
         got,
         *bases,
         *mts,
@@ -351,28 +397,50 @@
         in_specs=[ANY] * 6,
     )
     small = lax.all_to_all(small, "load", 0, 0)
-    a, b, c, small = lax.optimization_barrier((up(w), down(w), across(w), small))
+    arrived = up(w), down(w), across(w), small
+    staged = w, leaf_rows.reshape(24, 1, 128), rhs_seps
+    staged = call(
+        stage_kernel,
+        [shape(v.shape, v.dtype) for v in staged],
+        *staged,
+        scratch=[pltpu.SemaphoreType.DMA((len(staged),))],
+        in_specs=[ANY] * len(staged),
+    )
+    arrived, staged = lax.optimization_barrier((arrived, staged))
+    a, b, c, small = arrived
+    w, lists, rhs_seps = staged
     d, e, f = lax.optimization_barrier((up(a), across(a), down(c)))
+    g, h = up(e[:HALF]), down(f[HALF:])
     blocks = (w, a, b, c, d, e, f)
-    root_mats, pack = call(small_kernel, [(2, 256, 256), (4, 256, 256)], small, rhs_seps)
-
-    over_z = lambda v: [among(v, z_shift(k, range(4))) for k in (1, 2, 3)]
-    packs = over_z(pack)
-    g, h = up(e[:HALF]), down(f[HALF:])
-    (top,) = call(choose_kernel, [(4, 256, 256)], pack, *packs)
-    far = among(top, X_HI)
-    g, h, even_pack = lax.optimization_barrier((g, h, among(pack, TO_ODD)))
-
+    root_mats, keep, send = call(
+        small_kernel, [(2, 256, 256), (3, 256, 256), (3, 256, 256)], small, rhs_seps, rhs_leaves
+    )
+
+    over_z = lambda v: [among(v, z_shift(k)) for k in (1, 2, 3)]
+    even, odd, part = call(
+        sides_kernel,
+        [(3, 256, 256), (3, 256, 256), (2, 256, 256)],
+        keep,
+        among(send, CORES),
+    )
+    packs = over_z(part)
     m, inv, total = leaves_forward(
-        (*blocks, g, h), rhs_leaves, leaf_rows.reshape(24, 1, 128)
-    )
-
-    r_root, flow = call(root_kernel, [(256, 512)] * 2, rhs_roots, total, root_mats)
-    theirs, far = lax.optimization_barrier((among(flow, TO_ODD), far))
+        (*blocks, g, h), rhs_leaves, lists
+    )
+
+    r_root, flow, send = call(
+        root_kernel, [(256, 512), (256, 256), (256, 256)], rhs_roots, total, root_mats
+    )
+    packs2 = [among(v, CORES) for v in packs]
+    theirs, packs, packs2 = lax.optimization_barrier((among(send, CORES), packs, packs2))
+    top, carried = call(
+        choose_kernel, [(3, 256, 256), (2, 256, 256)], odd, part, *packs, *packs2
+    )
+    far = among(carried, X_HI)
     r0, flow, t0 = call(
         first_kernel,
-        [(256, 512), (256, 512), (2, 256, 256)],
-        even_pack,
+        [(256, 256), (256, 256), (2, 256, 256)],
+        even,
         flow,
         theirs,
     )
@@ -382,37 +450,40 @@
     flows, parts = lax.optimization_barrier((flows, parts))
     r, flow, t = call(
         middle_kernel,
-        [(2, 256, 512), (256, 512), (2, 2, 256, 256)],
-        pack,
+        [(2, 256, 256), (256, 256), (2, 2, 256, 256)],
+        odd,
         *packs,
+        *packs2,
         flow,
         *flows,
     )
+    far, flow = lax.optimization_barrier((far, flow))
     theirs = among(flow, X_HI)
+    far2 = among(far, CORES)
     held, flow = lax.optimization_barrier((held, flow))
     parts.append(prepare(16, 8, held, m, rhs_leaves))
     theirs, parts = lax.optimization_barrier((theirs, parts))
-    even, odd = call(
+    (own,) = call(
         top_kernel,
-        [(256, 512)] * 2,
+        [(2, 256, 256)],
         flow,
         theirs,
         top,
         far,
+        far2,
         t0,
         t,
         r0,
         r,
         above_solution,
-        scratch=[pltpu.VMEM((4, 256, 256), BF)] * 2,
+        scratch=[pltpu.VMEM((3, 256, 256), BF)] * 2,
     )
     return tuple(
         backward(
             r_root,
             root_mats,
-            even,
-            odd,
-            among(even, TO_EVEN),
+            own,
+            among(own, CORES),
             [p[0] for p in parts],
             [p[1] for p in parts],
         )

time: 101 us -> 91.3 us (0.904)
  waiting for transfers between devices: 17.7 us -> 38.5 us
  blocking collectives: 19.9 us -> 0 us
  starting transfers between devices: 43.3 us -> 30.3 us
  local copies, waits for them, and re-layouts: 2.77 us -> 5.56 us
    all_to_all x1 -> x0, blocking collectives: 19.9 us -> none  [local(): small = lax.all_to_all(small, 'load', 0, 0)]
    ppermute x11 -> x15, starting transfers between devices: 33.6 us -> 17.5 us  [among(): return lax.ppermute(v, 'leaf', pairs)]
    all_to_all x0 -> x1, waiting for transfers between devices: none -> 13.1 us  [local(): small = lax.all_to_all(small, 'load', 0, 0)]
    ppermute x11 -> x15, waiting for transfers between devices: 16.1 us -> 25.1 us  [among(): return lax.ppermute(v, 'leaf', pairs)]
    all_to_all x0 -> x1, starting transfers between devices: none -> 3.95 us  [local(): small = lax.all_to_all(small, 'load', 0, 0)]
    unnamed x12 -> x14, local copies, waits for them, and re-layouts: 2.73 us -> 5.52 us
    ppermute x3, waiting for transfers between devices: 1.63 us -> 0.01 us  [down(): return lax.ppermute(v, 'load', y_shift(3))]
    ppermute x3, starting transfers between devices: 7.08 us -> 5.82 us  [down(): return lax.ppermute(v, 'load', y_shift(3))]
  transfers between devices with their start and end apart: 19 -> 24, of which waited for: 8 -> 11; matrix products, arithmetic and copies ran while one was open for 0% -> 0% of each run, Pallas kernels for 7% -> 9%
where the time goes in v3:
time: 91.3 us; the launch traced here: 90.9 us
  waiting for transfers between devices  38.5 us (42%)
  starting transfers between devices  30.3 us (33%)
  Pallas kernels  15.6 us (17%)
  local copies, waits for them, and re-layouts  5.56 us (6%)
  between operations  1 us (1%)
    ppermute x15, waiting for transfers between devices, among(): return lax.ppermute(v, 'leaf', pairs)  25.1 us
    ppermute x15, starting transfers between devices, among(): return lax.ppermute(v, 'leaf', pairs)  17.5 us
    pallas_call x14, Pallas kernels, call(): pl.pallas_call(kernel, in_specs=specs.get('in_specs', [VMEM] * len(args))...  15.6 us
    all_to_all x1, waiting for transfers between devices, local(): small = lax.all_to_all(small, 'load', 0, 0)  13.1 us
    ppermute x3, starting transfers between devices, down(): return lax.ppermute(v, 'load', y_shift(3))  5.82 us
    unnamed x14, local copies, waits for them, and re-layouts  5.52 us
    all_to_all x1, starting transfers between devices, local(): small = lax.all_to_all(small, 'load', 0, 0)  3.95 us
    ppermute x2, starting transfers between devices, across(): return lax.ppermute(v, 'load', X_LO)  2.37 us
  transfers between devices with their start and end apart: 24, of which 11 were waited for; matrix products, arithmetic and copies ran while one was open for 0% of the time, Pallas kernels for 9%

profile of v3, /device:TPU:1, one launch (start us, length us, event | category | flops | bytes accessed | tf_op | source)
XLA Modules:
  0.0 90.9 jit_solution(4992197709682563593)
XLA Ops:
  0.6 2.7 %shard_map.130 = (bf16[24,48,256]{2,1,0:T(8,128)(2,1)}, bf16[8,128,256]{2,1,0:T(8,128)(2,1)}) custom-call(bf16[1,32,256]{2,1,0:T(8,128)(2,1)} %refs_0_.1, bf16[1,32,256]{2,1,0:T(8,128)(2,1)} %refs_1_.1, bf16[1,32,256]{2,1,0:T(8,128)(2,1)} %refs_2_.2, bf16[1,32,256]{2,1,0:T(8,128)(2,1)} %refs_3_.1, bf16[24,32,256]{2,1,0:T(8,128)(2,1)} %refs_4_.1, ...), custom_call_target="tpu_custom_call" | custom-call | flops 67108864 | bytes 1048576 | tf_op jit(solution)/shard_map/pallas_call | solution.py:73
  3.4 2.1 %collective-permute-start.2 = (bf16[24,48,256]{2,1,0:T(8,128)(2,1)}, bf16[24,48,256]{2,1,0:T(8,128)(2,1)S(1)}, u32[]{:S(2)}, u32[]{:S(2)}) collective-permute-start(bf16[24,48,256]{2,1,0:T(8,128)(2,1)} %get-tuple-element.71.refs_0_), channel_id=1, source_target_pairs={{0,4},{1,5},{2,6},{3,7},{4,0},{5,1},{6,2},{7,3},{8,12},{9,13},{10,... | collective-permute-start | bytes 1769480 | tf_op jit(solution)/shard_map/ppermute | solution.py:57
  5.5 2.7 %collective-permute-start.1 = (bf16[24,48,256]{2,1,0:T(8,128)(2,1)}, bf16[24,48,256]{2,1,0:T(8,128)(2,1)S(1)}, u32[]{:S(2)}, u32[]{:S(2)}) collective-permute-start(bf16[24,48,256]{2,1,0:T(8,128)(2,1)} %get-tuple-element.71.refs_0_), channel_id=1, source_target_pairs={{0,3},{1,0},{2,1},{3,2},{4,7},{5,4},{6,5},{7,6},{8,11},{9,8},{10,9... | collective-permute-start | bytes 1769480 | tf_op jit(solution)/shard_map/ppermute | solution.py:53
  8.2 0.0 collective-permute-start
  8.2 4.0 %all-to-all-start = ((bf16[8,128,256]{2,1,0:T(8,128)(2,1)}), bf16[8,128,256]{2,1,0:T(8,128)(2,1)S(1)}, u32[]{:S(2)}, u32[]{:S(2)}) async-start(bf16[8,128,256]{2,1,0:T(8,128)(2,1)} %get-tuple-element.72), calls=%async_computation | async-start | bytes 1048576 | tf_op jit(solution)/shard_map/all_to_all | solution.py:399
  12.2 1.1 %copy-done.2 = bf16[24,48,256]{2,1,0:T(8,128)(2,1)S(1)} copy-done((bf16[24,48,256]{2,1,0:T(8,128)(2,1)S(1)}, bf16[24,48,256]{2,1,0:T(8,128)(2,1)}, u32[]{:S(2)}) %copy-start.2) | copy-done | bytes 589848
  13.3 0.9 %copy-done.3 = bf16[1,256,512]{2,1,0:T(8,128)(2,1)S(1)} copy-done((bf16[1,256,512]{2,1,0:T(8,128)(2,1)S(1)}, bf16[1,256,512]{2,1,0:T(8,128)(2,1)}, u32[]{:S(2)}) %copy-start.3) | copy-done | bytes 262168
  14.2 0.7 copy-done.6
  14.9 0.2 shard_map.131
  15.1 13.1 %all-to-all-done.rows = bf16[8,128,256]{2,1,0:T(8,128)(2,1)S(1)} async-done(((bf16[8,128,256]{2,1,0:T(8,128)(2,1)}), bf16[8,128,256]{2,1,0:T(8,128)(2,1)S(1)}, u32[]{:S(2)}, u32[]{:S(2)}) %all-to-all-start) | async-done | bytes 524320 | tf_op jit(solution)/shard_map/all_to_all | solution.py:399
  28.2 0.0 collective-permute-done.2.refs_3_
  28.2 0.0 collective-permute-done.1.refs_2_
  28.2 0.0 collective-permute-done.refs_1_
  28.2 1.1 %collective-permute-start.5 = (bf16[24,48,256]{2,1,0:T(8,128)(2,1)S(1)}, bf16[24,48,256]{2,1,0:T(8,128)(2,1)S(1)}, u32[]{:S(2)}, u32[]{:S(2)}) collective-permute-start(bf16[24,48,256]{2,1,0:T(8,128)(2,1)S(1)} %collective-permute-done.2.refs_3_), channel_id=1, source_target_pairs={{0,3},{1,0},{2,1},{3,2},{4,7},{5,4},{6,5},{7,6},{8,11},{9,8},{10,9... | collective-permute-start | bytes 1769480 | tf_op jit(solution)/shard_map/ppermute | solution.py:53
  29.2 0.3 collective-permute-start.4
  29.5 0.6 collective-permute-start.3
  30.1 2.8 %copy-done = bf16[24,256,512]{2,1,0:T(8,128)(2,1)S(1)} copy-done((bf16[24,256,512]{2,1,0:T(8,128)(2,1)S(1)}, bf16[24,256,512]{2,1,0:T(8,128)(2,1)}, u32[]{:S(2)}) %copy-start) | copy-done | bytes 6291480
  32.9 0.3 shard_map.133
  33.3 3.6 %collective-permute-start.8 = (bf16[3,256,256]{2,1,0:T(8,128)(2,1)S(1)}, bf16[3,256,256]{2,1,0:T(8,128)(2,1)S(1)}, u32[]{:S(2)}, u32[]{:S(2)}) collective-permute-start(bf16[3,256,256]{2,1,0:T(8,128)(2,1)S(1)} %get-tuple-element.91), channel_id=1, source_target_pairs={{0,8},{8,0},{16,24},{24,16},{32,40},{40,32},{48,56},{56,48},{64,72... | collective-permute-start | bytes 1179656 | tf_op jit(solution)/shard_map/ppermute | solution.py:61
  36.9 1.3 %collective-permute-done.8.got = bf16[3,256,256]{2,1,0:T(8,128)(2,1)S(1)} collective-permute-done((bf16[3,256,256]{2,1,0:T(8,128)(2,1)S(1)}, bf16[3,256,256]{2,1,0:T(8,128)(2,1)S(1)}, u32[]{:S(2)}, u32[]{:S(2)}) %collective-permute-start.8) | collective-permute-done | bytes 393248 | tf_op jit(solution)/shard_map/ppermute | solution.py:61
  38.2 0.1 shard_map.135
  38.3 3.8 %collective-permute-start.12 = (bf16[2,256,256]{2,1,0:T(8,128)(2,1)S(1)}, bf16[2,256,256]{2,1,0:T(8,128)(2,1)S(1)}, u32[]{:S(2)}, u32[]{:S(2)}) collective-permute-start(bf16[2,256,256]{2,1,0:T(8,128)(2,1)S(1)} %get-tuple-element.95.part), channel_id=1, source_target_pairs={{0,48},{8,56},{16,0},{24,8},{32,16},{40,24},{48,32},{56,40},{64,11... | collective-permute-start | bytes 786440 | tf_op jit(solution)/shard_map/ppermute | solution.py:61
  42.1 0.0 collective-permute-start.11
  42.1 0.0 collective-permute-done.5.refs_6_
  42.1 0.7 collective-permute-start.10
  42.8 0.0 collective-permute-done.4.refs_5_
  42.8 0.3 collective-permute-done.3.refs_4_
  43.2 0.0 copy-start.4
  43.2 2.0 %collective-permute-start.7 = (bf16[12,48,256]{2,1,0:T(8,128)(2,1)S(1)}, bf16[12,48,256]{2,1,0:T(8,128)(2,1)S(1)}, u32[]{:S(2)}, u32[]{:S(2)}) collective-permute-start(bf16[12,48,256]{2,1,0:T(8,128)(2,1)S(1)} %slice.7), channel_id=1, source_target_pairs={{0,3},{1,0},{2,1},{3,2},{4,7},{5,4},{6,5},{7,6},{8,11},{9,8},{10,9... | collective-permute-start | bytes 884744 | tf_op jit(solution)/shard_map/ppermute | solution.py:53
  45.2 0.0 collective-permute-start.6
  45.2 7.8 %collective-permute-done.12.refs_2_ = bf16[2,256,256]{2,1,0:T(8,128)(2,1)S(1)} collective-permute-done((bf16[2,256,256]{2,1,0:T(8,128)(2,1)S(1)}, bf16[2,256,256]{2,1,0:T(8,128)(2,1)S(1)}, u32[]{:S(2)}, u32[]{:S(2)}) %collective-permute-start.12) | collective-permute-done | bytes 262176 | tf_op jit(solution)/shard_map/ppermute | solution.py:61
  53.0 1.2 %collective-permute-start.15 = (bf16[2,256,256]{2,1,0:T(8,128)(2,1)S(1)}, bf16[2,256,256]{2,1,0:T(8,128)(2,1)S(1)}, u32[]{:S(2)}, u32[]{:S(2)}) collective-permute-start(bf16[2,256,256]{2,1,0:T(8,128)(2,1)S(1)} %collective-permute-done.12.refs_2_), channel_id=1, source_target_pairs={{0,8},{8,0},{16,24},{24,16},{32,40},{40,32},{48,56},{56,48},{64,72... | collective-permute-start | bytes 786440 | tf_op jit(solution)/shard_map/ppermute | solution.py:61
  54.2 0.0 collective-permute-start.14
  54.3 2.6 %collective-permute-done.10.refs_0_ = bf16[2,256,256]{2,1,0:T(8,128)(2,1)S(1)} collective-permute-done((bf16[2,256,256]{2,1,0:T(8,128)(2,1)S(1)}, bf16[2,256,256]{2,1,0:T(8,128)(2,1)S(1)}, u32[]{:S(2)}, u32[]{:S(2)}) %collective-permute-start.10) | collective-permute-done | bytes 262176 | tf_op jit(solution)/shard_map/ppermute | solution.py:61
  56.8 0.8 collective-permute-start.13
  57.7 0.0 collective-permute-done.7.refs_8_
  57.7 0.0 collective-permute-done.6.refs_7_
  57.7 3.3 %shard_map.132 = (bf16[24,256,256]{2,1,0:T(8,128)(2,1)S(1)}, bf16[24,256,256]{2,1,0:T(8,128)(2,1)S(1)}, f32[256,512]{1,0:T(8,128)S(1)}) custom-call(bf16[24,48,256]{2,1,0:T(8,128)(2,1)S(1)} %get-tuple-element.76.refs_0_, bf16[24,48,256]{2,1,0:T(8,128)(2,1)S(1)} %collective-permute-done.refs_1_, bf16[24,48,256]{2,1,0:T(8,128)(2,1)S(1)} %collective-permute-done.1.refs_2_, ...), custom_call_target="tpu_custom_call" | custom-call | flops 1048576 | bytes 16777216 | tf_op jit(solution)/shard_map/pallas_call | solution.py:73
  61.0 0.3 shard_map.134
  61.3 0.1 collective-permute-start.9
  61.4 0.0 collective-permute-done.15.refs_5_
  61.4 0.0 collective-permute-done.14.refs_4_
  61.4 1.3 %collective-permute-done.9.theirs = bf16[256,256]{1,0:T(8,128)(2,1)S(1)} collective-permute-done((bf16[256,256]{1,0:T(8,128)(2,1)S(1)}, bf16[256,256]{1,0:T(8,128)(2,1)S(1)}, u32[]{:S(2)}, u32[]{:S(2)}) %collective-permute-start.9) | collective-permute-done | bytes 131104 | tf_op jit(solution)/shard_map/ppermute | solution.py:61
  62.7 0.1 shard_map.137
  62.8 2.8 %collective-permute-start.16 = (bf16[2,256,256]{2,1,0:T(8,128)(2,1)S(1)}, bf16[2,256,256]{2,1,0:T(8,128)(2,1)S(1)}, u32[]{:S(2)}, u32[]{:S(2)}) collective-permute-start(bf16[2,256,256]{2,1,0:T(8,128)(2,1)S(1)} %get-tuple-element.106), channel_id=1, source_target_pairs={{0,64},{8,72},{16,80},{24,88},{32,96},{40,104},{48,112},{56,120},{... | collective-permute-start | bytes 786440 | tf_op jit(solution)/shard_map/ppermute | solution.py:61
  65.6 0.2 shard_map.136
  65.8 0.7 collective-permute-start.19
  66.5 0.9 %collective-permute-start.18 = (bf16[256,256]{1,0:T(8,128)(2,1)S(1)}, bf16[256,256]{1,0:T(8,128)(2,1)S(1)}, u32[]{:S(2)}, u32[]{:S(2)}) collective-permute-start(bf16[256,256]{1,0:T(8,128)(2,1)S(1)} %get-tuple-element.107.refs_6_), channel_id=1, source_target_pairs={{0,32},{8,40},{16,48},{24,56},{32,0},{40,8},{48,16},{56,24},{64,96... | collective-permute-start | bytes 393224 | tf_op jit(solution)/shard_map/ppermute | solution.py:61
  67.4 0.7 collective-permute-start.17
  68.2 1.0 %shard_map.139 = (bf16[8,256,512]{2,1,0:T(8,128)(2,1)S(1)}, bf16[8,256,256]{2,1,0:T(8,128)(2,1)S(1)}) custom-call(bf16[24,256,256]{2,1,0:T(8,128)(2,1)S(1)} %get-tuple-element.123.inv, bf16[24,256,256]{2,1,0:T(8,128)(2,1)S(1)} %get-tuple-element.108.m, bf16[24,256,512]{2,1,0:T(8,128)(2,1)S(1)} %copy-done.1), custom_call_target="tpu_custom_call" | custom-call | flops 1073741824 | bytes 1048576 | tf_op jit(solution)/shard_map/pallas_call | solution.py:73
  69.2 1.1 %shard_map.138 = (bf16[8,256,512]{2,1,0:T(8,128)(2,1)S(1)}, bf16[8,256,256]{2,1,0:T(8,128)(2,1)S(1)}) custom-call(bf16[24,256,256]{2,1,0:T(8,128)(2,1)S(1)} %get-tuple-element.123.inv, bf16[24,256,256]{2,1,0:T(8,128)(2,1)S(1)} %get-tuple-element.108.m, bf16[24,256,512]{2,1,0:T(8,128)(2,1)S(1)} %copy-done.1), custom_call_target="tpu_custom_call" | custom-call | flops 1073741824 | bytes 1048576 | tf_op jit(solution)/shard_map/pallas_call | solution.py:73
  70.3 0.2 collective-permute-done.19.refs_9_
  70.5 1.8 %collective-permute-done.18.refs_8_ = bf16[256,256]{1,0:T(8,128)(2,1)S(1)} collective-permute-done((bf16[256,256]{1,0:T(8,128)(2,1)S(1)}, bf16[256,256]{1,0:T(8,128)(2,1)S(1)}, u32[]{:S(2)}, u32[]{:S(2)}) %collective-permute-start.18) | collective-permute-done | bytes 131104 | tf_op jit(solution)/shard_map/ppermute | solution.py:61
  72.3 3.6 %collective-permute-done.17.refs_7_ = bf16[256,256]{1,0:T(8,128)(2,1)S(1)} collective-permute-done((bf16[256,256]{1,0:T(8,128)(2,1)S(1)}, bf16[256,256]{1,0:T(8,128)(2,1)S(1)}, u32[]{:S(2)}, u32[]{:S(2)}) %collective-permute-start.17) | collective-permute-done | bytes 131104 | tf_op jit(solution)/shard_map/ppermute | solution.py:61
  75.9 0.5 shard_map.140
  76.4 0.0 copy-start.5
  76.4 0.9 collective-permute-start.21
  77.3 0.2 collective-permute-start.20
  77.6 1.0 %shard_map.141 = (bf16[8,256,512]{2,1,0:T(8,128)(2,1)S(1)}, bf16[8,256,256]{2,1,0:T(8,128)(2,1)S(1)}) custom-call(bf16[24,256,256]{2,1,0:T(8,128)(2,1)S(1)} %get-tuple-element.123.inv, bf16[24,256,256]{2,1,0:T(8,128)(2,1)S(1)} %get-tuple-element.108.m, bf16[24,256,512]{2,1,0:T(8,128)(2,1)S(1)} %copy-done.1), custom_call_target="tpu_custom_call" | custom-call | flops 1073741824 | bytes 1048576 | tf_op jit(solution)/shard_map/pallas_call | solution.py:73
  78.6 5.3 %collective-permute-done.20.theirs = bf16[256,256]{1,0:T(8,128)(2,1)S(1)} collective-permute-done((bf16[256,256]{1,0:T(8,128)(2,1)S(1)}, bf16[256,256]{1,0:T(8,128)(2,1)S(1)}, u32[]{:S(2)}, u32[]{:S(2)}) %collective-permute-start.20) | collective-permute-done | bytes 131104 | tf_op jit(solution)/shard_map/ppermute | solution.py:61
  83.9 1.2 %shard_map.142.own = bf16[2,256,256]{2,1,0:T(8,128)(2,1)S(1)} custom-call(bf16[256,256]{1,0:T(8,128)(2,1)S(1)} %get-tuple-element.118.mine, bf16[256,256]{1,0:T(8,128)(2,1)S(1)} %collective-permute-done.20.theirs, bf16[3,256,256]{2,1,0:T(8,128)(2,1)S(1)} %get-tuple-element.127.top, bf16[2,256,256]{2,1,0:T(8,128)(2,1)S(1)} %collective-permute-done.16.far, ...), custom_call_target="tpu_custom_call" | custom-call | flops 67108864 | bytes 1048576 | tf_op jit(solution)/shard_map/pallas_call | solution.py:73
  85.1 0.9 %collective-permute-start.22 = (bf16[2,256,256]{2,1,0:T(8,128)(2,1)S(1)}, bf16[2,256,256]{2,1,0:T(8,128)(2,1)S(1)}, u32[]{:S(2)}, u32[]{:S(2)}) collective-permute-start(bf16[2,256,256]{2,1,0:T(8,128)(2,1)S(1)} %shard_map.142.own), channel_id=1, source_target_pairs={{0,8},{8,0},{16,24},{24,16},{32,40},{40,32},{48,56},{56,48},{64,72... | collective-permute-start | bytes 786440 | tf_op jit(solution)/shard_map/ppermute | solution.py:61
  86.1 1.2 %collective-permute-done.22.got = bf16[2,256,256]{2,1,0:T(8,128)(2,1)S(1)} collective-permute-done((bf16[2,256,256]{2,1,0:T(8,128)(2,1)S(1)}, bf16[2,256,256]{2,1,0:T(8,128)(2,1)S(1)}, u32[]{:S(2)}, u32[]{:S(2)}) %collective-permute-start.22) | collective-permute-done | bytes 262176 | tf_op jit(solution)/shard_map/ppermute | solution.py:61
  87.2 3.5 %shard_map.143 = (bf16[24,256,512]{2,1,0:T(8,128)(2,1)}, bf16[1,256,512]{2,1,0:T(8,128)(2,1)}, bf16[1,256,512]{2,1,0:T(8,128)(2,1)}) custom-call(bf16[256,512]{1,0:T(8,128)(2,1)S(1)} %get-tuple-element.88.r, bf16[2,256,256]{2,1,0:T(8,128)(2,1)S(1)} %get-tuple-element.87.mats, bf16[2,256,256]{2,1,0:T(8,128)(2,1)S(1)} %shard_map.142.own, ...), custom_call_target="tpu_custom_call" | custom-call | flops 2147483648 | bytes 16777216 | tf_op jit(solution)/shard_map/pallas_call | solution.py:73
  (14 shorter events, 0.1 us)
Async XLA Ops:
  3.4 24.8 %collective-permute-start.2 = (bf16[24,48,256]{2,1,0:T(8,128)(2,1)}, bf16[24,48,256]{2,1,0:T(8,128)(2,1)S(1)}, u32[]{:S(2)}, u32[]{:S(2)}) collective-permute-start(bf16[24,48,256]{2,1,0:T(8,128)(2,1)} %get-tuple-element.71.refs_0_), channel_id=1, source_target_pairs={{0,4},{1,5},{2,6},{3,7},{4,0},{5,1},{6,2},{7,3},{8,12},{9,13},{10,... | collective-permute-start | bytes 1769480 | tf_op jit(solution)/shard_map/ppermute | solution.py:57
  5.5 22.7 %collective-permute-start.1 = (bf16[24,48,256]{2,1,0:T(8,128)(2,1)}, bf16[24,48,256]{2,1,0:T(8,128)(2,1)S(1)}, u32[]{:S(2)}, u32[]{:S(2)}) collective-permute-start(bf16[24,48,256]{2,1,0:T(8,128)(2,1)} %get-tuple-element.71.refs_0_), channel_id=1, source_target_pairs={{0,3},{1,0},{2,1},{3,2},{4,7},{5,4},{6,5},{7,6},{8,11},{9,8},{10,9... | collective-permute-start | bytes 1769480 | tf_op jit(solution)/shard_map/ppermute | solution.py:53
  8.2 19.9 %collective-permute-start = (bf16[24,48,256]{2,1,0:T(8,128)(2,1)}, bf16[24,48,256]{2,1,0:T(8,128)(2,1)S(1)}, u32[]{:S(2)}, u32[]{:S(2)}) collective-permute-start(bf16[24,48,256]{2,1,0:T(8,128)(2,1)} %get-tuple-element.71.refs_0_), channel_id=1, source_target_pairs={{0,1},{1,2},{2,3},{3,0},{4,5},{5,6},{6,7},{7,4},{8,9},{9,10},{10,1... | collective-permute-start | bytes 1769480 | tf_op jit(solution)/shard_map/ppermute | solution.py:49
  8.2 19.9 %all-to-all-start = ((bf16[8,128,256]{2,1,0:T(8,128)(2,1)}), bf16[8,128,256]{2,1,0:T(8,128)(2,1)S(1)}, u32[]{:S(2)}, u32[]{:S(2)}) async-start(bf16[8,128,256]{2,1,0:T(8,128)(2,1)} %get-tuple-element.72), calls=%async_computation | async-start | bytes 1048576 | tf_op jit(solution)/shard_map/all_to_all | solution.py:399
  12.2 1.1 %copy-start.2 = (bf16[24,48,256]{2,1,0:T(8,128)(2,1)S(1)}, bf16[24,48,256]{2,1,0:T(8,128)(2,1)}, u32[]{:S(2)}) copy-start(bf16[24,48,256]{2,1,0:T(8,128)(2,1)} %get-tuple-element.71.refs_0_) | copy-start | bytes 1769476
  13.3 0.9 %copy-start.3 = (bf16[1,256,512]{2,1,0:T(8,128)(2,1)S(1)}, bf16[1,256,512]{2,1,0:T(8,128)(2,1)}, u32[]{:S(2)}) copy-start(bf16[1,256,512]{2,1,0:T(8,128)(2,1)} %refs_2_.3) | copy-start | bytes 786436
  14.2 0.7 copy-start.6
  28.2 13.9 %collective-permute-start.5 = (bf16[24,48,256]{2,1,0:T(8,128)(2,1)S(1)}, bf16[24,48,256]{2,1,0:T(8,128)(2,1)S(1)}, u32[]{:S(2)}, u32[]{:S(2)}) collective-permute-start(bf16[24,48,256]{2,1,0:T(8,128)(2,1)S(1)} %collective-permute-done.2.refs_3_), channel_id=1, source_target_pairs={{0,3},{1,0},{2,1},{3,2},{4,7},{5,4},{6,5},{7,6},{8,11},{9,8},{10,9... | collective-permute-start | bytes 1769480 | tf_op jit(solution)/shard_map/ppermute | solution.py:53
  29.2 13.6 %collective-permute-start.4 = (bf16[24,48,256]{2,1,0:T(8,128)(2,1)S(1)}, bf16[24,48,256]{2,1,0:T(8,128)(2,1)S(1)}, u32[]{:S(2)}, u32[]{:S(2)}) collective-permute-start(bf16[24,48,256]{2,1,0:T(8,128)(2,1)S(1)} %collective-permute-done.refs_1_), channel_id=1, source_target_pairs={{0,4},{1,5},{2,6},{3,7},{4,0},{5,1},{6,2},{7,3},{8,12},{9,13},{10,... | collective-permute-start | bytes 1769480 | tf_op jit(solution)/shard_map/ppermute | solution.py:57
  29.5 13.6 %collective-permute-start.3 = (bf16[24,48,256]{2,1,0:T(8,128)(2,1)S(1)}, bf16[24,48,256]{2,1,0:T(8,128)(2,1)S(1)}, u32[]{:S(2)}, u32[]{:S(2)}) collective-permute-start(bf16[24,48,256]{2,1,0:T(8,128)(2,1)S(1)} %collective-permute-done.refs_1_), channel_id=1, source_target_pairs={{0,1},{1,2},{2,3},{3,0},{4,5},{5,6},{6,7},{7,4},{8,9},{9,10},{10,1... | collective-permute-start | bytes 1769480 | tf_op jit(solution)/shard_map/ppermute | solution.py:49
  30.1 2.8 %copy-start = (bf16[24,256,512]{2,1,0:T(8,128)(2,1)S(1)}, bf16[24,256,512]{2,1,0:T(8,128)(2,1)}, u32[]{:S(2)}) copy-start(bf16[24,256,512]{2,1,0:T(8,128)(2,1)} %rhs.7) | copy-start | bytes 18874372
  32.9 24.8 %copy-start.1 = (bf16[24,256,512]{2,1,0:T(8,128)(2,1)S(1)}, bf16[24,256,512]{2,1,0:T(8,128)(2,1)}, u32[]{:S(2)}) copy-start(bf16[24,256,512]{2,1,0:T(8,128)(2,1)} %rhs.7) | copy-start | bytes 18874372
  33.3 5.0 %collective-permute-start.8 = (bf16[3,256,256]{2,1,0:T(8,128)(2,1)S(1)}, bf16[3,256,256]{2,1,0:T(8,128)(2,1)S(1)}, u32[]{:S(2)}, u32[]{:S(2)}) collective-permute-start(bf16[3,256,256]{2,1,0:T(8,128)(2,1)S(1)} %get-tuple-element.91), channel_id=1, source_target_pairs={{0,8},{8,0},{16,24},{24,16},{32,40},{40,32},{48,56},{56,48},{64,72... | collective-permute-start | bytes 1179656 | tf_op jit(solution)/shard_map/ppermute | solution.py:61
  38.3 14.8 %collective-permute-start.12 = (bf16[2,256,256]{2,1,0:T(8,128)(2,1)S(1)}, bf16[2,256,256]{2,1,0:T(8,128)(2,1)S(1)}, u32[]{:S(2)}, u32[]{:S(2)}) collective-permute-start(bf16[2,256,256]{2,1,0:T(8,128)(2,1)S(1)} %get-tuple-element.95.part), channel_id=1, source_target_pairs={{0,48},{8,56},{16,0},{24,8},{32,16},{40,24},{48,32},{56,40},{64,11... | collective-permute-start | bytes 786440 | tf_op jit(solution)/shard_map/ppermute | solution.py:61
  42.1 12.1 %collective-permute-start.11 = (bf16[2,256,256]{2,1,0:T(8,128)(2,1)S(1)}, bf16[2,256,256]{2,1,0:T(8,128)(2,1)S(1)}, u32[]{:S(2)}, u32[]{:S(2)}) collective-permute-start(bf16[2,256,256]{2,1,0:T(8,128)(2,1)S(1)} %get-tuple-element.95.part), channel_id=1, source_target_pairs={{0,32},{8,40},{16,48},{24,56},{32,0},{40,8},{48,16},{56,24},{64,96... | collective-permute-start | bytes 786440 | tf_op jit(solution)/shard_map/ppermute | solution.py:61
  42.1 14.7 %collective-permute-start.10 = (bf16[2,256,256]{2,1,0:T(8,128)(2,1)S(1)}, bf16[2,256,256]{2,1,0:T(8,128)(2,1)S(1)}, u32[]{:S(2)}, u32[]{:S(2)}) collective-permute-start(bf16[2,256,256]{2,1,0:T(8,128)(2,1)S(1)} %get-tuple-element.95.part), channel_id=1, source_target_pairs={{0,16},{8,24},{16,32},{24,40},{32,48},{40,56},{48,0},{56,8},{64,80... | collective-permute-start | bytes 786440 | tf_op jit(solution)/shard_map/ppermute | solution.py:61
  43.2 17.8 %copy-start.4 = (bf16[1,256,512]{2,1,0:T(8,128)(2,1)S(1)}, bf16[1,256,512]{2,1,0:T(8,128)(2,1)}, u32[]{:S(2)}) copy-start(bf16[1,256,512]{2,1,0:T(8,128)(2,1)} %rhs.4) | copy-start | bytes 786436
  43.2 14.5 %collective-permute-start.7 = (bf16[12,48,256]{2,1,0:T(8,128)(2,1)S(1)}, bf16[12,48,256]{2,1,0:T(8,128)(2,1)S(1)}, u32[]{:S(2)}, u32[]{:S(2)}) collective-permute-start(bf16[12,48,256]{2,1,0:T(8,128)(2,1)S(1)} %slice.7), channel_id=1, source_target_pairs={{0,3},{1,0},{2,1},{3,2},{4,7},{5,4},{6,5},{7,6},{8,11},{9,8},{10,9... | collective-permute-start | bytes 884744 | tf_op jit(solution)/shard_map/ppermute | solution.py:53
  45.2 12.5 %collective-permute-start.6 = (bf16[12,48,256]{2,1,0:T(8,128)(2,1)S(1)}, bf16[12,48,256]{2,1,0:T(8,128)(2,1)S(1)}, u32[]{:S(2)}, u32[]{:S(2)}) collective-permute-start(bf16[12,48,256]{2,1,0:T(8,128)(2,1)S(1)} %slice.6), channel_id=1, source_target_pairs={{0,1},{1,2},{2,3},{3,0},{4,5},{5,6},{6,7},{7,4},{8,9},{9,10},{10,1... | collective-permute-start | bytes 884744 | tf_op jit(solution)/shard_map/ppermute | solution.py:49
  53.0 8.3 %collective-permute-start.15 = (bf16[2,256,256]{2,1,0:T(8,128)(2,1)S(1)}, bf16[2,256,256]{2,1,0:T(8,128)(2,1)S(1)}, u32[]{:S(2)}, u32[]{:S(2)}) collective-permute-start(bf16[2,256,256]{2,1,0:T(8,128)(2,1)S(1)} %collective-permute-done.12.refs_2_), channel_id=1, source_target_pairs={{0,8},{8,0},{16,24},{24,16},{32,40},{40,32},{48,56},{56,48},{64,72... | collective-permute-start | bytes 786440 | tf_op jit(solution)/shard_map/ppermute | solution.py:61
  54.2 7.1 %collective-permute-start.14 = (bf16[2,256,256]{2,1,0:T(8,128)(2,1)S(1)}, bf16[2,256,256]{2,1,0:T(8,128)(2,1)S(1)}, u32[]{:S(2)}, u32[]{:S(2)}) collective-permute-start(bf16[2,256,256]{2,1,0:T(8,128)(2,1)S(1)} %collective-permute-done.11.refs_1_), channel_id=1, source_target_pairs={{0,8},{8,0},{16,24},{24,16},{32,40},{40,32},{48,56},{56,48},{64,72... | collective-permute-start | bytes 786440 | tf_op jit(solution)/shard_map/ppermute | solution.py:61
  56.8 4.6 %collective-permute-start.13 = (bf16[2,256,256]{2,1,0:T(8,128)(2,1)S(1)}, bf16[2,256,256]{2,1,0:T(8,128)(2,1)S(1)}, u32[]{:S(2)}, u32[]{:S(2)}) collective-permute-start(bf16[2,256,256]{2,1,0:T(8,128)(2,1)S(1)} %collective-permute-done.10.refs_0_), channel_id=1, source_target_pairs={{0,8},{8,0},{16,24},{24,16},{32,40},{40,32},{48,56},{56,48},{64,72... | collective-permute-start | bytes 786440 | tf_op jit(solution)/shard_map/ppermute | solution.py:61
  61.3 1.4 %collective-permute-start.9 = (bf16[256,256]{1,0:T(8,128)(2,1)S(1)}, bf16[256,256]{1,0:T(8,128)(2,1)S(1)}, u32[]{:S(2)}, u32[]{:S(2)}) collective-permute-start(bf16[256,256]{1,0:T(8,128)(2,1)S(1)} %get-tuple-element.94), channel_id=1, source_target_pairs={{0,8},{8,0},{16,24},{24,16},{32,40},{40,32},{48,56},{56,48},{64,72... | collective-permute-start | bytes 393224 | tf_op jit(solution)/shard_map/ppermute | solution.py:61
  62.8 13.6 %collective-permute-start.16 = (bf16[2,256,256]{2,1,0:T(8,128)(2,1)S(1)}, bf16[2,256,256]{2,1,0:T(8,128)(2,1)S(1)}, u32[]{:S(2)}, u32[]{:S(2)}) collective-permute-start(bf16[2,256,256]{2,1,0:T(8,128)(2,1)S(1)} %get-tuple-element.106), channel_id=1, source_target_pairs={{0,64},{8,72},{16,80},{24,88},{32,96},{40,104},{48,112},{56,120},{... | collective-permute-start | bytes 786440 | tf_op jit(solution)/shard_map/ppermute | solution.py:61
  65.8 4.7 %collective-permute-start.19 = (bf16[256,256]{1,0:T(8,128)(2,1)S(1)}, bf16[256,256]{1,0:T(8,128)(2,1)S(1)}, u32[]{:S(2)}, u32[]{:S(2)}) collective-permute-start(bf16[256,256]{1,0:T(8,128)(2,1)S(1)} %get-tuple-element.107.refs_6_), channel_id=1, source_target_pairs={{0,48},{8,56},{16,0},{24,8},{32,16},{40,24},{48,32},{56,40},{64,11... | collective-permute-start | bytes 393224 | tf_op jit(solution)/shard_map/ppermute | solution.py:61
  66.5 5.8 %collective-permute-start.18 = (bf16[256,256]{1,0:T(8,128)(2,1)S(1)}, bf16[256,256]{1,0:T(8,128)(2,1)S(1)}, u32[]{:S(2)}, u32[]{:S(2)}) collective-permute-start(bf16[256,256]{1,0:T(8,128)(2,1)S(1)} %get-tuple-element.107.refs_6_), channel_id=1, source_target_pairs={{0,32},{8,40},{16,48},{24,56},{32,0},{40,8},{48,16},{56,24},{64,96... | collective-permute-start | bytes 393224 | tf_op jit(solution)/shard_map/ppermute | solution.py:61
  67.4 8.5 %collective-permute-start.17 = (bf16[256,256]{1,0:T(8,128)(2,1)S(1)}, bf16[256,256]{1,0:T(8,128)(2,1)S(1)}, u32[]{:S(2)}, u32[]{:S(2)}) collective-permute-start(bf16[256,256]{1,0:T(8,128)(2,1)S(1)} %get-tuple-element.107.refs_6_), channel_id=1, source_target_pairs={{0,16},{8,24},{16,32},{24,40},{32,48},{40,56},{48,0},{56,8},{64,80... | collective-permute-start | bytes 393224 | tf_op jit(solution)/shard_map/ppermute | solution.py:61
  76.4 7.5 %copy-start.5 = (bf16[256,512]{1,0:T(8,128)(2,1)S(1)}, bf16[256,512]{1,0:T(8,128)(2,1)}, u32[]{:S(2)}) copy-start(bf16[256,512]{1,0:T(8,128)(2,1)} %above.1) | copy-start | bytes 786436
  76.4 7.5 %collective-permute-start.21 = (bf16[2,256,256]{2,1,0:T(8,128)(2,1)S(1)}, bf16[2,256,256]{2,1,0:T(8,128)(2,1)S(1)}, u32[]{:S(2)}, u32[]{:S(2)}) collective-permute-start(bf16[2,256,256]{2,1,0:T(8,128)(2,1)S(1)} %collective-permute-done.16.far), channel_id=1, source_target_pairs={{0,8},{8,0},{16,24},{24,16},{32,40},{40,32},{48,56},{56,48},{64,72... | collective-permute-start | bytes 786440 | tf_op jit(solution)/shard_map/ppermute | solution.py:61
  77.3 6.6 %collective-permute-start.20 = (bf16[256,256]{1,0:T(8,128)(2,1)S(1)}, bf16[256,256]{1,0:T(8,128)(2,1)S(1)}, u32[]{:S(2)}, u32[]{:S(2)}) collective-permute-start(bf16[256,256]{1,0:T(8,128)(2,1)S(1)} %get-tuple-element.118.mine), channel_id=1, source_target_pairs={{0,64},{8,72},{16,80},{24,88},{32,96},{40,104},{48,112},{56,120},{... | collective-permute-start | bytes 393224 | tf_op jit(solution)/shard_map/ppermute | solution.py:61
  85.1 2.1 %collective-permute-start.22 = (bf16[2,256,256]{2,1,0:T(8,128)(2,1)S(1)}, bf16[2,256,256]{2,1,0:T(8,128)(2,1)S(1)}, u32[]{:S(2)}, u32[]{:S(2)}) collective-permute-start(bf16[2,256,256]{2,1,0:T(8,128)(2,1)S(1)} %shard_map.142.own), channel_id=1, source_target_pairs={{0,8},{8,0},{16,24},{24,16},{32,40},{40,32},{48,56},{56,48},{64,72... | collective-permute-start | bytes 786440 | tf_op jit(solution)/shard_map/ppermute | solution.py:61

commit v4 on v3

--- a/solution.py
+++ b/solution.py
@@ -95,12 +95,20 @@
     return lax.rem(position, 2), lax.rem(position // 2, 4), position // 8
 
 
-def pack_kernel(*refs):
-    smalls, (inv, upd, out, small, sems) = refs[:4], refs[4:]
-    pairs = [(inv, out.at[:, pl.ds(0, 32)]), (upd, out.at[:, pl.ds(32, 16)])]
+def pack_kernel(inv, upd, out, sems):
+    move([(inv, out.at[:, pl.ds(0, 32)]), (upd, out.at[:, pl.ds(32, 16)])], sems)
+
+
+def pack_small_kernel(*refs):
+    smalls, (out, sems) = refs[:4], refs[4:]
+    pairs = []
     for n, ref in enumerate(smalls):
         for to in range(8):
-            pairs.append((ref.at[0], small.at[to, pl.ds(32 * n, 32)]))
+            pairs.append((ref.at[0], out.at[to, pl.ds(32 * n, 32)]))
+    move(pairs, sems)
+
+
+def move(pairs, sems):
     copies = [pltpu.make_async_copy(a, b, sems.at[n]) for n, (a, b) in enumerate(pairs)]
     for copy in copies:
         copy.start()
@@ -264,14 +272,13 @@
                 mats[n, 1] = p[j][1]
 
 
-def choose_kernel(odd, part, *refs):
-    mine, theirs, (top, carried) = refs[:3], refs[3:6], refs[6:]
+def choose_kernel(odd, *refs):
+    mine, theirs, top = refs[:3], refs[3:6], refs[6]
     core, z, _ = leaf_place()
 
     @pl.when(z == 3)
     def _():
         top[...] = odd[...]
-        carried[...] = part[...]
 
     for k in range(3):
 
@@ -279,10 +286,9 @@
         def _():
             for n, value in enumerate(joined(core, mine[k], theirs[k])):
                 top[n] = value
-            carried[...] = mine[k][...]
-
-
-def top_kernel(mine, theirs, top, far, far2, t0, t, r0, r, above, out, p3, p4):
+
+
+def top_kernel(mine, theirs, top, far, t0, t, r0, r, above, out, p3, p4):
     core, z, x_hi = leaf_place()
     above = above[:, pl.ds(pl.multiple_of(core * 256, 256), 256)]
     for h, (a, b) in enumerate(((p3, p4), (p4, p3))):
@@ -290,8 +296,7 @@
         @pl.when(x_hi == h)
         def _():
             a[...] = top[...]
-            for n, value in enumerate(joined(core, far, far2)):
-                b[n] = value
+            b[...] = far[...]
 
     r3 = sub(p3[2], f32sum(mine[...], theirs[...]))
     r4 = sub(p4[2], mm(p3[0], r3).astype(BF).astype(F32))
@@ -383,18 +388,25 @@
     sep_inverse,
     sep_coupling,
 ):
-    w, small = call(
+    (w,) = call(
         pack_kernel,
-        [(24, 48, 256), (8, 128, 256)],
+        [(24, 48, 256)],
+        leaf_inverse,
+        leaf_update,
+        scratch=[pltpu.SemaphoreType.DMA((2,))],
+        limit=56,
+        in_specs=[ANY] * 2,
+    )
+    (small,) = call(
+        pack_small_kernel,
+        [(8, 128, 256)],
         root_inverse,
         root_coupling,
         sep_inverse,
         sep_coupling,
-        leaf_inverse,
-        leaf_update,
-        scratch=[pltpu.SemaphoreType.DMA((34,))],
+        scratch=[pltpu.SemaphoreType.DMA((32,))],
         limit=56,
-        in_specs=[ANY] * 6,
+        in_specs=[ANY] * 4,
     )
     small = lax.all_to_all(small, "load", 0, 0)
     arrived = up(w), down(w), across(w), small
@@ -433,10 +445,10 @@
     )
     packs2 = [among(v, CORES) for v in packs]
     theirs, packs, packs2 = lax.optimization_barrier((among(send, CORES), packs, packs2))
-    top, carried = call(
-        choose_kernel, [(3, 256, 256), (2, 256, 256)], odd, part, *packs, *packs2
-    )
-    far = among(carried, X_HI)
+    (top,) = call(
+        choose_kernel, [(3, 256, 256)], odd, *packs, *packs2
+    )
+    far = among(top, X_HI)
     r0, flow, t0 = call(
         first_kernel,
         [(256, 256), (256, 256), (2, 256, 256)],
@@ -457,9 +469,7 @@
         flow,
         *flows,
     )
-    far, flow = lax.optimization_barrier((far, flow))
     theirs = among(flow, X_HI)
-    far2 = among(far, CORES)
     held, flow = lax.optimization_barrier((held, flow))
     parts.append(prepare(16, 8, held, m, rhs_leaves))
     theirs, parts = lax.optimization_barrier((theirs, parts))
@@ -470,7 +480,6 @@
         theirs,
         top,
         far,
-        far2,
         t0,
         t,
         r0,

time: 91.3 us -> 89.7 us (0.982)
  waiting for transfers between devices: 38.5 us -> 35.3 us
  Pallas kernels: 15.6 us -> 17.1 us
    all_to_all x1, waiting for transfers between devices: 13.1 us -> 10.6 us  [local(): small = lax.all_to_all(small, 'load', 0, 0)]
    pallas_call x14 -> x15, Pallas kernels: 15.6 us -> 17.1 us  [call(): pl.pallas_call(kernel, in_specs=specs.get('in_specs', [VMEM] * len(args))...]
    ppermute x15 -> x14, waiting for transfers between devices: 25.1 us -> 24.4 us  [among(): return lax.ppermute(v, 'leaf', pairs)]
    ppermute x15 -> x14, starting transfers between devices: 17.5 us -> 17.4 us  [among(): return lax.ppermute(v, 'leaf', pairs)]
  transfers between devices with their start and end apart: 24 -> 23, of which waited for: 11 -> 11; matrix products, arithmetic and copies ran while one was open for 0% -> 0% of each run, Pallas kernels for 9% -> 12%
where the time goes in v4:
time: 89.7 us; the launch traced here: 89.2 us
  waiting for transfers between devices  35.3 us (39%)
  starting transfers between devices  30.2 us (34%)
  Pallas kernels  17.1 us (19%)
  local copies, waits for them, and re-layouts  5.56 us (6%)
  between operations  0.99 us (1%)
    ppermute x14, waiting for transfers between devices, among(): return lax.ppermute(v, 'leaf', pairs)  24.4 us
    ppermute x14, starting transfers between devices, among(): return lax.ppermute(v, 'leaf', pairs)  17.4 us
    pallas_call x15, Pallas kernels, call(): pl.pallas_call(kernel, in_specs=specs.get('in_specs', [VMEM] * len(args))...  17.1 us
    all_to_all x1, waiting for transfers between devices, local(): small = lax.all_to_all(small, 'load', 0, 0)  10.6 us
    ppermute x3, starting transfers between devices, down(): return lax.ppermute(v, 'load', y_shift(3))  5.82 us
    unnamed x14, local copies, waits for them, and re-layouts  5.52 us
    all_to_all x1, starting transfers between devices, local(): small = lax.all_to_all(small, 'load', 0, 0)  3.96 us
    ppermute x2, starting transfers between devices, across(): return lax.ppermute(v, 'load', X_LO)  2.37 us
  transfers between devices with their start and end apart: 23, of which 11 were waited for; matrix products, arithmetic and copies ran while one was open for 0% of the time, Pallas kernels for 12%

profile of v4, /device:TPU:1, one launch (start us, length us, event | category | flops | bytes accessed | tf_op | source)
XLA Modules:
  0.0 89.2 jit_solution(3089806968484316582)
XLA Ops:
  0.6 1.9 %shard_map.130.refs_0_ = bf16[24,48,256]{2,1,0:T(8,128)(2,1)} custom-call(bf16[24,32,256]{2,1,0:T(8,128)(2,1)} %inv.1, bf16[24,16,256]{2,1,0:T(8,128)(2,1)} %upd.1), custom_call_target="tpu_custom_call" | custom-call | flops 67108864 | bytes 1048576 | tf_op jit(solution)/shard_map/pallas_call | solution.py:73
  2.5 2.1 %collective-permute-start.2 = (bf16[24,48,256]{2,1,0:T(8,128)(2,1)}, bf16[24,48,256]{2,1,0:T(8,128)(2,1)S(1)}, u32[]{:S(2)}, u32[]{:S(2)}) collective-permute-start(bf16[24,48,256]{2,1,0:T(8,128)(2,1)} %shard_map.130.refs_0_), channel_id=1, source_target_pairs={{0,4},{1,5},{2,6},{3,7},{4,0},{5,1},{6,2},{7,3},{8,12},{9,13},{10,... | collective-permute-start | bytes 1769480 | tf_op jit(solution)/shard_map/ppermute | solution.py:57
  4.6 2.7 %collective-permute-start.1 = (bf16[24,48,256]{2,1,0:T(8,128)(2,1)}, bf16[24,48,256]{2,1,0:T(8,128)(2,1)S(1)}, u32[]{:S(2)}, u32[]{:S(2)}) collective-permute-start(bf16[24,48,256]{2,1,0:T(8,128)(2,1)} %shard_map.130.refs_0_), channel_id=1, source_target_pairs={{0,3},{1,0},{2,1},{3,2},{4,7},{5,4},{6,5},{7,6},{8,11},{9,8},{10,9... | collective-permute-start | bytes 1769480 | tf_op jit(solution)/shard_map/ppermute | solution.py:53
  7.4 0.0 collective-permute-start
  7.4 2.4 %shard_map.131 = bf16[8,128,256]{2,1,0:T(8,128)(2,1)} custom-call(bf16[1,32,256]{2,1,0:T(8,128)(2,1)} %refs_0_.1, bf16[1,32,256]{2,1,0:T(8,128)(2,1)} %refs_1_.1, bf16[1,32,256]{2,1,0:T(8,128)(2,1)} %refs_2_.2, bf16[1,32,256]{2,1,0:T(8,128)(2,1)} %refs_3_.1), custom_call_target="tpu_custom_call" | custom-call | flops 67108864 | bytes 1048576 | tf_op jit(solution)/shard_map/pallas_call | solution.py:73
  9.8 4.0 %all-to-all-start = ((bf16[8,128,256]{2,1,0:T(8,128)(2,1)}), bf16[8,128,256]{2,1,0:T(8,128)(2,1)S(1)}, u32[]{:S(2)}, u32[]{:S(2)}) async-start(bf16[8,128,256]{2,1,0:T(8,128)(2,1)} %shard_map.131), calls=%async_computation | async-start | bytes 1048576 | tf_op jit(solution)/shard_map/all_to_all | solution.py:411
  13.8 1.1 %copy-done.2 = bf16[24,48,256]{2,1,0:T(8,128)(2,1)S(1)} copy-done((bf16[24,48,256]{2,1,0:T(8,128)(2,1)S(1)}, bf16[24,48,256]{2,1,0:T(8,128)(2,1)}, u32[]{:S(2)}) %copy-start.2) | copy-done | bytes 589848
  14.9 0.9 %copy-done.3 = bf16[1,256,512]{2,1,0:T(8,128)(2,1)S(1)} copy-done((bf16[1,256,512]{2,1,0:T(8,128)(2,1)S(1)}, bf16[1,256,512]{2,1,0:T(8,128)(2,1)}, u32[]{:S(2)}) %copy-start.3) | copy-done | bytes 262168
  15.8 0.7 copy-done.6
  16.5 0.2 shard_map.132
  16.7 10.6 %all-to-all-done.rows = bf16[8,128,256]{2,1,0:T(8,128)(2,1)S(1)} async-done(((bf16[8,128,256]{2,1,0:T(8,128)(2,1)}), bf16[8,128,256]{2,1,0:T(8,128)(2,1)S(1)}, u32[]{:S(2)}, u32[]{:S(2)}) %all-to-all-start) | async-done | bytes 524320 | tf_op jit(solution)/shard_map/all_to_all | solution.py:411
  27.3 0.0 collective-permute-done.2.refs_3_
  27.3 0.0 collective-permute-done.1.refs_2_
  27.3 0.0 collective-permute-done.refs_1_
  27.3 1.1 %collective-permute-start.5 = (bf16[24,48,256]{2,1,0:T(8,128)(2,1)S(1)}, bf16[24,48,256]{2,1,0:T(8,128)(2,1)S(1)}, u32[]{:S(2)}, u32[]{:S(2)}) collective-permute-start(bf16[24,48,256]{2,1,0:T(8,128)(2,1)S(1)} %collective-permute-done.2.refs_3_), channel_id=1, source_target_pairs={{0,3},{1,0},{2,1},{3,2},{4,7},{5,4},{6,5},{7,6},{8,11},{9,8},{10,9... | collective-permute-start | bytes 1769480 | tf_op jit(solution)/shard_map/ppermute | solution.py:53
  28.4 0.3 collective-permute-start.4
  28.6 0.6 collective-permute-start.3
  29.3 2.8 %copy-done = bf16[24,256,512]{2,1,0:T(8,128)(2,1)S(1)} copy-done((bf16[24,256,512]{2,1,0:T(8,128)(2,1)S(1)}, bf16[24,256,512]{2,1,0:T(8,128)(2,1)}, u32[]{:S(2)}) %copy-start) | copy-done | bytes 6291480
  32.0 0.3 shard_map.134
  32.4 3.6 %collective-permute-start.8 = (bf16[3,256,256]{2,1,0:T(8,128)(2,1)S(1)}, bf16[3,256,256]{2,1,0:T(8,128)(2,1)S(1)}, u32[]{:S(2)}, u32[]{:S(2)}) collective-permute-start(bf16[3,256,256]{2,1,0:T(8,128)(2,1)S(1)} %get-tuple-element.83), channel_id=1, source_target_pairs={{0,8},{8,0},{16,24},{24,16},{32,40},{40,32},{48,56},{56,48},{64,72... | collective-permute-start | bytes 1179656 | tf_op jit(solution)/shard_map/ppermute | solution.py:61
  36.0 1.3 %collective-permute-done.8.got = bf16[3,256,256]{2,1,0:T(8,128)(2,1)S(1)} collective-permute-done((bf16[3,256,256]{2,1,0:T(8,128)(2,1)S(1)}, bf16[3,256,256]{2,1,0:T(8,128)(2,1)S(1)}, u32[]{:S(2)}, u32[]{:S(2)}) %collective-permute-start.8) | collective-permute-done | bytes 393248 | tf_op jit(solution)/shard_map/ppermute | solution.py:61
  37.3 0.1 shard_map.136
  37.4 3.8 %collective-permute-start.12 = (bf16[2,256,256]{2,1,0:T(8,128)(2,1)S(1)}, bf16[2,256,256]{2,1,0:T(8,128)(2,1)S(1)}, u32[]{:S(2)}, u32[]{:S(2)}) collective-permute-start(bf16[2,256,256]{2,1,0:T(8,128)(2,1)S(1)} %get-tuple-element.87), channel_id=1, source_target_pairs={{0,48},{8,56},{16,0},{24,8},{32,16},{40,24},{48,32},{56,40},{64,11... | collective-permute-start | bytes 786440 | tf_op jit(solution)/shard_map/ppermute | solution.py:61
  41.2 0.0 collective-permute-start.11
  41.2 0.0 collective-permute-done.5.refs_6_
  41.2 0.7 collective-permute-start.10
  41.9 0.0 collective-permute-done.4.refs_5_
  41.9 0.3 collective-permute-done.3.refs_4_
  42.3 0.0 copy-start.4
  42.3 2.0 %collective-permute-start.7 = (bf16[12,48,256]{2,1,0:T(8,128)(2,1)S(1)}, bf16[12,48,256]{2,1,0:T(8,128)(2,1)S(1)}, u32[]{:S(2)}, u32[]{:S(2)}) collective-permute-start(bf16[12,48,256]{2,1,0:T(8,128)(2,1)S(1)} %slice.7), channel_id=1, source_target_pairs={{0,3},{1,0},{2,1},{3,2},{4,7},{5,4},{6,5},{7,6},{8,11},{9,8},{10,9... | collective-permute-start | bytes 884744 | tf_op jit(solution)/shard_map/ppermute | solution.py:53
  44.3 0.0 collective-permute-start.6
  44.3 7.8 %collective-permute-done.12.refs_2_ = bf16[2,256,256]{2,1,0:T(8,128)(2,1)S(1)} collective-permute-done((bf16[2,256,256]{2,1,0:T(8,128)(2,1)S(1)}, bf16[2,256,256]{2,1,0:T(8,128)(2,1)S(1)}, u32[]{:S(2)}, u32[]{:S(2)}) %collective-permute-start.12) | collective-permute-done | bytes 262176 | tf_op jit(solution)/shard_map/ppermute | solution.py:61
  52.2 1.2 %collective-permute-start.15 = (bf16[2,256,256]{2,1,0:T(8,128)(2,1)S(1)}, bf16[2,256,256]{2,1,0:T(8,128)(2,1)S(1)}, u32[]{:S(2)}, u32[]{:S(2)}) collective-permute-start(bf16[2,256,256]{2,1,0:T(8,128)(2,1)S(1)} %collective-permute-done.12.refs_2_), channel_id=1, source_target_pairs={{0,8},{8,0},{16,24},{24,16},{32,40},{40,32},{48,56},{56,48},{64,72... | collective-permute-start | bytes 786440 | tf_op jit(solution)/shard_map/ppermute | solution.py:61
  53.4 0.0 collective-permute-done.11.refs_1_
  53.4 0.0 collective-permute-start.14
  53.4 2.6 %collective-permute-done.10.refs_0_ = bf16[2,256,256]{2,1,0:T(8,128)(2,1)S(1)} collective-permute-done((bf16[2,256,256]{2,1,0:T(8,128)(2,1)S(1)}, bf16[2,256,256]{2,1,0:T(8,128)(2,1)S(1)}, u32[]{:S(2)}, u32[]{:S(2)}) %collective-permute-start.10) | collective-permute-done | bytes 262176 | tf_op jit(solution)/shard_map/ppermute | solution.py:61
  55.9 0.8 collective-permute-start.13
  56.8 0.0 collective-permute-done.7.refs_8_
  56.8 3.3 %shard_map.133 = (bf16[24,256,256]{2,1,0:T(8,128)(2,1)S(1)}, bf16[24,256,256]{2,1,0:T(8,128)(2,1)S(1)}, f32[256,512]{1,0:T(8,128)S(1)}) custom-call(bf16[24,48,256]{2,1,0:T(8,128)(2,1)S(1)} %get-tuple-element.68.refs_0_, bf16[24,48,256]{2,1,0:T(8,128)(2,1)S(1)} %collective-permute-done.refs_1_, bf16[24,48,256]{2,1,0:T(8,128)(2,1)S(1)} %collective-permute-done.1.refs_2_, ...), custom_call_target="tpu_custom_call" | custom-call | flops 1048576 | bytes 16777216 | tf_op jit(solution)/shard_map/pallas_call | solution.py:73
  60.1 0.3 shard_map.135
  60.4 0.1 collective-permute-start.9
  60.5 0.0 collective-permute-done.15.refs_5_
  60.5 0.0 collective-permute-done.14.refs_4_
  60.5 1.3 %collective-permute-done.9.theirs = bf16[256,256]{1,0:T(8,128)(2,1)S(1)} collective-permute-done((bf16[256,256]{1,0:T(8,128)(2,1)S(1)}, bf16[256,256]{1,0:T(8,128)(2,1)S(1)}, u32[]{:S(2)}, u32[]{:S(2)}) %collective-permute-start.9) | collective-permute-done | bytes 131104 | tf_op jit(solution)/shard_map/ppermute | solution.py:61
  61.9 2.8 %collective-permute-start.20 = (bf16[3,256,256]{2,1,0:T(8,128)(2,1)S(1)}, bf16[3,256,256]{2,1,0:T(8,128)(2,1)S(1)}, u32[]{:S(2)}, u32[]{:S(2)}) collective-permute-start(bf16[3,256,256]{2,1,0:T(8,128)(2,1)S(1)} %shard_map.142.top), channel_id=1, source_target_pairs={{0,64},{8,72},{16,80},{24,88},{32,96},{40,104},{48,112},{56,120},{... | collective-permute-start | bytes 1179656 | tf_op jit(solution)/shard_map/ppermute | solution.py:61
  64.7 0.2 shard_map.137
  64.9 0.7 collective-permute-start.18
  65.6 0.9 %collective-permute-start.17 = (bf16[256,256]{1,0:T(8,128)(2,1)S(1)}, bf16[256,256]{1,0:T(8,128)(2,1)S(1)}, u32[]{:S(2)}, u32[]{:S(2)}) collective-permute-start(bf16[256,256]{1,0:T(8,128)(2,1)S(1)} %get-tuple-element.98.refs_6_), channel_id=1, source_target_pairs={{0,32},{8,40},{16,48},{24,56},{32,0},{40,8},{48,16},{56,24},{64,96... | collective-permute-start | bytes 393224 | tf_op jit(solution)/shard_map/ppermute | solution.py:61
  66.6 0.7 collective-permute-start.16
  67.3 1.0 %shard_map.139 = (bf16[8,256,512]{2,1,0:T(8,128)(2,1)S(1)}, bf16[8,256,256]{2,1,0:T(8,128)(2,1)S(1)}) custom-call(bf16[24,256,256]{2,1,0:T(8,128)(2,1)S(1)} %get-tuple-element.113.inv, bf16[24,256,256]{2,1,0:T(8,128)(2,1)S(1)} %get-tuple-element.99.m, bf16[24,256,512]{2,1,0:T(8,128)(2,1)S(1)} %copy-done.1), custom_call_target="tpu_custom_call" | custom-call | flops 1073741824 | bytes 1048576 | tf_op jit(solution)/shard_map/pallas_call | solution.py:73
  68.3 1.0 %shard_map.138 = (bf16[8,256,512]{2,1,0:T(8,128)(2,1)S(1)}, bf16[8,256,256]{2,1,0:T(8,128)(2,1)S(1)}) custom-call(bf16[24,256,256]{2,1,0:T(8,128)(2,1)S(1)} %get-tuple-element.113.inv, bf16[24,256,256]{2,1,0:T(8,128)(2,1)S(1)} %get-tuple-element.99.m, bf16[24,256,512]{2,1,0:T(8,128)(2,1)S(1)} %copy-done.1), custom_call_target="tpu_custom_call" | custom-call | flops 1073741824 | bytes 1048576 | tf_op jit(solution)/shard_map/pallas_call | solution.py:73
  69.4 0.2 collective-permute-done.18.refs_9_
  69.6 1.8 %collective-permute-done.17.refs_8_ = bf16[256,256]{1,0:T(8,128)(2,1)S(1)} collective-permute-done((bf16[256,256]{1,0:T(8,128)(2,1)S(1)}, bf16[256,256]{1,0:T(8,128)(2,1)S(1)}, u32[]{:S(2)}, u32[]{:S(2)}) %collective-permute-start.17) | collective-permute-done | bytes 131104 | tf_op jit(solution)/shard_map/ppermute | solution.py:61
  71.4 3.6 %collective-permute-done.16.refs_7_ = bf16[256,256]{1,0:T(8,128)(2,1)S(1)} collective-permute-done((bf16[256,256]{1,0:T(8,128)(2,1)S(1)}, bf16[256,256]{1,0:T(8,128)(2,1)S(1)}, u32[]{:S(2)}, u32[]{:S(2)}) %collective-permute-start.16) | collective-permute-done | bytes 131104 | tf_op jit(solution)/shard_map/ppermute | solution.py:61
  75.0 0.5 shard_map.140
  75.5 0.0 copy-start.5
  75.6 0.2 collective-permute-start.19
  75.7 1.0 %shard_map.141 = (bf16[8,256,512]{2,1,0:T(8,128)(2,1)S(1)}, bf16[8,256,256]{2,1,0:T(8,128)(2,1)S(1)}) custom-call(bf16[24,256,256]{2,1,0:T(8,128)(2,1)S(1)} %get-tuple-element.113.inv, bf16[24,256,256]{2,1,0:T(8,128)(2,1)S(1)} %get-tuple-element.99.m, bf16[24,256,512]{2,1,0:T(8,128)(2,1)S(1)} %copy-done.1), custom_call_target="tpu_custom_call" | custom-call | flops 1073741824 | bytes 1048576 | tf_op jit(solution)/shard_map/pallas_call | solution.py:73
  76.8 4.6 %collective-permute-done.19.theirs = bf16[256,256]{1,0:T(8,128)(2,1)S(1)} collective-permute-done((bf16[256,256]{1,0:T(8,128)(2,1)S(1)}, bf16[256,256]{1,0:T(8,128)(2,1)S(1)}, u32[]{:S(2)}, u32[]{:S(2)}) %collective-permute-start.19) | collective-permute-done | bytes 131104 | tf_op jit(solution)/shard_map/ppermute | solution.py:61
  81.3 0.0 collective-permute-done.20.far
  81.3 1.2 %shard_map.143.own = bf16[2,256,256]{2,1,0:T(8,128)(2,1)S(1)} custom-call(bf16[256,256]{1,0:T(8,128)(2,1)S(1)} %get-tuple-element.108.mine, bf16[256,256]{1,0:T(8,128)(2,1)S(1)} %collective-permute-done.19.theirs, bf16[3,256,256]{2,1,0:T(8,128)(2,1)S(1)} %shard_map.142.top, bf16[3,256,256]{2,1,0:T(8,128)(2,1)S(1)} %collective-permute-done.20.far, ...), custom_call_target="tpu_custom_call" | custom-call | flops 67108864 | bytes 1048576 | tf_op jit(solution)/shard_map/pallas_call | solution.py:73
  82.6 1.8 %collective-permute-start.21 = (bf16[2,256,256]{2,1,0:T(8,128)(2,1)S(1)}, bf16[2,256,256]{2,1,0:T(8,128)(2,1)S(1)}, u32[]{:S(2)}, u32[]{:S(2)}) collective-permute-start(bf16[2,256,256]{2,1,0:T(8,128)(2,1)S(1)} %shard_map.143.own), channel_id=1, source_target_pairs={{0,8},{8,0},{16,24},{24,16},{32,40},{40,32},{48,56},{56,48},{64,72... | collective-permute-start | bytes 786440 | tf_op jit(solution)/shard_map/ppermute | solution.py:61
  84.4 1.2 %collective-permute-done.21.got = bf16[2,256,256]{2,1,0:T(8,128)(2,1)S(1)} collective-permute-done((bf16[2,256,256]{2,1,0:T(8,128)(2,1)S(1)}, bf16[2,256,256]{2,1,0:T(8,128)(2,1)S(1)}, u32[]{:S(2)}, u32[]{:S(2)}) %collective-permute-start.21) | collective-permute-done | bytes 262176 | tf_op jit(solution)/shard_map/ppermute | solution.py:61
  85.5 3.5 %shard_map.144 = (bf16[24,256,512]{2,1,0:T(8,128)(2,1)}, bf16[1,256,512]{2,1,0:T(8,128)(2,1)}, bf16[1,256,512]{2,1,0:T(8,128)(2,1)}) custom-call(bf16[256,512]{1,0:T(8,128)(2,1)S(1)} %get-tuple-element.80.r, bf16[2,256,256]{2,1,0:T(8,128)(2,1)S(1)} %get-tuple-element.79.mats, bf16[2,256,256]{2,1,0:T(8,128)(2,1)S(1)} %shard_map.143.own, ...), custom_call_target="tpu_custom_call" | custom-call | flops 2147483648 | bytes 16777216 | tf_op jit(solution)/shard_map/pallas_call | solution.py:73
  (13 shorter events, 0.1 us)
Async XLA Ops:
  2.5 24.8 %collective-permute-start.2 = (bf16[24,48,256]{2,1,0:T(8,128)(2,1)}, bf16[24,48,256]{2,1,0:T(8,128)(2,1)S(1)}, u32[]{:S(2)}, u32[]{:S(2)}) collective-permute-start(bf16[24,48,256]{2,1,0:T(8,128)(2,1)} %shard_map.130.refs_0_), channel_id=1, source_target_pairs={{0,4},{1,5},{2,6},{3,7},{4,0},{5,1},{6,2},{7,3},{8,12},{9,13},{10,... | collective-permute-start | bytes 1769480 | tf_op jit(solution)/shard_map/ppermute | solution.py:57
  4.6 22.7 %collective-permute-start.1 = (bf16[24,48,256]{2,1,0:T(8,128)(2,1)}, bf16[24,48,256]{2,1,0:T(8,128)(2,1)S(1)}, u32[]{:S(2)}, u32[]{:S(2)}) collective-permute-start(bf16[24,48,256]{2,1,0:T(8,128)(2,1)} %shard_map.130.refs_0_), channel_id=1, source_target_pairs={{0,3},{1,0},{2,1},{3,2},{4,7},{5,4},{6,5},{7,6},{8,11},{9,8},{10,9... | collective-permute-start | bytes 1769480 | tf_op jit(solution)/shard_map/ppermute | solution.py:53
  7.4 19.9 %collective-permute-start = (bf16[24,48,256]{2,1,0:T(8,128)(2,1)}, bf16[24,48,256]{2,1,0:T(8,128)(2,1)S(1)}, u32[]{:S(2)}, u32[]{:S(2)}) collective-permute-start(bf16[24,48,256]{2,1,0:T(8,128)(2,1)} %shard_map.130.refs_0_), channel_id=1, source_target_pairs={{0,1},{1,2},{2,3},{3,0},{4,5},{5,6},{6,7},{7,4},{8,9},{9,10},{10,1... | collective-permute-start | bytes 1769480 | tf_op jit(solution)/shard_map/ppermute | solution.py:49
  9.8 17.5 %all-to-all-start = ((bf16[8,128,256]{2,1,0:T(8,128)(2,1)}), bf16[8,128,256]{2,1,0:T(8,128)(2,1)S(1)}, u32[]{:S(2)}, u32[]{:S(2)}) async-start(bf16[8,128,256]{2,1,0:T(8,128)(2,1)} %shard_map.131), calls=%async_computation | async-start | bytes 1048576 | tf_op jit(solution)/shard_map/all_to_all | solution.py:411
  13.8 1.1 %copy-start.2 = (bf16[24,48,256]{2,1,0:T(8,128)(2,1)S(1)}, bf16[24,48,256]{2,1,0:T(8,128)(2,1)}, u32[]{:S(2)}) copy-start(bf16[24,48,256]{2,1,0:T(8,128)(2,1)} %shard_map.130.refs_0_) | copy-start | bytes 1769476
  14.9 0.9 %copy-start.3 = (bf16[1,256,512]{2,1,0:T(8,128)(2,1)S(1)}, bf16[1,256,512]{2,1,0:T(8,128)(2,1)}, u32[]{:S(2)}) copy-start(bf16[1,256,512]{2,1,0:T(8,128)(2,1)} %refs_2_.3) | copy-start | bytes 786436
  15.8 0.7 copy-start.6
  27.3 13.9 %collective-permute-start.5 = (bf16[24,48,256]{2,1,0:T(8,128)(2,1)S(1)}, bf16[24,48,256]{2,1,0:T(8,128)(2,1)S(1)}, u32[]{:S(2)}, u32[]{:S(2)}) collective-permute-start(bf16[24,48,256]{2,1,0:T(8,128)(2,1)S(1)} %collective-permute-done.2.refs_3_), channel_id=1, source_target_pairs={{0,3},{1,0},{2,1},{3,2},{4,7},{5,4},{6,5},{7,6},{8,11},{9,8},{10,9... | collective-permute-start | bytes 1769480 | tf_op jit(solution)/shard_map/ppermute | solution.py:53
  28.4 13.6 %collective-permute-start.4 = (bf16[24,48,256]{2,1,0:T(8,128)(2,1)S(1)}, bf16[24,48,256]{2,1,0:T(8,128)(2,1)S(1)}, u32[]{:S(2)}, u32[]{:S(2)}) collective-permute-start(bf16[24,48,256]{2,1,0:T(8,128)(2,1)S(1)} %collective-permute-done.refs_1_), channel_id=1, source_target_pairs={{0,4},{1,5},{2,6},{3,7},{4,0},{5,1},{6,2},{7,3},{8,12},{9,13},{10,... | collective-permute-start | bytes 1769480 | tf_op jit(solution)/shard_map/ppermute | solution.py:57
  28.6 13.6 %collective-permute-start.3 = (bf16[24,48,256]{2,1,0:T(8,128)(2,1)S(1)}, bf16[24,48,256]{2,1,0:T(8,128)(2,1)S(1)}, u32[]{:S(2)}, u32[]{:S(2)}) collective-permute-start(bf16[24,48,256]{2,1,0:T(8,128)(2,1)S(1)} %collective-permute-done.refs_1_), channel_id=1, source_target_pairs={{0,1},{1,2},{2,3},{3,0},{4,5},{5,6},{6,7},{7,4},{8,9},{9,10},{10,1... | collective-permute-start | bytes 1769480 | tf_op jit(solution)/shard_map/ppermute | solution.py:49
  29.3 2.8 %copy-start = (bf16[24,256,512]{2,1,0:T(8,128)(2,1)S(1)}, bf16[24,256,512]{2,1,0:T(8,128)(2,1)}, u32[]{:S(2)}) copy-start(bf16[24,256,512]{2,1,0:T(8,128)(2,1)} %rhs.7) | copy-start | bytes 18874372
  32.0 24.8 %copy-start.1 = (bf16[24,256,512]{2,1,0:T(8,128)(2,1)S(1)}, bf16[24,256,512]{2,1,0:T(8,128)(2,1)}, u32[]{:S(2)}) copy-start(bf16[24,256,512]{2,1,0:T(8,128)(2,1)} %rhs.7) | copy-start | bytes 18874372
  32.4 5.0 %collective-permute-start.8 = (bf16[3,256,256]{2,1,0:T(8,128)(2,1)S(1)}, bf16[3,256,256]{2,1,0:T(8,128)(2,1)S(1)}, u32[]{:S(2)}, u32[]{:S(2)}) collective-permute-start(bf16[3,256,256]{2,1,0:T(8,128)(2,1)S(1)} %get-tuple-element.83), channel_id=1, source_target_pairs={{0,8},{8,0},{16,24},{24,16},{32,40},{40,32},{48,56},{56,48},{64,72... | collective-permute-start | bytes 1179656 | tf_op jit(solution)/shard_map/ppermute | solution.py:61
  37.4 14.8 %collective-permute-start.12 = (bf16[2,256,256]{2,1,0:T(8,128)(2,1)S(1)}, bf16[2,256,256]{2,1,0:T(8,128)(2,1)S(1)}, u32[]{:S(2)}, u32[]{:S(2)}) collective-permute-start(bf16[2,256,256]{2,1,0:T(8,128)(2,1)S(1)} %get-tuple-element.87), channel_id=1, source_target_pairs={{0,48},{8,56},{16,0},{24,8},{32,16},{40,24},{48,32},{56,40},{64,11... | collective-permute-start | bytes 786440 | tf_op jit(solution)/shard_map/ppermute | solution.py:61
  41.2 12.1 %collective-permute-start.11 = (bf16[2,256,256]{2,1,0:T(8,128)(2,1)S(1)}, bf16[2,256,256]{2,1,0:T(8,128)(2,1)S(1)}, u32[]{:S(2)}, u32[]{:S(2)}) collective-permute-start(bf16[2,256,256]{2,1,0:T(8,128)(2,1)S(1)} %get-tuple-element.87), channel_id=1, source_target_pairs={{0,32},{8,40},{16,48},{24,56},{32,0},{40,8},{48,16},{56,24},{64,96... | collective-permute-start | bytes 786440 | tf_op jit(solution)/shard_map/ppermute | solution.py:61
  41.2 14.7 %collective-permute-start.10 = (bf16[2,256,256]{2,1,0:T(8,128)(2,1)S(1)}, bf16[2,256,256]{2,1,0:T(8,128)(2,1)S(1)}, u32[]{:S(2)}, u32[]{:S(2)}) collective-permute-start(bf16[2,256,256]{2,1,0:T(8,128)(2,1)S(1)} %get-tuple-element.87), channel_id=1, source_target_pairs={{0,16},{8,24},{16,32},{24,40},{32,48},{40,56},{48,0},{56,8},{64,80... | collective-permute-start | bytes 786440 | tf_op jit(solution)/shard_map/ppermute | solution.py:61
  42.3 17.8 %copy-start.4 = (bf16[1,256,512]{2,1,0:T(8,128)(2,1)S(1)}, bf16[1,256,512]{2,1,0:T(8,128)(2,1)}, u32[]{:S(2)}) copy-start(bf16[1,256,512]{2,1,0:T(8,128)(2,1)} %rhs.4) | copy-start | bytes 786436
  42.3 14.5 %collective-permute-start.7 = (bf16[12,48,256]{2,1,0:T(8,128)(2,1)S(1)}, bf16[12,48,256]{2,1,0:T(8,128)(2,1)S(1)}, u32[]{:S(2)}, u32[]{:S(2)}) collective-permute-start(bf16[12,48,256]{2,1,0:T(8,128)(2,1)S(1)} %slice.7), channel_id=1, source_target_pairs={{0,3},{1,0},{2,1},{3,2},{4,7},{5,4},{6,5},{7,6},{8,11},{9,8},{10,9... | collective-permute-start | bytes 884744 | tf_op jit(solution)/shard_map/ppermute | solution.py:53
  44.3 12.5 %collective-permute-start.6 = (bf16[12,48,256]{2,1,0:T(8,128)(2,1)S(1)}, bf16[12,48,256]{2,1,0:T(8,128)(2,1)S(1)}, u32[]{:S(2)}, u32[]{:S(2)}) collective-permute-start(bf16[12,48,256]{2,1,0:T(8,128)(2,1)S(1)} %slice.6), channel_id=1, source_target_pairs={{0,1},{1,2},{2,3},{3,0},{4,5},{5,6},{6,7},{7,4},{8,9},{9,10},{10,1... | collective-permute-start | bytes 884744 | tf_op jit(solution)/shard_map/ppermute | solution.py:49
  52.2 8.3 %collective-permute-start.15 = (bf16[2,256,256]{2,1,0:T(8,128)(2,1)S(1)}, bf16[2,256,256]{2,1,0:T(8,128)(2,1)S(1)}, u32[]{:S(2)}, u32[]{:S(2)}) collective-permute-start(bf16[2,256,256]{2,1,0:T(8,128)(2,1)S(1)} %collective-permute-done.12.refs_2_), channel_id=1, source_target_pairs={{0,8},{8,0},{16,24},{24,16},{32,40},{40,32},{48,56},{56,48},{64,72... | collective-permute-start | bytes 786440 | tf_op jit(solution)/shard_map/ppermute | solution.py:61
  53.4 7.1 %collective-permute-start.14 = (bf16[2,256,256]{2,1,0:T(8,128)(2,1)S(1)}, bf16[2,256,256]{2,1,0:T(8,128)(2,1)S(1)}, u32[]{:S(2)}, u32[]{:S(2)}) collective-permute-start(bf16[2,256,256]{2,1,0:T(8,128)(2,1)S(1)} %collective-permute-done.11.refs_1_), channel_id=1, source_target_pairs={{0,8},{8,0},{16,24},{24,16},{32,40},{40,32},{48,56},{56,48},{64,72... | collective-permute-start | bytes 786440 | tf_op jit(solution)/shard_map/ppermute | solution.py:61
  55.9 4.6 %collective-permute-start.13 = (bf16[2,256,256]{2,1,0:T(8,128)(2,1)S(1)}, bf16[2,256,256]{2,1,0:T(8,128)(2,1)S(1)}, u32[]{:S(2)}, u32[]{:S(2)}) collective-permute-start(bf16[2,256,256]{2,1,0:T(8,128)(2,1)S(1)} %collective-permute-done.10.refs_0_), channel_id=1, source_target_pairs={{0,8},{8,0},{16,24},{24,16},{32,40},{40,32},{48,56},{56,48},{64,72... | collective-permute-start | bytes 786440 | tf_op jit(solution)/shard_map/ppermute | solution.py:61
  60.4 1.4 %collective-permute-start.9 = (bf16[256,256]{1,0:T(8,128)(2,1)S(1)}, bf16[256,256]{1,0:T(8,128)(2,1)S(1)}, u32[]{:S(2)}, u32[]{:S(2)}) collective-permute-start(bf16[256,256]{1,0:T(8,128)(2,1)S(1)} %get-tuple-element.86), channel_id=1, source_target_pairs={{0,8},{8,0},{16,24},{24,16},{32,40},{40,32},{48,56},{56,48},{64,72... | collective-permute-start | bytes 393224 | tf_op jit(solution)/shard_map/ppermute | solution.py:61
  61.9 19.5 %collective-permute-start.20 = (bf16[3,256,256]{2,1,0:T(8,128)(2,1)S(1)}, bf16[3,256,256]{2,1,0:T(8,128)(2,1)S(1)}, u32[]{:S(2)}, u32[]{:S(2)}) collective-permute-start(bf16[3,256,256]{2,1,0:T(8,128)(2,1)S(1)} %shard_map.142.top), channel_id=1, source_target_pairs={{0,64},{8,72},{16,80},{24,88},{32,96},{40,104},{48,112},{56,120},{... | collective-permute-start | bytes 1179656 | tf_op jit(solution)/shard_map/ppermute | solution.py:61
  64.9 4.7 %collective-permute-start.18 = (bf16[256,256]{1,0:T(8,128)(2,1)S(1)}, bf16[256,256]{1,0:T(8,128)(2,1)S(1)}, u32[]{:S(2)}, u32[]{:S(2)}) collective-permute-start(bf16[256,256]{1,0:T(8,128)(2,1)S(1)} %get-tuple-element.98.refs_6_), channel_id=1, source_target_pairs={{0,48},{8,56},{16,0},{24,8},{32,16},{40,24},{48,32},{56,40},{64,11... | collective-permute-start | bytes 393224 | tf_op jit(solution)/shard_map/ppermute | solution.py:61
  65.6 5.8 %collective-permute-start.17 = (bf16[256,256]{1,0:T(8,128)(2,1)S(1)}, bf16[256,256]{1,0:T(8,128)(2,1)S(1)}, u32[]{:S(2)}, u32[]{:S(2)}) collective-permute-start(bf16[256,256]{1,0:T(8,128)(2,1)S(1)} %get-tuple-element.98.refs_6_), channel_id=1, source_target_pairs={{0,32},{8,40},{16,48},{24,56},{32,0},{40,8},{48,16},{56,24},{64,96... | collective-permute-start | bytes 393224 | tf_op jit(solution)/shard_map/ppermute | solution.py:61
  66.6 8.5 %collective-permute-start.16 = (bf16[256,256]{1,0:T(8,128)(2,1)S(1)}, bf16[256,256]{1,0:T(8,128)(2,1)S(1)}, u32[]{:S(2)}, u32[]{:S(2)}) collective-permute-start(bf16[256,256]{1,0:T(8,128)(2,1)S(1)} %get-tuple-element.98.refs_6_), channel_id=1, source_target_pairs={{0,16},{8,24},{16,32},{24,40},{32,48},{40,56},{48,0},{56,8},{64,80... | collective-permute-start | bytes 393224 | tf_op jit(solution)/shard_map/ppermute | solution.py:61
  75.5 5.8 %copy-start.5 = (bf16[256,512]{1,0:T(8,128)(2,1)S(1)}, bf16[256,512]{1,0:T(8,128)(2,1)}, u32[]{:S(2)}) copy-start(bf16[256,512]{1,0:T(8,128)(2,1)} %above.1) | copy-start | bytes 786436
  75.6 5.8 %collective-permute-start.19 = (bf16[256,256]{1,0:T(8,128)(2,1)S(1)}, bf16[256,256]{1,0:T(8,128)(2,1)S(1)}, u32[]{:S(2)}, u32[]{:S(2)}) collective-permute-start(bf16[256,256]{1,0:T(8,128)(2,1)S(1)} %get-tuple-element.108.mine), channel_id=1, source_target_pairs={{0,64},{8,72},{16,80},{24,88},{32,96},{40,104},{48,112},{56,120},{... | collective-permute-start | bytes 393224 | tf_op jit(solution)/shard_map/ppermute | solution.py:61
  82.6 2.9 %collective-permute-start.21 = (bf16[2,256,256]{2,1,0:T(8,128)(2,1)S(1)}, bf16[2,256,256]{2,1,0:T(8,128)(2,1)S(1)}, u32[]{:S(2)}, u32[]{:S(2)}) collective-permute-start(bf16[2,256,256]{2,1,0:T(8,128)(2,1)S(1)} %shard_map.143.own), channel_id=1, source_target_pairs={{0,8},{8,0},{16,24},{24,16},{32,40},{40,32},{48,56},{56,48},{64,72... | collective-permute-start | bytes 786440 | tf_op jit(solution)/shard_map/ppermute | solution.py:61

commit v5 on v4

--- a/solution.py
+++ b/solution.py
@@ -100,12 +100,9 @@
 
 
 def pack_small_kernel(*refs):
-    smalls, (out, sems) = refs[:4], refs[4:]
-    pairs = []
-    for n, ref in enumerate(smalls):
-        for to in range(8):
-            pairs.append((ref.at[0], out.at[to, pl.ds(32 * n, 32)]))
-    move(pairs, sems)
+    smalls, (out, held, sems) = refs[:4], refs[4:]
+    move([(ref.at[0], held.at[pl.ds(32 * n, 32)]) for n, ref in enumerate(smalls)], sems)
+    move([(held, out.at[n]) for n in range(8)], sems)
 
 
 def move(pairs, sems):
@@ -288,35 +285,21 @@
                 top[n] = value
 
 
-def top_kernel(mine, theirs, top, far, t0, t, r0, r, above, out, p3, p4):
+def top_kernel(mine, theirs, top, far, t0, t, r0, r, above, out):
     core, z, x_hi = leaf_place()
     above = above[:, pl.ds(pl.multiple_of(core * 256, 256), 256)]
-    for h, (a, b) in enumerate(((p3, p4), (p4, p3))):
+    for h, (p3, p4) in enumerate(((top, far), (far, top))):
 
         @pl.when(x_hi == h)
         def _():
-            a[...] = top[...]
-            b[...] = far[...]
-
-    r3 = sub(p3[2], f32sum(mine[...], theirs[...]))
-    r4 = sub(p4[2], mm(p3[0], r3).astype(BF).astype(F32))
-    x4 = (mm(p4[1], r4) - mmt(p4[0], above)).astype(BF)
-    x3 = (mm(p3[1], r3) - mmt(p3[0], x4)).astype(BF)
-    x2 = (mm(t[1, 1], r[1]) - mm(t[1, 0], x3)).astype(BF)
-    x1 = (mm(t[0, 1], r[0]) - mm(t[0, 0], x2)).astype(BF)
-    out[0] = (mm(t0[1], r0[...]) - mm(t0[0], x1)).astype(BF)
-
-    @pl.when(z % 2 == 0)
-    def _():
-        out[1] = x1
-
-    @pl.when(z == 1)
-    def _():
-        out[1] = x2
-
-    @pl.when(z == 3)
-    def _():
-        out[1] = jnp.where(x_hi == 0, x3, x4)
+            r3 = sub(p3[2], f32sum(mine[...], theirs[...]))
+            r4 = sub(p4[2], mm(p3[0], r3).astype(BF).astype(F32))
+            x4 = (mm(p4[1], r4) - mmt(p4[0], above)).astype(BF)
+            x3 = (mm(p3[1], r3) - mmt(p3[0], x4)).astype(BF)
+            x2 = (mm(t[1, 1], r[1]) - mm(t[1, 0], x3)).astype(BF)
+            x1 = (mm(t[0, 1], r[0]) - mm(t[0, 0], x2)).astype(BF)
+            out[0] = (mm(t0[1], r0[...]) - mm(t0[0], x1)).astype(BF)
+            out[1] = jnp.where(z % 2 == 0, x1, jnp.where(z == 1, x2, x4 if h else x3))
 
 
 PIECE = 2
@@ -404,7 +387,7 @@
         root_coupling,
         sep_inverse,
         sep_coupling,
-        scratch=[pltpu.SemaphoreType.DMA((32,))],
+        scratch=[pltpu.VMEM((128, 256), BF), pltpu.SemaphoreType.DMA((8,))],
         limit=56,
         in_specs=[ANY] * 4,
     )
@@ -444,7 +427,7 @@
         root_kernel, [(256, 512), (256, 256), (256, 256)], rhs_roots, total, root_mats
     )
     packs2 = [among(v, CORES) for v in packs]
-    theirs, packs, packs2 = lax.optimization_barrier((among(send, CORES), packs, packs2))
+    theirs, even, odd = lax.optimization_barrier((among(send, CORES), even, odd))
     (top,) = call(
         choose_kernel, [(3, 256, 256)], odd, *packs, *packs2
     )
@@ -485,7 +468,6 @@
         r0,
         r,
         above_solution,
-        scratch=[pltpu.VMEM((3, 256, 256), BF)] * 2,
     )
     return tuple(
         backward(

time: 89.7 us -> 89.6 us (level)
  no operation moved by 1% of the time
where the time goes in v5:
time: 89.6 us; the launch traced here: 89.2 us
  waiting for transfers between devices  35.5 us (40%)
  starting transfers between devices  30.2 us (34%)
  Pallas kernels  16.9 us (19%)
  local copies, waits for them, and re-layouts  5.56 us (6%)
  between operations  0.97 us (1%)
    ppermute x14, waiting for transfers between devices, among(): return lax.ppermute(v, 'leaf', pairs)  24.4 us
    ppermute x14, starting transfers between devices, among(): return lax.ppermute(v, 'leaf', pairs)  17.4 us
    pallas_call x15, Pallas kernels, call(): pl.pallas_call(kernel, in_specs=specs.get('in_specs', [VMEM] * len(args))...  16.9 us
    all_to_all x1, waiting for transfers between devices, local(): small = lax.all_to_all(small, 'load', 0, 0)  10.8 us
    ppermute x3, starting transfers between devices, down(): return lax.ppermute(v, 'load', y_shift(3))  5.82 us
    unnamed x14, local copies, waits for them, and re-layouts  5.52 us
    all_to_all x1, starting transfers between devices, local(): small = lax.all_to_all(small, 'load', 0, 0)  3.96 us
    ppermute x2, starting transfers between devices, across(): return lax.ppermute(v, 'load', X_LO)  2.37 us
  transfers between devices with their start and end apart: 23, of which 11 were waited for; matrix products, arithmetic and copies ran while one was open for 0% of the time, Pallas kernels for 12%

profile of v5, /device:TPU:1, one launch (start us, length us, event | category | flops | bytes accessed | tf_op | source)
XLA Modules:
  0.0 89.2 jit_solution(15751673184701149624)
XLA Ops:
  0.6 1.9 %shard_map.130.refs_0_ = bf16[24,48,256]{2,1,0:T(8,128)(2,1)} custom-call(bf16[24,32,256]{2,1,0:T(8,128)(2,1)} %inv.1, bf16[24,16,256]{2,1,0:T(8,128)(2,1)} %upd.1), custom_call_target="tpu_custom_call" | custom-call | flops 67108864 | bytes 1048576 | tf_op jit(solution)/shard_map/pallas_call | solution.py:73
  2.5 2.1 %collective-permute-start.2 = (bf16[24,48,256]{2,1,0:T(8,128)(2,1)}, bf16[24,48,256]{2,1,0:T(8,128)(2,1)S(1)}, u32[]{:S(2)}, u32[]{:S(2)}) collective-permute-start(bf16[24,48,256]{2,1,0:T(8,128)(2,1)} %shard_map.130.refs_0_), channel_id=1, source_target_pairs={{0,4},{1,5},{2,6},{3,7},{4,0},{5,1},{6,2},{7,3},{8,12},{9,13},{10,... | collective-permute-start | bytes 1769480 | tf_op jit(solution)/shard_map/ppermute | solution.py:57
  4.6 2.7 %collective-permute-start.1 = (bf16[24,48,256]{2,1,0:T(8,128)(2,1)}, bf16[24,48,256]{2,1,0:T(8,128)(2,1)S(1)}, u32[]{:S(2)}, u32[]{:S(2)}) collective-permute-start(bf16[24,48,256]{2,1,0:T(8,128)(2,1)} %shard_map.130.refs_0_), channel_id=1, source_target_pairs={{0,3},{1,0},{2,1},{3,2},{4,7},{5,4},{6,5},{7,6},{8,11},{9,8},{10,9... | collective-permute-start | bytes 1769480 | tf_op jit(solution)/shard_map/ppermute | solution.py:53
  7.4 0.0 collective-permute-start
  7.4 2.3 %shard_map.131 = bf16[8,128,256]{2,1,0:T(8,128)(2,1)} custom-call(bf16[1,32,256]{2,1,0:T(8,128)(2,1)} %refs_0_.1, bf16[1,32,256]{2,1,0:T(8,128)(2,1)} %refs_1_.1, bf16[1,32,256]{2,1,0:T(8,128)(2,1)} %refs_2_.2, bf16[1,32,256]{2,1,0:T(8,128)(2,1)} %refs_3_.1), custom_call_target="tpu_custom_call" | custom-call | flops 67108864 | bytes 1048576 | tf_op jit(solution)/shard_map/pallas_call | solution.py:73
  9.7 4.0 %all-to-all-start = ((bf16[8,128,256]{2,1,0:T(8,128)(2,1)}), bf16[8,128,256]{2,1,0:T(8,128)(2,1)S(1)}, u32[]{:S(2)}, u32[]{:S(2)}) async-start(bf16[8,128,256]{2,1,0:T(8,128)(2,1)} %shard_map.131), calls=%async_computation | async-start | bytes 1048576 | tf_op jit(solution)/shard_map/all_to_all | solution.py:394
  13.6 1.1 %copy-done.2 = bf16[24,48,256]{2,1,0:T(8,128)(2,1)S(1)} copy-done((bf16[24,48,256]{2,1,0:T(8,128)(2,1)S(1)}, bf16[24,48,256]{2,1,0:T(8,128)(2,1)}, u32[]{:S(2)}) %copy-start.2) | copy-done | bytes 589848
  14.7 0.9 %copy-done.3 = bf16[1,256,512]{2,1,0:T(8,128)(2,1)S(1)} copy-done((bf16[1,256,512]{2,1,0:T(8,128)(2,1)S(1)}, bf16[1,256,512]{2,1,0:T(8,128)(2,1)}, u32[]{:S(2)}) %copy-start.3) | copy-done | bytes 262168
  15.6 0.7 copy-done.6
  16.3 0.2 shard_map.132
  16.5 10.8 %all-to-all-done.rows = bf16[8,128,256]{2,1,0:T(8,128)(2,1)S(1)} async-done(((bf16[8,128,256]{2,1,0:T(8,128)(2,1)}), bf16[8,128,256]{2,1,0:T(8,128)(2,1)S(1)}, u32[]{:S(2)}, u32[]{:S(2)}) %all-to-all-start) | async-done | bytes 524320 | tf_op jit(solution)/shard_map/all_to_all | solution.py:394
  27.3 0.0 collective-permute-done.2.refs_3_
  27.3 0.0 collective-permute-done.1.refs_2_
  27.3 0.0 collective-permute-done.refs_1_
  27.3 1.1 %collective-permute-start.5 = (bf16[24,48,256]{2,1,0:T(8,128)(2,1)S(1)}, bf16[24,48,256]{2,1,0:T(8,128)(2,1)S(1)}, u32[]{:S(2)}, u32[]{:S(2)}) collective-permute-start(bf16[24,48,256]{2,1,0:T(8,128)(2,1)S(1)} %collective-permute-done.2.refs_3_), channel_id=1, source_target_pairs={{0,3},{1,0},{2,1},{3,2},{4,7},{5,4},{6,5},{7,6},{8,11},{9,8},{10,9... | collective-permute-start | bytes 1769480 | tf_op jit(solution)/shard_map/ppermute | solution.py:53
  28.4 0.3 collective-permute-start.4
  28.6 0.6 collective-permute-start.3
  29.3 2.8 %copy-done = bf16[24,256,512]{2,1,0:T(8,128)(2,1)S(1)} copy-done((bf16[24,256,512]{2,1,0:T(8,128)(2,1)S(1)}, bf16[24,256,512]{2,1,0:T(8,128)(2,1)}, u32[]{:S(2)}) %copy-start) | copy-done | bytes 6291480
  32.0 0.3 shard_map.134
  32.4 3.6 %collective-permute-start.9 = (bf16[3,256,256]{2,1,0:T(8,128)(2,1)S(1)}, bf16[3,256,256]{2,1,0:T(8,128)(2,1)S(1)}, u32[]{:S(2)}, u32[]{:S(2)}) collective-permute-start(bf16[3,256,256]{2,1,0:T(8,128)(2,1)S(1)} %get-tuple-element.80), channel_id=1, source_target_pairs={{0,8},{8,0},{16,24},{24,16},{32,40},{40,32},{48,56},{56,48},{64,72... | collective-permute-start | bytes 1179656 | tf_op jit(solution)/shard_map/ppermute | solution.py:61
  36.0 1.3 %collective-permute-done.9.got = bf16[3,256,256]{2,1,0:T(8,128)(2,1)S(1)} collective-permute-done((bf16[3,256,256]{2,1,0:T(8,128)(2,1)S(1)}, bf16[3,256,256]{2,1,0:T(8,128)(2,1)S(1)}, u32[]{:S(2)}, u32[]{:S(2)}) %collective-permute-start.9) | collective-permute-done | bytes 393248 | tf_op jit(solution)/shard_map/ppermute | solution.py:61
  37.3 0.1 shard_map.136
  37.4 3.8 %collective-permute-start.12 = (bf16[2,256,256]{2,1,0:T(8,128)(2,1)S(1)}, bf16[2,256,256]{2,1,0:T(8,128)(2,1)S(1)}, u32[]{:S(2)}, u32[]{:S(2)}) collective-permute-start(bf16[2,256,256]{2,1,0:T(8,128)(2,1)S(1)} %get-tuple-element.89), channel_id=1, source_target_pairs={{0,48},{8,56},{16,0},{24,8},{32,16},{40,24},{48,32},{56,40},{64,11... | collective-permute-start | bytes 786440 | tf_op jit(solution)/shard_map/ppermute | solution.py:61
  41.2 0.0 collective-permute-start.11
  41.2 0.0 collective-permute-done.5.refs_6_
  41.2 0.7 collective-permute-start.10
  41.9 0.0 collective-permute-done.4.refs_5_
  41.9 0.3 collective-permute-done.3.refs_4_
  42.3 0.0 copy-start.4
  42.3 2.0 %collective-permute-start.7 = (bf16[12,48,256]{2,1,0:T(8,128)(2,1)S(1)}, bf16[12,48,256]{2,1,0:T(8,128)(2,1)S(1)}, u32[]{:S(2)}, u32[]{:S(2)}) collective-permute-start(bf16[12,48,256]{2,1,0:T(8,128)(2,1)S(1)} %slice.7), channel_id=1, source_target_pairs={{0,3},{1,0},{2,1},{3,2},{4,7},{5,4},{6,5},{7,6},{8,11},{9,8},{10,9... | collective-permute-start | bytes 884744 | tf_op jit(solution)/shard_map/ppermute | solution.py:53
  44.3 7.8 %collective-permute-done.12.refs_2_ = bf16[2,256,256]{2,1,0:T(8,128)(2,1)S(1)} collective-permute-done((bf16[2,256,256]{2,1,0:T(8,128)(2,1)S(1)}, bf16[2,256,256]{2,1,0:T(8,128)(2,1)S(1)}, u32[]{:S(2)}, u32[]{:S(2)}) %collective-permute-start.12) | collective-permute-done | bytes 262176 | tf_op jit(solution)/shard_map/ppermute | solution.py:61
  52.2 1.2 %collective-permute-start.15 = (bf16[2,256,256]{2,1,0:T(8,128)(2,1)S(1)}, bf16[2,256,256]{2,1,0:T(8,128)(2,1)S(1)}, u32[]{:S(2)}, u32[]{:S(2)}) collective-permute-start(bf16[2,256,256]{2,1,0:T(8,128)(2,1)S(1)} %collective-permute-done.12.refs_2_), channel_id=1, source_target_pairs={{0,8},{8,0},{16,24},{24,16},{32,40},{40,32},{48,56},{56,48},{64,72... | collective-permute-start | bytes 786440 | tf_op jit(solution)/shard_map/ppermute | solution.py:61
  53.4 0.0 collective-permute-done.11.refs_1_
  53.4 0.0 collective-permute-start.14
  53.4 2.6 %collective-permute-done.10.refs_0_ = bf16[2,256,256]{2,1,0:T(8,128)(2,1)S(1)} collective-permute-done((bf16[2,256,256]{2,1,0:T(8,128)(2,1)S(1)}, bf16[2,256,256]{2,1,0:T(8,128)(2,1)S(1)}, u32[]{:S(2)}, u32[]{:S(2)}) %collective-permute-start.10) | collective-permute-done | bytes 262176 | tf_op jit(solution)/shard_map/ppermute | solution.py:61
  55.9 0.8 collective-permute-start.13
  56.8 3.3 %shard_map.133 = (bf16[24,256,256]{2,1,0:T(8,128)(2,1)S(1)}, bf16[24,256,256]{2,1,0:T(8,128)(2,1)S(1)}, f32[256,512]{1,0:T(8,128)S(1)}) custom-call(bf16[24,48,256]{2,1,0:T(8,128)(2,1)S(1)} %get-tuple-element.64.refs_0_, bf16[24,48,256]{2,1,0:T(8,128)(2,1)S(1)} %collective-permute-done.refs_1_, bf16[24,48,256]{2,1,0:T(8,128)(2,1)S(1)} %collective-permute-done.1.refs_2_, ...), custom_call_target="tpu_custom_call" | custom-call | flops 1048576 | bytes 16777216 | tf_op jit(solution)/shard_map/pallas_call | solution.py:73
  60.1 0.3 shard_map.135
  60.4 0.1 collective-permute-start.8
  60.5 1.3 %collective-permute-done.8.theirs = bf16[256,256]{1,0:T(8,128)(2,1)S(1)} collective-permute-done((bf16[256,256]{1,0:T(8,128)(2,1)S(1)}, bf16[256,256]{1,0:T(8,128)(2,1)S(1)}, u32[]{:S(2)}, u32[]{:S(2)}) %collective-permute-start.8) | collective-permute-done | bytes 131104 | tf_op jit(solution)/shard_map/ppermute | solution.py:61
  61.8 0.0 collective-permute-done.15.refs_5_
  61.8 0.0 collective-permute-done.14.refs_4_
  61.8 0.0 collective-permute-done.13.refs_3_
  61.8 0.1 shard_map.142.top
  61.9 2.8 %collective-permute-start.20 = (bf16[3,256,256]{2,1,0:T(8,128)(2,1)S(1)}, bf16[3,256,256]{2,1,0:T(8,128)(2,1)S(1)}, u32[]{:S(2)}, u32[]{:S(2)}) collective-permute-start(bf16[3,256,256]{2,1,0:T(8,128)(2,1)S(1)} %shard_map.142.top), channel_id=1, source_target_pairs={{0,64},{8,72},{16,80},{24,88},{32,96},{40,104},{48,112},{56,120},{... | collective-permute-start | bytes 1179656 | tf_op jit(solution)/shard_map/ppermute | solution.py:61
  64.7 0.2 shard_map.137
  65.0 0.7 collective-permute-start.18
  65.6 1.0 %collective-permute-start.17 = (bf16[256,256]{1,0:T(8,128)(2,1)S(1)}, bf16[256,256]{1,0:T(8,128)(2,1)S(1)}, u32[]{:S(2)}, u32[]{:S(2)}) collective-permute-start(bf16[256,256]{1,0:T(8,128)(2,1)S(1)} %get-tuple-element.90.refs_6_), channel_id=1, source_target_pairs={{0,32},{8,40},{16,48},{24,56},{32,0},{40,8},{48,16},{56,24},{64,96... | collective-permute-start | bytes 393224 | tf_op jit(solution)/shard_map/ppermute | solution.py:61
  66.6 0.7 collective-permute-start.16
  67.3 1.0 %shard_map.139 = (bf16[8,256,512]{2,1,0:T(8,128)(2,1)S(1)}, bf16[8,256,256]{2,1,0:T(8,128)(2,1)S(1)}) custom-call(bf16[24,256,256]{2,1,0:T(8,128)(2,1)S(1)} %get-tuple-element.105.inv, bf16[24,256,256]{2,1,0:T(8,128)(2,1)S(1)} %get-tuple-element.91.m, bf16[24,256,512]{2,1,0:T(8,128)(2,1)S(1)} %copy-done.1), custom_call_target="tpu_custom_call" | custom-call | flops 1073741824 | bytes 1048576 | tf_op jit(solution)/shard_map/pallas_call | solution.py:73
  68.4 1.0 %shard_map.138 = (bf16[8,256,512]{2,1,0:T(8,128)(2,1)S(1)}, bf16[8,256,256]{2,1,0:T(8,128)(2,1)S(1)}) custom-call(bf16[24,256,256]{2,1,0:T(8,128)(2,1)S(1)} %get-tuple-element.105.inv, bf16[24,256,256]{2,1,0:T(8,128)(2,1)S(1)} %get-tuple-element.91.m, bf16[24,256,512]{2,1,0:T(8,128)(2,1)S(1)} %copy-done.1), custom_call_target="tpu_custom_call" | custom-call | flops 1073741824 | bytes 1048576 | tf_op jit(solution)/shard_map/pallas_call | solution.py:73
  69.5 0.2 collective-permute-done.18.refs_9_
  69.7 1.8 %collective-permute-done.17.refs_8_ = bf16[256,256]{1,0:T(8,128)(2,1)S(1)} collective-permute-done((bf16[256,256]{1,0:T(8,128)(2,1)S(1)}, bf16[256,256]{1,0:T(8,128)(2,1)S(1)}, u32[]{:S(2)}, u32[]{:S(2)}) %collective-permute-start.17) | collective-permute-done | bytes 131104 | tf_op jit(solution)/shard_map/ppermute | solution.py:61
  71.5 3.6 %collective-permute-done.16.refs_7_ = bf16[256,256]{1,0:T(8,128)(2,1)S(1)} collective-permute-done((bf16[256,256]{1,0:T(8,128)(2,1)S(1)}, bf16[256,256]{1,0:T(8,128)(2,1)S(1)}, u32[]{:S(2)}, u32[]{:S(2)}) %collective-permute-start.16) | collective-permute-done | bytes 131104 | tf_op jit(solution)/shard_map/ppermute | solution.py:61
  75.0 0.5 shard_map.140
  75.6 0.0 copy-start.5
  75.6 0.2 collective-permute-start.19
  75.7 1.0 %shard_map.141 = (bf16[8,256,512]{2,1,0:T(8,128)(2,1)S(1)}, bf16[8,256,256]{2,1,0:T(8,128)(2,1)S(1)}) custom-call(bf16[24,256,256]{2,1,0:T(8,128)(2,1)S(1)} %get-tuple-element.105.inv, bf16[24,256,256]{2,1,0:T(8,128)(2,1)S(1)} %get-tuple-element.91.m, bf16[24,256,512]{2,1,0:T(8,128)(2,1)S(1)} %copy-done.1), custom_call_target="tpu_custom_call" | custom-call | flops 1073741824 | bytes 1048576 | tf_op jit(solution)/shard_map/pallas_call | solution.py:73
  76.8 4.6 %collective-permute-done.19.theirs = bf16[256,256]{1,0:T(8,128)(2,1)S(1)} collective-permute-done((bf16[256,256]{1,0:T(8,128)(2,1)S(1)}, bf16[256,256]{1,0:T(8,128)(2,1)S(1)}, u32[]{:S(2)}, u32[]{:S(2)}) %collective-permute-start.19) | collective-permute-done | bytes 131104 | tf_op jit(solution)/shard_map/ppermute | solution.py:61
  81.4 0.0 collective-permute-done.20.far
  81.4 1.2 %shard_map.143.own = bf16[2,256,256]{2,1,0:T(8,128)(2,1)S(1)} custom-call(bf16[256,256]{1,0:T(8,128)(2,1)S(1)} %get-tuple-element.100.mine, bf16[256,256]{1,0:T(8,128)(2,1)S(1)} %collective-permute-done.19.theirs, bf16[3,256,256]{2,1,0:T(8,128)(2,1)S(1)} %shard_map.142.top, bf16[3,256,256]{2,1,0:T(8,128)(2,1)S(1)} %collective-permute-done.20.far, ...), custom_call_target="tpu_custom_call" | custom-call | flops 67108864 | bytes 1048576 | tf_op jit(solution)/shard_map/pallas_call | solution.py:73
  82.5 1.8 %collective-permute-start.21 = (bf16[2,256,256]{2,1,0:T(8,128)(2,1)S(1)}, bf16[2,256,256]{2,1,0:T(8,128)(2,1)S(1)}, u32[]{:S(2)}, u32[]{:S(2)}) collective-permute-start(bf16[2,256,256]{2,1,0:T(8,128)(2,1)S(1)} %shard_map.143.own), channel_id=1, source_target_pairs={{0,8},{8,0},{16,24},{24,16},{32,40},{40,32},{48,56},{56,48},{64,72... | collective-permute-start | bytes 786440 | tf_op jit(solution)/shard_map/ppermute | solution.py:61
  84.3 1.2 %collective-permute-done.21.got = bf16[2,256,256]{2,1,0:T(8,128)(2,1)S(1)} collective-permute-done((bf16[2,256,256]{2,1,0:T(8,128)(2,1)S(1)}, bf16[2,256,256]{2,1,0:T(8,128)(2,1)S(1)}, u32[]{:S(2)}, u32[]{:S(2)}) %collective-permute-start.21) | collective-permute-done | bytes 262176 | tf_op jit(solution)/shard_map/ppermute | solution.py:61
  85.5 3.5 %shard_map.144 = (bf16[24,256,512]{2,1,0:T(8,128)(2,1)}, bf16[1,256,512]{2,1,0:T(8,128)(2,1)}, bf16[1,256,512]{2,1,0:T(8,128)(2,1)}) custom-call(bf16[256,512]{1,0:T(8,128)(2,1)S(1)} %get-tuple-element.76.r, bf16[2,256,256]{2,1,0:T(8,128)(2,1)S(1)} %get-tuple-element.75.mats, bf16[2,256,256]{2,1,0:T(8,128)(2,1)S(1)} %shard_map.143.own, ...), custom_call_target="tpu_custom_call" | custom-call | flops 2147483648 | bytes 16777216 | tf_op jit(solution)/shard_map/pallas_call | solution.py:73
  (13 shorter events, 0.1 us)
Async XLA Ops:
  2.5 24.8 %collective-permute-start.2 = (bf16[24,48,256]{2,1,0:T(8,128)(2,1)}, bf16[24,48,256]{2,1,0:T(8,128)(2,1)S(1)}, u32[]{:S(2)}, u32[]{:S(2)}) collective-permute-start(bf16[24,48,256]{2,1,0:T(8,128)(2,1)} %shard_map.130.refs_0_), channel_id=1, source_target_pairs={{0,4},{1,5},{2,6},{3,7},{4,0},{5,1},{6,2},{7,3},{8,12},{9,13},{10,... | collective-permute-start | bytes 1769480 | tf_op jit(solution)/shard_map/ppermute | solution.py:57
  4.6 22.7 %collective-permute-start.1 = (bf16[24,48,256]{2,1,0:T(8,128)(2,1)}, bf16[24,48,256]{2,1,0:T(8,128)(2,1)S(1)}, u32[]{:S(2)}, u32[]{:S(2)}) collective-permute-start(bf16[24,48,256]{2,1,0:T(8,128)(2,1)} %shard_map.130.refs_0_), channel_id=1, source_target_pairs={{0,3},{1,0},{2,1},{3,2},{4,7},{5,4},{6,5},{7,6},{8,11},{9,8},{10,9... | collective-permute-start | bytes 1769480 | tf_op jit(solution)/shard_map/ppermute | solution.py:53
  7.4 19.9 %collective-permute-start = (bf16[24,48,256]{2,1,0:T(8,128)(2,1)}, bf16[24,48,256]{2,1,0:T(8,128)(2,1)S(1)}, u32[]{:S(2)}, u32[]{:S(2)}) collective-permute-start(bf16[24,48,256]{2,1,0:T(8,128)(2,1)} %shard_map.130.refs_0_), channel_id=1, source_target_pairs={{0,1},{1,2},{2,3},{3,0},{4,5},{5,6},{6,7},{7,4},{8,9},{9,10},{10,1... | collective-permute-start | bytes 1769480 | tf_op jit(solution)/shard_map/ppermute | solution.py:49
  9.7 17.6 %all-to-all-start = ((bf16[8,128,256]{2,1,0:T(8,128)(2,1)}), bf16[8,128,256]{2,1,0:T(8,128)(2,1)S(1)}, u32[]{:S(2)}, u32[]{:S(2)}) async-start(bf16[8,128,256]{2,1,0:T(8,128)(2,1)} %shard_map.131), calls=%async_computation | async-start | bytes 1048576 | tf_op jit(solution)/shard_map/all_to_all | solution.py:394
  13.6 1.1 %copy-start.2 = (bf16[24,48,256]{2,1,0:T(8,128)(2,1)S(1)}, bf16[24,48,256]{2,1,0:T(8,128)(2,1)}, u32[]{:S(2)}) copy-start(bf16[24,48,256]{2,1,0:T(8,128)(2,1)} %shard_map.130.refs_0_) | copy-start | bytes 1769476
  14.7 0.9 %copy-start.3 = (bf16[1,256,512]{2,1,0:T(8,128)(2,1)S(1)}, bf16[1,256,512]{2,1,0:T(8,128)(2,1)}, u32[]{:S(2)}) copy-start(bf16[1,256,512]{2,1,0:T(8,128)(2,1)} %refs_2_.3) | copy-start | bytes 786436
  15.6 0.7 copy-start.6
  27.3 13.9 %collective-permute-start.5 = (bf16[24,48,256]{2,1,0:T(8,128)(2,1)S(1)}, bf16[24,48,256]{2,1,0:T(8,128)(2,1)S(1)}, u32[]{:S(2)}, u32[]{:S(2)}) collective-permute-start(bf16[24,48,256]{2,1,0:T(8,128)(2,1)S(1)} %collective-permute-done.2.refs_3_), channel_id=1, source_target_pairs={{0,3},{1,0},{2,1},{3,2},{4,7},{5,4},{6,5},{7,6},{8,11},{9,8},{10,9... | collective-permute-start | bytes 1769480 | tf_op jit(solution)/shard_map/ppermute | solution.py:53
  28.4 13.6 %collective-permute-start.4 = (bf16[24,48,256]{2,1,0:T(8,128)(2,1)S(1)}, bf16[24,48,256]{2,1,0:T(8,128)(2,1)S(1)}, u32[]{:S(2)}, u32[]{:S(2)}) collective-permute-start(bf16[24,48,256]{2,1,0:T(8,128)(2,1)S(1)} %collective-permute-done.refs_1_), channel_id=1, source_target_pairs={{0,4},{1,5},{2,6},{3,7},{4,0},{5,1},{6,2},{7,3},{8,12},{9,13},{10,... | collective-permute-start | bytes 1769480 | tf_op jit(solution)/shard_map/ppermute | solution.py:57
  28.6 13.6 %collective-permute-start.3 = (bf16[24,48,256]{2,1,0:T(8,128)(2,1)S(1)}, bf16[24,48,256]{2,1,0:T(8,128)(2,1)S(1)}, u32[]{:S(2)}, u32[]{:S(2)}) collective-permute-start(bf16[24,48,256]{2,1,0:T(8,128)(2,1)S(1)} %collective-permute-done.refs_1_), channel_id=1, source_target_pairs={{0,1},{1,2},{2,3},{3,0},{4,5},{5,6},{6,7},{7,4},{8,9},{9,10},{10,1... | collective-permute-start | bytes 1769480 | tf_op jit(solution)/shard_map/ppermute | solution.py:49
  29.3 2.8 %copy-start = (bf16[24,256,512]{2,1,0:T(8,128)(2,1)S(1)}, bf16[24,256,512]{2,1,0:T(8,128)(2,1)}, u32[]{:S(2)}) copy-start(bf16[24,256,512]{2,1,0:T(8,128)(2,1)} %rhs.7) | copy-start | bytes 18874372
  32.0 24.8 %copy-start.1 = (bf16[24,256,512]{2,1,0:T(8,128)(2,1)S(1)}, bf16[24,256,512]{2,1,0:T(8,128)(2,1)}, u32[]{:S(2)}) copy-start(bf16[24,256,512]{2,1,0:T(8,128)(2,1)} %rhs.7) | copy-start | bytes 18874372
  32.4 5.0 %collective-permute-start.9 = (bf16[3,256,256]{2,1,0:T(8,128)(2,1)S(1)}, bf16[3,256,256]{2,1,0:T(8,128)(2,1)S(1)}, u32[]{:S(2)}, u32[]{:S(2)}) collective-permute-start(bf16[3,256,256]{2,1,0:T(8,128)(2,1)S(1)} %get-tuple-element.80), channel_id=1, source_target_pairs={{0,8},{8,0},{16,24},{24,16},{32,40},{40,32},{48,56},{56,48},{64,72... | collective-permute-start | bytes 1179656 | tf_op jit(solution)/shard_map/ppermute | solution.py:61
  37.4 14.8 %collective-permute-start.12 = (bf16[2,256,256]{2,1,0:T(8,128)(2,1)S(1)}, bf16[2,256,256]{2,1,0:T(8,128)(2,1)S(1)}, u32[]{:S(2)}, u32[]{:S(2)}) collective-permute-start(bf16[2,256,256]{2,1,0:T(8,128)(2,1)S(1)} %get-tuple-element.89), channel_id=1, source_target_pairs={{0,48},{8,56},{16,0},{24,8},{32,16},{40,24},{48,32},{56,40},{64,11... | collective-permute-start | bytes 786440 | tf_op jit(solution)/shard_map/ppermute | solution.py:61
  41.2 12.1 %collective-permute-start.11 = (bf16[2,256,256]{2,1,0:T(8,128)(2,1)S(1)}, bf16[2,256,256]{2,1,0:T(8,128)(2,1)S(1)}, u32[]{:S(2)}, u32[]{:S(2)}) collective-permute-start(bf16[2,256,256]{2,1,0:T(8,128)(2,1)S(1)} %get-tuple-element.89), channel_id=1, source_target_pairs={{0,32},{8,40},{16,48},{24,56},{32,0},{40,8},{48,16},{56,24},{64,96... | collective-permute-start | bytes 786440 | tf_op jit(solution)/shard_map/ppermute | solution.py:61
  41.2 14.7 %collective-permute-start.10 = (bf16[2,256,256]{2,1,0:T(8,128)(2,1)S(1)}, bf16[2,256,256]{2,1,0:T(8,128)(2,1)S(1)}, u32[]{:S(2)}, u32[]{:S(2)}) collective-permute-start(bf16[2,256,256]{2,1,0:T(8,128)(2,1)S(1)} %get-tuple-element.89), channel_id=1, source_target_pairs={{0,16},{8,24},{16,32},{24,40},{32,48},{40,56},{48,0},{56,8},{64,80... | collective-permute-start | bytes 786440 | tf_op jit(solution)/shard_map/ppermute | solution.py:61
  42.3 17.8 %copy-start.4 = (bf16[1,256,512]{2,1,0:T(8,128)(2,1)S(1)}, bf16[1,256,512]{2,1,0:T(8,128)(2,1)}, u32[]{:S(2)}) copy-start(bf16[1,256,512]{2,1,0:T(8,128)(2,1)} %rhs.4) | copy-start | bytes 786436
  42.3 14.5 %collective-permute-start.7 = (bf16[12,48,256]{2,1,0:T(8,128)(2,1)S(1)}, bf16[12,48,256]{2,1,0:T(8,128)(2,1)S(1)}, u32[]{:S(2)}, u32[]{:S(2)}) collective-permute-start(bf16[12,48,256]{2,1,0:T(8,128)(2,1)S(1)} %slice.7), channel_id=1, source_target_pairs={{0,3},{1,0},{2,1},{3,2},{4,7},{5,4},{6,5},{7,6},{8,11},{9,8},{10,9... | collective-permute-start | bytes 884744 | tf_op jit(solution)/shard_map/ppermute | solution.py:53
  44.3 12.5 %collective-permute-start.6 = (bf16[12,48,256]{2,1,0:T(8,128)(2,1)S(1)}, bf16[12,48,256]{2,1,0:T(8,128)(2,1)S(1)}, u32[]{:S(2)}, u32[]{:S(2)}) collective-permute-start(bf16[12,48,256]{2,1,0:T(8,128)(2,1)S(1)} %slice.6), channel_id=1, source_target_pairs={{0,1},{1,2},{2,3},{3,0},{4,5},{5,6},{6,7},{7,4},{8,9},{9,10},{10,1... | collective-permute-start | bytes 884744 | tf_op jit(solution)/shard_map/ppermute | solution.py:49
  52.2 9.7 %collective-permute-start.15 = (bf16[2,256,256]{2,1,0:T(8,128)(2,1)S(1)}, bf16[2,256,256]{2,1,0:T(8,128)(2,1)S(1)}, u32[]{:S(2)}, u32[]{:S(2)}) collective-permute-start(bf16[2,256,256]{2,1,0:T(8,128)(2,1)S(1)} %collective-permute-done.12.refs_2_), channel_id=1, source_target_pairs={{0,8},{8,0},{16,24},{24,16},{32,40},{40,32},{48,56},{56,48},{64,72... | collective-permute-start | bytes 786440 | tf_op jit(solution)/shard_map/ppermute | solution.py:61
  53.4 8.5 %collective-permute-start.14 = (bf16[2,256,256]{2,1,0:T(8,128)(2,1)S(1)}, bf16[2,256,256]{2,1,0:T(8,128)(2,1)S(1)}, u32[]{:S(2)}, u32[]{:S(2)}) collective-permute-start(bf16[2,256,256]{2,1,0:T(8,128)(2,1)S(1)} %collective-permute-done.11.refs_1_), channel_id=1, source_target_pairs={{0,8},{8,0},{16,24},{24,16},{32,40},{40,32},{48,56},{56,48},{64,72... | collective-permute-start | bytes 786440 | tf_op jit(solution)/shard_map/ppermute | solution.py:61
  55.9 5.9 %collective-permute-start.13 = (bf16[2,256,256]{2,1,0:T(8,128)(2,1)S(1)}, bf16[2,256,256]{2,1,0:T(8,128)(2,1)S(1)}, u32[]{:S(2)}, u32[]{:S(2)}) collective-permute-start(bf16[2,256,256]{2,1,0:T(8,128)(2,1)S(1)} %collective-permute-done.10.refs_0_), channel_id=1, source_target_pairs={{0,8},{8,0},{16,24},{24,16},{32,40},{40,32},{48,56},{56,48},{64,72... | collective-permute-start | bytes 786440 | tf_op jit(solution)/shard_map/ppermute | solution.py:61
  60.4 1.4 %collective-permute-start.8 = (bf16[256,256]{1,0:T(8,128)(2,1)S(1)}, bf16[256,256]{1,0:T(8,128)(2,1)S(1)}, u32[]{:S(2)}, u32[]{:S(2)}) collective-permute-start(bf16[256,256]{1,0:T(8,128)(2,1)S(1)} %get-tuple-element.78), channel_id=1, source_target_pairs={{0,8},{8,0},{16,24},{24,16},{32,40},{40,32},{48,56},{56,48},{64,72... | collective-permute-start | bytes 393224 | tf_op jit(solution)/shard_map/ppermute | solution.py:61
  61.9 19.4 %collective-permute-start.20 = (bf16[3,256,256]{2,1,0:T(8,128)(2,1)S(1)}, bf16[3,256,256]{2,1,0:T(8,128)(2,1)S(1)}, u32[]{:S(2)}, u32[]{:S(2)}) collective-permute-start(bf16[3,256,256]{2,1,0:T(8,128)(2,1)S(1)} %shard_map.142.top), channel_id=1, source_target_pairs={{0,64},{8,72},{16,80},{24,88},{32,96},{40,104},{48,112},{56,120},{... | collective-permute-start | bytes 1179656 | tf_op jit(solution)/shard_map/ppermute | solution.py:61
  65.0 4.7 %collective-permute-start.18 = (bf16[256,256]{1,0:T(8,128)(2,1)S(1)}, bf16[256,256]{1,0:T(8,128)(2,1)S(1)}, u32[]{:S(2)}, u32[]{:S(2)}) collective-permute-start(bf16[256,256]{1,0:T(8,128)(2,1)S(1)} %get-tuple-element.90.refs_6_), channel_id=1, source_target_pairs={{0,48},{8,56},{16,0},{24,8},{32,16},{40,24},{48,32},{56,40},{64,11... | collective-permute-start | bytes 393224 | tf_op jit(solution)/shard_map/ppermute | solution.py:61
  65.6 5.8 %collective-permute-start.17 = (bf16[256,256]{1,0:T(8,128)(2,1)S(1)}, bf16[256,256]{1,0:T(8,128)(2,1)S(1)}, u32[]{:S(2)}, u32[]{:S(2)}) collective-permute-start(bf16[256,256]{1,0:T(8,128)(2,1)S(1)} %get-tuple-element.90.refs_6_), channel_id=1, source_target_pairs={{0,32},{8,40},{16,48},{24,56},{32,0},{40,8},{48,16},{56,24},{64,96... | collective-permute-start | bytes 393224 | tf_op jit(solution)/shard_map/ppermute | solution.py:61
  66.6 8.4 %collective-permute-start.16 = (bf16[256,256]{1,0:T(8,128)(2,1)S(1)}, bf16[256,256]{1,0:T(8,128)(2,1)S(1)}, u32[]{:S(2)}, u32[]{:S(2)}) collective-permute-start(bf16[256,256]{1,0:T(8,128)(2,1)S(1)} %get-tuple-element.90.refs_6_), channel_id=1, source_target_pairs={{0,16},{8,24},{16,32},{24,40},{32,48},{40,56},{48,0},{56,8},{64,80... | collective-permute-start | bytes 393224 | tf_op jit(solution)/shard_map/ppermute | solution.py:61
  75.6 5.8 %copy-start.5 = (bf16[256,512]{1,0:T(8,128)(2,1)S(1)}, bf16[256,512]{1,0:T(8,128)(2,1)}, u32[]{:S(2)}) copy-start(bf16[256,512]{1,0:T(8,128)(2,1)} %above.1) | copy-start | bytes 786436
  75.6 5.8 %collective-permute-start.19 = (bf16[256,256]{1,0:T(8,128)(2,1)S(1)}, bf16[256,256]{1,0:T(8,128)(2,1)S(1)}, u32[]{:S(2)}, u32[]{:S(2)}) collective-permute-start(bf16[256,256]{1,0:T(8,128)(2,1)S(1)} %get-tuple-element.100.mine), channel_id=1, source_target_pairs={{0,64},{8,72},{16,80},{24,88},{32,96},{40,104},{48,112},{56,120},{... | collective-permute-start | bytes 393224 | tf_op jit(solution)/shard_map/ppermute | solution.py:61
  82.5 3.0 %collective-permute-start.21 = (bf16[2,256,256]{2,1,0:T(8,128)(2,1)S(1)}, bf16[2,256,256]{2,1,0:T(8,128)(2,1)S(1)}, u32[]{:S(2)}, u32[]{:S(2)}) collective-permute-start(bf16[2,256,256]{2,1,0:T(8,128)(2,1)S(1)} %shard_map.143.own), channel_id=1, source_target_pairs={{0,8},{8,0},{16,24},{24,16},{32,40},{40,32},{48,56},{56,48},{64,72... | collective-permute-start | bytes 786440 | tf_op jit(solution)/shard_map/ppermute | solution.py:61

commit v6 on v4

--- a/solution.py
+++ b/solution.py
@@ -444,7 +444,7 @@
         root_kernel, [(256, 512), (256, 256), (256, 256)], rhs_roots, total, root_mats
     )
     packs2 = [among(v, CORES) for v in packs]
-    theirs, packs, packs2 = lax.optimization_barrier((among(send, CORES), packs, packs2))
+    theirs, even, odd = lax.optimization_barrier((among(send, CORES), even, odd))
     (top,) = call(
         choose_kernel, [(3, 256, 256)], odd, *packs, *packs2
     )

time: 89.7 us -> 89.7 us (level)
  no operation moved by 1% of the time
where the time goes in v6:
time: 89.7 us; the launch traced here: 89.2 us
  waiting for transfers between devices  35.3 us (39%)
  starting transfers between devices  30.2 us (34%)
  Pallas kernels  17.1 us (19%)
  local copies, waits for them, and re-layouts  5.56 us (6%)
  between operations  0.97 us (1%)
    ppermute x14, waiting for transfers between devices, among(): return lax.ppermute(v, 'leaf', pairs)  24.4 us
    ppermute x14, starting transfers between devices, among(): return lax.ppermute(v, 'leaf', pairs)  17.4 us
    pallas_call x15, Pallas kernels, call(): pl.pallas_call(kernel, in_specs=specs.get('in_specs', [VMEM] * len(args))...  17.1 us
    all_to_all x1, waiting for transfers between devices, local(): small = lax.all_to_all(small, 'load', 0, 0)  10.6 us
    ppermute x3, starting transfers between devices, down(): return lax.ppermute(v, 'load', y_shift(3))  5.82 us
    unnamed x14, local copies, waits for them, and re-layouts  5.52 us
    all_to_all x1, starting transfers between devices, local(): small = lax.all_to_all(small, 'load', 0, 0)  3.96 us
    ppermute x2, starting transfers between devices, across(): return lax.ppermute(v, 'load', X_LO)  2.37 us
  transfers between devices with their start and end apart: 23, of which 11 were waited for; matrix products, arithmetic and copies ran while one was open for 0% of the time, Pallas kernels for 12%

profile of v6, /device:TPU:1, one launch (start us, length us, event | category | flops | bytes accessed | tf_op | source)
XLA Modules:
  0.0 89.2 jit_solution(15306477191163647780)
XLA Ops:
  0.6 1.9 %shard_map.130.refs_0_ = bf16[24,48,256]{2,1,0:T(8,128)(2,1)} custom-call(bf16[24,32,256]{2,1,0:T(8,128)(2,1)} %inv.1, bf16[24,16,256]{2,1,0:T(8,128)(2,1)} %upd.1), custom_call_target="tpu_custom_call" | custom-call | flops 67108864 | bytes 1048576 | tf_op jit(solution)/shard_map/pallas_call | solution.py:73
  2.5 2.1 %collective-permute-start.2 = (bf16[24,48,256]{2,1,0:T(8,128)(2,1)}, bf16[24,48,256]{2,1,0:T(8,128)(2,1)S(1)}, u32[]{:S(2)}, u32[]{:S(2)}) collective-permute-start(bf16[24,48,256]{2,1,0:T(8,128)(2,1)} %shard_map.130.refs_0_), channel_id=1, source_target_pairs={{0,4},{1,5},{2,6},{3,7},{4,0},{5,1},{6,2},{7,3},{8,12},{9,13},{10,... | collective-permute-start | bytes 1769480 | tf_op jit(solution)/shard_map/ppermute | solution.py:57
  4.6 2.7 %collective-permute-start.1 = (bf16[24,48,256]{2,1,0:T(8,128)(2,1)}, bf16[24,48,256]{2,1,0:T(8,128)(2,1)S(1)}, u32[]{:S(2)}, u32[]{:S(2)}) collective-permute-start(bf16[24,48,256]{2,1,0:T(8,128)(2,1)} %shard_map.130.refs_0_), channel_id=1, source_target_pairs={{0,3},{1,0},{2,1},{3,2},{4,7},{5,4},{6,5},{7,6},{8,11},{9,8},{10,9... | collective-permute-start | bytes 1769480 | tf_op jit(solution)/shard_map/ppermute | solution.py:53
  7.4 0.0 collective-permute-start
  7.4 2.4 %shard_map.131 = bf16[8,128,256]{2,1,0:T(8,128)(2,1)} custom-call(bf16[1,32,256]{2,1,0:T(8,128)(2,1)} %refs_0_.1, bf16[1,32,256]{2,1,0:T(8,128)(2,1)} %refs_1_.1, bf16[1,32,256]{2,1,0:T(8,128)(2,1)} %refs_2_.2, bf16[1,32,256]{2,1,0:T(8,128)(2,1)} %refs_3_.1), custom_call_target="tpu_custom_call" | custom-call | flops 67108864 | bytes 1048576 | tf_op jit(solution)/shard_map/pallas_call | solution.py:73
  9.8 4.0 %all-to-all-start = ((bf16[8,128,256]{2,1,0:T(8,128)(2,1)}), bf16[8,128,256]{2,1,0:T(8,128)(2,1)S(1)}, u32[]{:S(2)}, u32[]{:S(2)}) async-start(bf16[8,128,256]{2,1,0:T(8,128)(2,1)} %shard_map.131), calls=%async_computation | async-start | bytes 1048576 | tf_op jit(solution)/shard_map/all_to_all | solution.py:411
  13.8 1.1 %copy-done.2 = bf16[24,48,256]{2,1,0:T(8,128)(2,1)S(1)} copy-done((bf16[24,48,256]{2,1,0:T(8,128)(2,1)S(1)}, bf16[24,48,256]{2,1,0:T(8,128)(2,1)}, u32[]{:S(2)}) %copy-start.2) | copy-done | bytes 589848
  14.9 0.9 %copy-done.3 = bf16[1,256,512]{2,1,0:T(8,128)(2,1)S(1)} copy-done((bf16[1,256,512]{2,1,0:T(8,128)(2,1)S(1)}, bf16[1,256,512]{2,1,0:T(8,128)(2,1)}, u32[]{:S(2)}) %copy-start.3) | copy-done | bytes 262168
  15.8 0.7 copy-done.6
  16.5 0.2 shard_map.132
  16.7 10.6 %all-to-all-done.rows = bf16[8,128,256]{2,1,0:T(8,128)(2,1)S(1)} async-done(((bf16[8,128,256]{2,1,0:T(8,128)(2,1)}), bf16[8,128,256]{2,1,0:T(8,128)(2,1)S(1)}, u32[]{:S(2)}, u32[]{:S(2)}) %all-to-all-start) | async-done | bytes 524320 | tf_op jit(solution)/shard_map/all_to_all | solution.py:411
  27.3 0.0 collective-permute-done.2.refs_3_
  27.3 0.0 collective-permute-done.1.refs_2_
  27.3 0.0 collective-permute-done.refs_1_
  27.3 1.1 %collective-permute-start.5 = (bf16[24,48,256]{2,1,0:T(8,128)(2,1)S(1)}, bf16[24,48,256]{2,1,0:T(8,128)(2,1)S(1)}, u32[]{:S(2)}, u32[]{:S(2)}) collective-permute-start(bf16[24,48,256]{2,1,0:T(8,128)(2,1)S(1)} %collective-permute-done.2.refs_3_), channel_id=1, source_target_pairs={{0,3},{1,0},{2,1},{3,2},{4,7},{5,4},{6,5},{7,6},{8,11},{9,8},{10,9... | collective-permute-start | bytes 1769480 | tf_op jit(solution)/shard_map/ppermute | solution.py:53
  28.4 0.3 collective-permute-start.4
  28.6 0.6 collective-permute-start.3
  29.3 2.8 %copy-done = bf16[24,256,512]{2,1,0:T(8,128)(2,1)S(1)} copy-done((bf16[24,256,512]{2,1,0:T(8,128)(2,1)S(1)}, bf16[24,256,512]{2,1,0:T(8,128)(2,1)}, u32[]{:S(2)}) %copy-start) | copy-done | bytes 6291480
  32.0 0.3 shard_map.134
  32.4 3.6 %collective-permute-start.9 = (bf16[3,256,256]{2,1,0:T(8,128)(2,1)S(1)}, bf16[3,256,256]{2,1,0:T(8,128)(2,1)S(1)}, u32[]{:S(2)}, u32[]{:S(2)}) collective-permute-start(bf16[3,256,256]{2,1,0:T(8,128)(2,1)S(1)} %get-tuple-element.80), channel_id=1, source_target_pairs={{0,8},{8,0},{16,24},{24,16},{32,40},{40,32},{48,56},{56,48},{64,72... | collective-permute-start | bytes 1179656 | tf_op jit(solution)/shard_map/ppermute | solution.py:61
  36.0 1.3 %collective-permute-done.9.got = bf16[3,256,256]{2,1,0:T(8,128)(2,1)S(1)} collective-permute-done((bf16[3,256,256]{2,1,0:T(8,128)(2,1)S(1)}, bf16[3,256,256]{2,1,0:T(8,128)(2,1)S(1)}, u32[]{:S(2)}, u32[]{:S(2)}) %collective-permute-start.9) | collective-permute-done | bytes 393248 | tf_op jit(solution)/shard_map/ppermute | solution.py:61
  37.3 0.1 shard_map.136
  37.4 3.8 %collective-permute-start.12 = (bf16[2,256,256]{2,1,0:T(8,128)(2,1)S(1)}, bf16[2,256,256]{2,1,0:T(8,128)(2,1)S(1)}, u32[]{:S(2)}, u32[]{:S(2)}) collective-permute-start(bf16[2,256,256]{2,1,0:T(8,128)(2,1)S(1)} %get-tuple-element.89), channel_id=1, source_target_pairs={{0,48},{8,56},{16,0},{24,8},{32,16},{40,24},{48,32},{56,40},{64,11... | collective-permute-start | bytes 786440 | tf_op jit(solution)/shard_map/ppermute | solution.py:61
  41.2 0.0 collective-permute-start.11
  41.2 0.0 collective-permute-done.5.refs_6_
  41.2 0.7 collective-permute-start.10
  41.9 0.0 collective-permute-done.4.refs_5_
  41.9 0.3 collective-permute-done.3.refs_4_
  42.3 0.0 copy-start.4
  42.3 2.0 %collective-permute-start.7 = (bf16[12,48,256]{2,1,0:T(8,128)(2,1)S(1)}, bf16[12,48,256]{2,1,0:T(8,128)(2,1)S(1)}, u32[]{:S(2)}, u32[]{:S(2)}) collective-permute-start(bf16[12,48,256]{2,1,0:T(8,128)(2,1)S(1)} %slice.7), channel_id=1, source_target_pairs={{0,3},{1,0},{2,1},{3,2},{4,7},{5,4},{6,5},{7,6},{8,11},{9,8},{10,9... | collective-permute-start | bytes 884744 | tf_op jit(solution)/shard_map/ppermute | solution.py:53
  44.3 7.8 %collective-permute-done.12.refs_2_ = bf16[2,256,256]{2,1,0:T(8,128)(2,1)S(1)} collective-permute-done((bf16[2,256,256]{2,1,0:T(8,128)(2,1)S(1)}, bf16[2,256,256]{2,1,0:T(8,128)(2,1)S(1)}, u32[]{:S(2)}, u32[]{:S(2)}) %collective-permute-start.12) | collective-permute-done | bytes 262176 | tf_op jit(solution)/shard_map/ppermute | solution.py:61
  52.2 1.2 %collective-permute-start.15 = (bf16[2,256,256]{2,1,0:T(8,128)(2,1)S(1)}, bf16[2,256,256]{2,1,0:T(8,128)(2,1)S(1)}, u32[]{:S(2)}, u32[]{:S(2)}) collective-permute-start(bf16[2,256,256]{2,1,0:T(8,128)(2,1)S(1)} %collective-permute-done.12.refs_2_), channel_id=1, source_target_pairs={{0,8},{8,0},{16,24},{24,16},{32,40},{40,32},{48,56},{56,48},{64,72... | collective-permute-start | bytes 786440 | tf_op jit(solution)/shard_map/ppermute | solution.py:61
  53.4 0.0 collective-permute-done.11.refs_1_
  53.4 0.0 collective-permute-start.14
  53.4 2.6 %collective-permute-done.10.refs_0_ = bf16[2,256,256]{2,1,0:T(8,128)(2,1)S(1)} collective-permute-done((bf16[2,256,256]{2,1,0:T(8,128)(2,1)S(1)}, bf16[2,256,256]{2,1,0:T(8,128)(2,1)S(1)}, u32[]{:S(2)}, u32[]{:S(2)}) %collective-permute-start.10) | collective-permute-done | bytes 262176 | tf_op jit(solution)/shard_map/ppermute | solution.py:61
  55.9 0.8 collective-permute-start.13
  56.8 3.3 %shard_map.133 = (bf16[24,256,256]{2,1,0:T(8,128)(2,1)S(1)}, bf16[24,256,256]{2,1,0:T(8,128)(2,1)S(1)}, f32[256,512]{1,0:T(8,128)S(1)}) custom-call(bf16[24,48,256]{2,1,0:T(8,128)(2,1)S(1)} %get-tuple-element.64.refs_0_, bf16[24,48,256]{2,1,0:T(8,128)(2,1)S(1)} %collective-permute-done.refs_1_, bf16[24,48,256]{2,1,0:T(8,128)(2,1)S(1)} %collective-permute-done.1.refs_2_, ...), custom_call_target="tpu_custom_call" | custom-call | flops 1048576 | bytes 16777216 | tf_op jit(solution)/shard_map/pallas_call | solution.py:73
  60.1 0.3 shard_map.135
  60.4 0.1 collective-permute-start.8
  60.5 1.3 %collective-permute-done.8.theirs = bf16[256,256]{1,0:T(8,128)(2,1)S(1)} collective-permute-done((bf16[256,256]{1,0:T(8,128)(2,1)S(1)}, bf16[256,256]{1,0:T(8,128)(2,1)S(1)}, u32[]{:S(2)}, u32[]{:S(2)}) %collective-permute-start.8) | collective-permute-done | bytes 131104 | tf_op jit(solution)/shard_map/ppermute | solution.py:61
  61.8 0.0 collective-permute-done.15.refs_5_
  61.8 0.0 collective-permute-done.14.refs_4_
  61.8 0.0 collective-permute-done.13.refs_3_
  61.8 0.1 shard_map.142.top
  61.9 2.8 %collective-permute-start.20 = (bf16[3,256,256]{2,1,0:T(8,128)(2,1)S(1)}, bf16[3,256,256]{2,1,0:T(8,128)(2,1)S(1)}, u32[]{:S(2)}, u32[]{:S(2)}) collective-permute-start(bf16[3,256,256]{2,1,0:T(8,128)(2,1)S(1)} %shard_map.142.top), channel_id=1, source_target_pairs={{0,64},{8,72},{16,80},{24,88},{32,96},{40,104},{48,112},{56,120},{... | collective-permute-start | bytes 1179656 | tf_op jit(solution)/shard_map/ppermute | solution.py:61
  64.7 0.2 shard_map.137
  65.0 0.7 collective-permute-start.18
  65.6 1.0 %collective-permute-start.17 = (bf16[256,256]{1,0:T(8,128)(2,1)S(1)}, bf16[256,256]{1,0:T(8,128)(2,1)S(1)}, u32[]{:S(2)}, u32[]{:S(2)}) collective-permute-start(bf16[256,256]{1,0:T(8,128)(2,1)S(1)} %get-tuple-element.90.refs_6_), channel_id=1, source_target_pairs={{0,32},{8,40},{16,48},{24,56},{32,0},{40,8},{48,16},{56,24},{64,96... | collective-permute-start | bytes 393224 | tf_op jit(solution)/shard_map/ppermute | solution.py:61
  66.6 0.7 collective-permute-start.16
  67.3 1.0 %shard_map.139 = (bf16[8,256,512]{2,1,0:T(8,128)(2,1)S(1)}, bf16[8,256,256]{2,1,0:T(8,128)(2,1)S(1)}) custom-call(bf16[24,256,256]{2,1,0:T(8,128)(2,1)S(1)} %get-tuple-element.105.inv, bf16[24,256,256]{2,1,0:T(8,128)(2,1)S(1)} %get-tuple-element.91.m, bf16[24,256,512]{2,1,0:T(8,128)(2,1)S(1)} %copy-done.1), custom_call_target="tpu_custom_call" | custom-call | flops 1073741824 | bytes 1048576 | tf_op jit(solution)/shard_map/pallas_call | solution.py:73
  68.4 1.0 %shard_map.138 = (bf16[8,256,512]{2,1,0:T(8,128)(2,1)S(1)}, bf16[8,256,256]{2,1,0:T(8,128)(2,1)S(1)}) custom-call(bf16[24,256,256]{2,1,0:T(8,128)(2,1)S(1)} %get-tuple-element.105.inv, bf16[24,256,256]{2,1,0:T(8,128)(2,1)S(1)} %get-tuple-element.91.m, bf16[24,256,512]{2,1,0:T(8,128)(2,1)S(1)} %copy-done.1), custom_call_target="tpu_custom_call" | custom-call | flops 1073741824 | bytes 1048576 | tf_op jit(solution)/shard_map/pallas_call | solution.py:73
  69.5 0.2 collective-permute-done.18.refs_9_
  69.7 1.8 %collective-permute-done.17.refs_8_ = bf16[256,256]{1,0:T(8,128)(2,1)S(1)} collective-permute-done((bf16[256,256]{1,0:T(8,128)(2,1)S(1)}, bf16[256,256]{1,0:T(8,128)(2,1)S(1)}, u32[]{:S(2)}, u32[]{:S(2)}) %collective-permute-start.17) | collective-permute-done | bytes 131104 | tf_op jit(solution)/shard_map/ppermute | solution.py:61
  71.5 3.6 %collective-permute-done.16.refs_7_ = bf16[256,256]{1,0:T(8,128)(2,1)S(1)} collective-permute-done((bf16[256,256]{1,0:T(8,128)(2,1)S(1)}, bf16[256,256]{1,0:T(8,128)(2,1)S(1)}, u32[]{:S(2)}, u32[]{:S(2)}) %collective-permute-start.16) | collective-permute-done | bytes 131104 | tf_op jit(solution)/shard_map/ppermute | solution.py:61
  75.0 0.5 shard_map.140
  75.6 0.0 copy-start.5
  75.6 0.2 collective-permute-start.19
  75.7 1.0 %shard_map.141 = (bf16[8,256,512]{2,1,0:T(8,128)(2,1)S(1)}, bf16[8,256,256]{2,1,0:T(8,128)(2,1)S(1)}) custom-call(bf16[24,256,256]{2,1,0:T(8,128)(2,1)S(1)} %get-tuple-element.105.inv, bf16[24,256,256]{2,1,0:T(8,128)(2,1)S(1)} %get-tuple-element.91.m, bf16[24,256,512]{2,1,0:T(8,128)(2,1)S(1)} %copy-done.1), custom_call_target="tpu_custom_call" | custom-call | flops 1073741824 | bytes 1048576 | tf_op jit(solution)/shard_map/pallas_call | solution.py:73
  76.8 4.6 %collective-permute-done.19.theirs = bf16[256,256]{1,0:T(8,128)(2,1)S(1)} collective-permute-done((bf16[256,256]{1,0:T(8,128)(2,1)S(1)}, bf16[256,256]{1,0:T(8,128)(2,1)S(1)}, u32[]{:S(2)}, u32[]{:S(2)}) %collective-permute-start.19) | collective-permute-done | bytes 131104 | tf_op jit(solution)/shard_map/ppermute | solution.py:61
  81.4 0.0 collective-permute-done.20.far
  81.4 1.2 %shard_map.143.own = bf16[2,256,256]{2,1,0:T(8,128)(2,1)S(1)} custom-call(bf16[256,256]{1,0:T(8,128)(2,1)S(1)} %get-tuple-element.100.mine, bf16[256,256]{1,0:T(8,128)(2,1)S(1)} %collective-permute-done.19.theirs, bf16[3,256,256]{2,1,0:T(8,128)(2,1)S(1)} %shard_map.142.top, bf16[3,256,256]{2,1,0:T(8,128)(2,1)S(1)} %collective-permute-done.20.far, ...), custom_call_target="tpu_custom_call" | custom-call | flops 67108864 | bytes 1048576 | tf_op jit(solution)/shard_map/pallas_call | solution.py:73
  82.6 1.8 %collective-permute-start.21 = (bf16[2,256,256]{2,1,0:T(8,128)(2,1)S(1)}, bf16[2,256,256]{2,1,0:T(8,128)(2,1)S(1)}, u32[]{:S(2)}, u32[]{:S(2)}) collective-permute-start(bf16[2,256,256]{2,1,0:T(8,128)(2,1)S(1)} %shard_map.143.own), channel_id=1, source_target_pairs={{0,8},{8,0},{16,24},{24,16},{32,40},{40,32},{48,56},{56,48},{64,72... | collective-permute-start | bytes 786440 | tf_op jit(solution)/shard_map/ppermute | solution.py:61
  84.4 1.2 %collective-permute-done.21.got = bf16[2,256,256]{2,1,0:T(8,128)(2,1)S(1)} collective-permute-done((bf16[2,256,256]{2,1,0:T(8,128)(2,1)S(1)}, bf16[2,256,256]{2,1,0:T(8,128)(2,1)S(1)}, u32[]{:S(2)}, u32[]{:S(2)}) %collective-permute-start.21) | collective-permute-done | bytes 262176 | tf_op jit(solution)/shard_map/ppermute | solution.py:61
  85.5 3.5 %shard_map.144 = (bf16[24,256,512]{2,1,0:T(8,128)(2,1)}, bf16[1,256,512]{2,1,0:T(8,128)(2,1)}, bf16[1,256,512]{2,1,0:T(8,128)(2,1)}) custom-call(bf16[256,512]{1,0:T(8,128)(2,1)S(1)} %get-tuple-element.76.r, bf16[2,256,256]{2,1,0:T(8,128)(2,1)S(1)} %get-tuple-element.75.mats, bf16[2,256,256]{2,1,0:T(8,128)(2,1)S(1)} %shard_map.143.own, ...), custom_call_target="tpu_custom_call" | custom-call | flops 2147483648 | bytes 16777216 | tf_op jit(solution)/shard_map/pallas_call | solution.py:73
  (13 shorter events, 0.1 us)
Async XLA Ops:
  2.5 24.8 %collective-permute-start.2 = (bf16[24,48,256]{2,1,0:T(8,128)(2,1)}, bf16[24,48,256]{2,1,0:T(8,128)(2,1)S(1)}, u32[]{:S(2)}, u32[]{:S(2)}) collective-permute-start(bf16[24,48,256]{2,1,0:T(8,128)(2,1)} %shard_map.130.refs_0_), channel_id=1, source_target_pairs={{0,4},{1,5},{2,6},{3,7},{4,0},{5,1},{6,2},{7,3},{8,12},{9,13},{10,... | collective-permute-start | bytes 1769480 | tf_op jit(solution)/shard_map/ppermute | solution.py:57
  4.6 22.7 %collective-permute-start.1 = (bf16[24,48,256]{2,1,0:T(8,128)(2,1)}, bf16[24,48,256]{2,1,0:T(8,128)(2,1)S(1)}, u32[]{:S(2)}, u32[]{:S(2)}) collective-permute-start(bf16[24,48,256]{2,1,0:T(8,128)(2,1)} %shard_map.130.refs_0_), channel_id=1, source_target_pairs={{0,3},{1,0},{2,1},{3,2},{4,7},{5,4},{6,5},{7,6},{8,11},{9,8},{10,9... | collective-permute-start | bytes 1769480 | tf_op jit(solution)/shard_map/ppermute | solution.py:53
  7.4 19.9 %collective-permute-start = (bf16[24,48,256]{2,1,0:T(8,128)(2,1)}, bf16[24,48,256]{2,1,0:T(8,128)(2,1)S(1)}, u32[]{:S(2)}, u32[]{:S(2)}) collective-permute-start(bf16[24,48,256]{2,1,0:T(8,128)(2,1)} %shard_map.130.refs_0_), channel_id=1, source_target_pairs={{0,1},{1,2},{2,3},{3,0},{4,5},{5,6},{6,7},{7,4},{8,9},{9,10},{10,1... | collective-permute-start | bytes 1769480 | tf_op jit(solution)/shard_map/ppermute | solution.py:49
  9.8 17.5 %all-to-all-start = ((bf16[8,128,256]{2,1,0:T(8,128)(2,1)}), bf16[8,128,256]{2,1,0:T(8,128)(2,1)S(1)}, u32[]{:S(2)}, u32[]{:S(2)}) async-start(bf16[8,128,256]{2,1,0:T(8,128)(2,1)} %shard_map.131), calls=%async_computation | async-start | bytes 1048576 | tf_op jit(solution)/shard_map/all_to_all | solution.py:411
  13.8 1.1 %copy-start.2 = (bf16[24,48,256]{2,1,0:T(8,128)(2,1)S(1)}, bf16[24,48,256]{2,1,0:T(8,128)(2,1)}, u32[]{:S(2)}) copy-start(bf16[24,48,256]{2,1,0:T(8,128)(2,1)} %shard_map.130.refs_0_) | copy-start | bytes 1769476
  14.9 0.9 %copy-start.3 = (bf16[1,256,512]{2,1,0:T(8,128)(2,1)S(1)}, bf16[1,256,512]{2,1,0:T(8,128)(2,1)}, u32[]{:S(2)}) copy-start(bf16[1,256,512]{2,1,0:T(8,128)(2,1)} %refs_2_.3) | copy-start | bytes 786436
  15.8 0.7 copy-start.6
  27.3 13.9 %collective-permute-start.5 = (bf16[24,48,256]{2,1,0:T(8,128)(2,1)S(1)}, bf16[24,48,256]{2,1,0:T(8,128)(2,1)S(1)}, u32[]{:S(2)}, u32[]{:S(2)}) collective-permute-start(bf16[24,48,256]{2,1,0:T(8,128)(2,1)S(1)} %collective-permute-done.2.refs_3_), channel_id=1, source_target_pairs={{0,3},{1,0},{2,1},{3,2},{4,7},{5,4},{6,5},{7,6},{8,11},{9,8},{10,9... | collective-permute-start | bytes 1769480 | tf_op jit(solution)/shard_map/ppermute | solution.py:53
  28.4 13.6 %collective-permute-start.4 = (bf16[24,48,256]{2,1,0:T(8,128)(2,1)S(1)}, bf16[24,48,256]{2,1,0:T(8,128)(2,1)S(1)}, u32[]{:S(2)}, u32[]{:S(2)}) collective-permute-start(bf16[24,48,256]{2,1,0:T(8,128)(2,1)S(1)} %collective-permute-done.refs_1_), channel_id=1, source_target_pairs={{0,4},{1,5},{2,6},{3,7},{4,0},{5,1},{6,2},{7,3},{8,12},{9,13},{10,... | collective-permute-start | bytes 1769480 | tf_op jit(solution)/shard_map/ppermute | solution.py:57
  28.6 13.6 %collective-permute-start.3 = (bf16[24,48,256]{2,1,0:T(8,128)(2,1)S(1)}, bf16[24,48,256]{2,1,0:T(8,128)(2,1)S(1)}, u32[]{:S(2)}, u32[]{:S(2)}) collective-permute-start(bf16[24,48,256]{2,1,0:T(8,128)(2,1)S(1)} %collective-permute-done.refs_1_), channel_id=1, source_target_pairs={{0,1},{1,2},{2,3},{3,0},{4,5},{5,6},{6,7},{7,4},{8,9},{9,10},{10,1... | collective-permute-start | bytes 1769480 | tf_op jit(solution)/shard_map/ppermute | solution.py:49
  29.3 2.8 %copy-start = (bf16[24,256,512]{2,1,0:T(8,128)(2,1)S(1)}, bf16[24,256,512]{2,1,0:T(8,128)(2,1)}, u32[]{:S(2)}) copy-start(bf16[24,256,512]{2,1,0:T(8,128)(2,1)} %rhs.7) | copy-start | bytes 18874372
  32.0 24.8 %copy-start.1 = (bf16[24,256,512]{2,1,0:T(8,128)(2,1)S(1)}, bf16[24,256,512]{2,1,0:T(8,128)(2,1)}, u32[]{:S(2)}) copy-start(bf16[24,256,512]{2,1,0:T(8,128)(2,1)} %rhs.7) | copy-start | bytes 18874372
  32.4 5.0 %collective-permute-start.9 = (bf16[3,256,256]{2,1,0:T(8,128)(2,1)S(1)}, bf16[3,256,256]{2,1,0:T(8,128)(2,1)S(1)}, u32[]{:S(2)}, u32[]{:S(2)}) collective-permute-start(bf16[3,256,256]{2,1,0:T(8,128)(2,1)S(1)} %get-tuple-element.80), channel_id=1, source_target_pairs={{0,8},{8,0},{16,24},{24,16},{32,40},{40,32},{48,56},{56,48},{64,72... | collective-permute-start | bytes 1179656 | tf_op jit(solution)/shard_map/ppermute | solution.py:61
  37.4 14.8 %collective-permute-start.12 = (bf16[2,256,256]{2,1,0:T(8,128)(2,1)S(1)}, bf16[2,256,256]{2,1,0:T(8,128)(2,1)S(1)}, u32[]{:S(2)}, u32[]{:S(2)}) collective-permute-start(bf16[2,256,256]{2,1,0:T(8,128)(2,1)S(1)} %get-tuple-element.89), channel_id=1, source_target_pairs={{0,48},{8,56},{16,0},{24,8},{32,16},{40,24},{48,32},{56,40},{64,11... | collective-permute-start | bytes 786440 | tf_op jit(solution)/shard_map/ppermute | solution.py:61
  41.2 12.1 %collective-permute-start.11 = (bf16[2,256,256]{2,1,0:T(8,128)(2,1)S(1)}, bf16[2,256,256]{2,1,0:T(8,128)(2,1)S(1)}, u32[]{:S(2)}, u32[]{:S(2)}) collective-permute-start(bf16[2,256,256]{2,1,0:T(8,128)(2,1)S(1)} %get-tuple-element.89), channel_id=1, source_target_pairs={{0,32},{8,40},{16,48},{24,56},{32,0},{40,8},{48,16},{56,24},{64,96... | collective-permute-start | bytes 786440 | tf_op jit(solution)/shard_map/ppermute | solution.py:61
  41.2 14.7 %collective-permute-start.10 = (bf16[2,256,256]{2,1,0:T(8,128)(2,1)S(1)}, bf16[2,256,256]{2,1,0:T(8,128)(2,1)S(1)}, u32[]{:S(2)}, u32[]{:S(2)}) collective-permute-start(bf16[2,256,256]{2,1,0:T(8,128)(2,1)S(1)} %get-tuple-element.89), channel_id=1, source_target_pairs={{0,16},{8,24},{16,32},{24,40},{32,48},{40,56},{48,0},{56,8},{64,80... | collective-permute-start | bytes 786440 | tf_op jit(solution)/shard_map/ppermute | solution.py:61
  42.3 17.8 %copy-start.4 = (bf16[1,256,512]{2,1,0:T(8,128)(2,1)S(1)}, bf16[1,256,512]{2,1,0:T(8,128)(2,1)}, u32[]{:S(2)}) copy-start(bf16[1,256,512]{2,1,0:T(8,128)(2,1)} %rhs.4) | copy-start | bytes 786436
  42.3 14.5 %collective-permute-start.7 = (bf16[12,48,256]{2,1,0:T(8,128)(2,1)S(1)}, bf16[12,48,256]{2,1,0:T(8,128)(2,1)S(1)}, u32[]{:S(2)}, u32[]{:S(2)}) collective-permute-start(bf16[12,48,256]{2,1,0:T(8,128)(2,1)S(1)} %slice.7), channel_id=1, source_target_pairs={{0,3},{1,0},{2,1},{3,2},{4,7},{5,4},{6,5},{7,6},{8,11},{9,8},{10,9... | collective-permute-start | bytes 884744 | tf_op jit(solution)/shard_map/ppermute | solution.py:53
  44.3 12.5 %collective-permute-start.6 = (bf16[12,48,256]{2,1,0:T(8,128)(2,1)S(1)}, bf16[12,48,256]{2,1,0:T(8,128)(2,1)S(1)}, u32[]{:S(2)}, u32[]{:S(2)}) collective-permute-start(bf16[12,48,256]{2,1,0:T(8,128)(2,1)S(1)} %slice.6), channel_id=1, source_target_pairs={{0,1},{1,2},{2,3},{3,0},{4,5},{5,6},{6,7},{7,4},{8,9},{9,10},{10,1... | collective-permute-start | bytes 884744 | tf_op jit(solution)/shard_map/ppermute | solution.py:49
  52.2 9.7 %collective-permute-start.15 = (bf16[2,256,256]{2,1,0:T(8,128)(2,1)S(1)}, bf16[2,256,256]{2,1,0:T(8,128)(2,1)S(1)}, u32[]{:S(2)}, u32[]{:S(2)}) collective-permute-start(bf16[2,256,256]{2,1,0:T(8,128)(2,1)S(1)} %collective-permute-done.12.refs_2_), channel_id=1, source_target_pairs={{0,8},{8,0},{16,24},{24,16},{32,40},{40,32},{48,56},{56,48},{64,72... | collective-permute-start | bytes 786440 | tf_op jit(solution)/shard_map/ppermute | solution.py:61
  53.4 8.5 %collective-permute-start.14 = (bf16[2,256,256]{2,1,0:T(8,128)(2,1)S(1)}, bf16[2,256,256]{2,1,0:T(8,128)(2,1)S(1)}, u32[]{:S(2)}, u32[]{:S(2)}) collective-permute-start(bf16[2,256,256]{2,1,0:T(8,128)(2,1)S(1)} %collective-permute-done.11.refs_1_), channel_id=1, source_target_pairs={{0,8},{8,0},{16,24},{24,16},{32,40},{40,32},{48,56},{56,48},{64,72... | collective-permute-start | bytes 786440 | tf_op jit(solution)/shard_map/ppermute | solution.py:61
  55.9 5.9 %collective-permute-start.13 = (bf16[2,256,256]{2,1,0:T(8,128)(2,1)S(1)}, bf16[2,256,256]{2,1,0:T(8,128)(2,1)S(1)}, u32[]{:S(2)}, u32[]{:S(2)}) collective-permute-start(bf16[2,256,256]{2,1,0:T(8,128)(2,1)S(1)} %collective-permute-done.10.refs_0_), channel_id=1, source_target_pairs={{0,8},{8,0},{16,24},{24,16},{32,40},{40,32},{48,56},{56,48},{64,72... | collective-permute-start | bytes 786440 | tf_op jit(solution)/shard_map/ppermute | solution.py:61
  60.4 1.4 %collective-permute-start.8 = (bf16[256,256]{1,0:T(8,128)(2,1)S(1)}, bf16[256,256]{1,0:T(8,128)(2,1)S(1)}, u32[]{:S(2)}, u32[]{:S(2)}) collective-permute-start(bf16[256,256]{1,0:T(8,128)(2,1)S(1)} %get-tuple-element.78), channel_id=1, source_target_pairs={{0,8},{8,0},{16,24},{24,16},{32,40},{40,32},{48,56},{56,48},{64,72... | collective-permute-start | bytes 393224 | tf_op jit(solution)/shard_map/ppermute | solution.py:61
  61.9 19.4 %collective-permute-start.20 = (bf16[3,256,256]{2,1,0:T(8,128)(2,1)S(1)}, bf16[3,256,256]{2,1,0:T(8,128)(2,1)S(1)}, u32[]{:S(2)}, u32[]{:S(2)}) collective-permute-start(bf16[3,256,256]{2,1,0:T(8,128)(2,1)S(1)} %shard_map.142.top), channel_id=1, source_target_pairs={{0,64},{8,72},{16,80},{24,88},{32,96},{40,104},{48,112},{56,120},{... | collective-permute-start | bytes 1179656 | tf_op jit(solution)/shard_map/ppermute | solution.py:61
  65.0 4.7 %collective-permute-start.18 = (bf16[256,256]{1,0:T(8,128)(2,1)S(1)}, bf16[256,256]{1,0:T(8,128)(2,1)S(1)}, u32[]{:S(2)}, u32[]{:S(2)}) collective-permute-start(bf16[256,256]{1,0:T(8,128)(2,1)S(1)} %get-tuple-element.90.refs_6_), channel_id=1, source_target_pairs={{0,48},{8,56},{16,0},{24,8},{32,16},{40,24},{48,32},{56,40},{64,11... | collective-permute-start | bytes 393224 | tf_op jit(solution)/shard_map/ppermute | solution.py:61
  65.6 5.8 %collective-permute-start.17 = (bf16[256,256]{1,0:T(8,128)(2,1)S(1)}, bf16[256,256]{1,0:T(8,128)(2,1)S(1)}, u32[]{:S(2)}, u32[]{:S(2)}) collective-permute-start(bf16[256,256]{1,0:T(8,128)(2,1)S(1)} %get-tuple-element.90.refs_6_), channel_id=1, source_target_pairs={{0,32},{8,40},{16,48},{24,56},{32,0},{40,8},{48,16},{56,24},{64,96... | collective-permute-start | bytes 393224 | tf_op jit(solution)/shard_map/ppermute | solution.py:61
  66.6 8.4 %collective-permute-start.16 = (bf16[256,256]{1,0:T(8,128)(2,1)S(1)}, bf16[256,256]{1,0:T(8,128)(2,1)S(1)}, u32[]{:S(2)}, u32[]{:S(2)}) collective-permute-start(bf16[256,256]{1,0:T(8,128)(2,1)S(1)} %get-tuple-element.90.refs_6_), channel_id=1, source_target_pairs={{0,16},{8,24},{16,32},{24,40},{32,48},{40,56},{48,0},{56,8},{64,80... | collective-permute-start | bytes 393224 | tf_op jit(solution)/shard_map/ppermute | solution.py:61
  75.6 5.8 %copy-start.5 = (bf16[256,512]{1,0:T(8,128)(2,1)S(1)}, bf16[256,512]{1,0:T(8,128)(2,1)}, u32[]{:S(2)}) copy-start(bf16[256,512]{1,0:T(8,128)(2,1)} %above.1) | copy-start | bytes 786436
  75.6 5.8 %collective-permute-start.19 = (bf16[256,256]{1,0:T(8,128)(2,1)S(1)}, bf16[256,256]{1,0:T(8,128)(2,1)S(1)}, u32[]{:S(2)}, u32[]{:S(2)}) collective-permute-start(bf16[256,256]{1,0:T(8,128)(2,1)S(1)} %get-tuple-element.100.mine), channel_id=1, source_target_pairs={{0,64},{8,72},{16,80},{24,88},{32,96},{40,104},{48,112},{56,120},{... | collective-permute-start | bytes 393224 | tf_op jit(solution)/shard_map/ppermute | solution.py:61
  82.6 3.0 %collective-permute-start.21 = (bf16[2,256,256]{2,1,0:T(8,128)(2,1)S(1)}, bf16[2,256,256]{2,1,0:T(8,128)(2,1)S(1)}, u32[]{:S(2)}, u32[]{:S(2)}) collective-permute-start(bf16[2,256,256]{2,1,0:T(8,128)(2,1)S(1)} %shard_map.143.own), channel_id=1, source_target_pairs={{0,8},{8,0},{16,24},{24,16},{32,40},{40,32},{48,56},{56,48},{64,72... | collective-permute-start | bytes 786440 | tf_op jit(solution)/shard_map/ppermute | solution.py:61
